TPU v7x, 32 devices: a whole 2x2x4 slice. The times are simulated.
32 devices in a mesh: blk: 8 (over z, core), pack: 4 (over y, x).
Axes of the slice: x: 2, y: 2, z: 4, core: 2. Of those that a mesh axis runs over, the one named last changes fastest.
Arguments:
- tokens: bfloat16 [4, 2048, 1536], P('pack', 'blk'), may hold values from -6 to 6
- lengths: int32 [4, 8], P('pack'), may hold values from 1 to 1936, as said below
- out_grad: bfloat16 [4, 2048, 1536], P('pack', 'blk'), may hold values from -6 to 6
- w_qkv: float32 [1536, 2048], P(('blk', 'pack')), may hold values from -0.21875 to 0.21875
- b_qkv: float32 [2048], P(('blk', 'pack')), may hold values from -0.6 to 0.6
- w_out: float32 [1536, 1536], P(('blk', 'pack')), may hold values from -0.625 to 0.625
- gain_attn: float32 [1536], P(('blk', 'pack')), may hold values from 0.5 to 1.5
- w_gate: float32 [1536, 8960], P(('blk', 'pack')), may hold values from -0.15625 to 0.15625
- w_up: float32 [1536, 8960], P(('blk', 'pack')), may hold values from -0.15625 to 0.15625
- w_down: float32 [8960, 1536], P(('blk', 'pack')), may hold values from -0.0625 to 0.0625
- gain_mlp: float32 [1536], P(('blk', 'pack')), may hold values from 0.5 to 1.5
Outputs:
- output: bfloat16 [4, 2048, 1536], P('pack', 'blk')
- tokens_grad: bfloat16 [4, 2048, 1536], P('pack', 'blk')
- grad_w_qkv: float32 [1536, 2048], P(('blk', 'pack'))
- grad_b_qkv: float32 [2048], P(('blk', 'pack'))
- grad_w_out: float32 [1536, 1536], P(('blk', 'pack'))
- grad_gain_attn: float32 [1536], P(('blk', 'pack'))
- grad_w_gate: float32 [1536, 8960], P(('blk', 'pack'))
- grad_w_up: float32 [1536, 8960], P(('blk', 'pack'))
- grad_w_down: float32 [8960, 1536], P(('blk', 'pack'))
- grad_gain_mlp: float32 [1536], P(('blk', 'pack'))
Inputs may be any that keep to these rules, and one draw needn't show every extreme that they name: In each pack the 8 lengths sum to 2048; exactly one document starts within the first 256 tokens and ends within the last 256 tokens, and the other documents together hold fewer than 256 tokens and lie within the first or the last 256 tokens.
All inputs are finite; a program needn't handle non-finite values.
Results may differ from a plain program's by a relative error of at most 0.018.
The roundings to bfloat16 on the way count: a program that leaves them out, or rounds other values in their place, can miss the bound.
Values may be sent and summed in bfloat16 or wider, within the bound.
No kernel may reach another device: no remote copies, remote signals or barrier semaphores. Data moves between devices by JAX's collectives and lax.ppermute only.
A program may use at most 704 MiB of HBM per device.

v0:
```python
import jax
import jax.numpy as jnp
from jax import lax
from jax.sharding import PartitionSpec as P

H = 12
KVH = 2
HD = 128


NEG = -1e30


def passed_along(shard, axis, by):
    peers = lax.axis_size(axis)
    return lax.ppermute(shard, axis, [(i, (i + by) % peers) for i in range(peers)])


def shifted(block, axis, distance):
    devices = range(lax.axis_size(axis))
    route = [(i - distance, i) for i in devices if i - distance in devices]
    return lax.ppermute(block, axis, route)


def matmul(left, right):
    return jnp.dot(left, right, preferred_element_type=jnp.float32)


def matmul_tn(left, right):
    return lax.dot_general(
        left, right, (((0,), (0,)), ((), ())), preferred_element_type=jnp.float32
    )


def matmul_nt(left, right):
    return lax.dot_general(
        left, right, (((1,), (1,)), ((), ())), preferred_element_type=jnp.float32
    )


def rms_norm(values, gain):
    return values * lax.rsqrt(jnp.mean(values * values, axis=-1, keepdims=True) + 1e-06) * gain


def rotate(values, position):
    half = values.shape[-1] // 2
    freq = 10000.0 ** (-2.0 * jnp.arange(half, dtype=jnp.float32) / values.shape[-1])
    angle = position.astype(jnp.float32)[:, None] * freq[None, :]
    cosine = jnp.cos(angle)[:, None, :]
    sine = jnp.sin(angle)[:, None, :]
    first = values[..., :half]
    second = values[..., half:]
    return jnp.concatenate(
        [first * cosine - second * sine, second * cosine + first * sine], axis=-1
    )


def doc_layout(lengths_row, token_index):
    ends = jnp.cumsum(lengths_row)
    starts = ends - lengths_row
    inside = (token_index[:, None] >= starts[None, :]) & (token_index[:, None] < ends[None, :])
    numbers = jnp.arange(lengths_row.shape[0], dtype=jnp.int32)
    doc_number = jnp.sum(jnp.where(inside, numbers[None, :], 0), axis=1)
    begin = jnp.sum(jnp.where(inside, starts[None, :], 0), axis=1)
    return (doc_number, token_index - begin)


def pass_grads(key_value_grads):
    return passed_along(key_value_grads.astype(jnp.bfloat16), "blk", 1).astype(
        key_value_grads.dtype
    )


def on_device(
    tokens, lengths, out_grad, w_qkv, b_qkv, w_out, gain_attn, w_gate, w_up, w_down, gain_mlp
):
    block_rows = tokens.shape[1]
    blocks = lax.axis_size("blk")
    my_block = lax.axis_index("blk")
    groups = H // KVH
    score_scale = HD ** (-0.5)
    pack_lengths = lengths[0]
    token_index = my_block * block_rows + jnp.arange(block_rows, dtype=jnp.int32)
    doc_number, position = doc_layout(pack_lengths, token_index)
    first_begin = token_index[0] - position[0]

    def block_meta(source):
        key_index = source * block_rows + jnp.arange(block_rows, dtype=jnp.int32)
        key_doc, unused_position = doc_layout(pack_lengths, key_index)
        allowed = (key_doc[None, :] == doc_number[:, None]) & (
            key_index[None, :] <= token_index[:, None]
        )
        needed = (source <= my_block) & (source * block_rows + block_rows - 1 >= first_begin)
        return (allowed, needed)

    attn_shards = (
        w_qkv.astype(jnp.bfloat16),
        b_qkv.astype(jnp.bfloat16),
        w_out.astype(jnp.bfloat16),
        gain_attn.astype(jnp.bfloat16),
    )
    qkv_full, bias_full, out_full, attn_gain = (
        lax.all_gather(attn_shards[0], ("blk", "pack"), axis=0, tiled=True),
        lax.all_gather(attn_shards[1], ("blk", "pack"), axis=0, tiled=True),
        lax.all_gather(attn_shards[2], ("blk", "pack"), axis=0, tiled=True),
        lax.all_gather(attn_shards[3], ("blk", "pack"), axis=0, tiled=True),
    )
    stream = tokens[0].astype(jnp.float32)
    normed_low = rms_norm(stream, attn_gain.astype(jnp.float32)).astype(jnp.bfloat16)
    projected = matmul(normed_low, qkv_full) + bias_full.astype(jnp.float32)
    width = H * HD
    query = projected[:, :width].reshape(block_rows, H, HD)
    key = projected[:, width : width + KVH * HD].reshape(block_rows, KVH, HD)
    value = projected[:, width + KVH * HD :].reshape(block_rows, KVH, HD)
    query_low = (
        (rotate(query, position) * score_scale)
        .astype(jnp.bfloat16)
        .reshape(block_rows, KVH, groups, HD)
    )
    key_low = rotate(key, position).astype(jnp.bfloat16)
    value_low = value.astype(jnp.bfloat16)
    own_pair = jnp.stack([key_low, value_low])

    def forward_step(state, visiting, source):
        allowed, needed = block_meta(source)

        def forward_work(carry):
            weighted_sum, row_max, row_total = carry
            scores = jnp.einsum(
                "tkgd,ukd->kgtu", query_low, visiting[0], preferred_element_type=jnp.float32
            )
            masked = jnp.where(allowed, scores, NEG)
            new_max = jnp.maximum(row_max, jnp.max(masked, axis=-1))
            weights = jnp.where(allowed, jnp.exp(masked - new_max[..., None]), 0.0)
            factor = jnp.exp(row_max - new_max)
            weighted_sum = weighted_sum * factor[..., None] + jnp.einsum(
                "kgtu,ukd->kgtd",
                weights.astype(jnp.bfloat16),
                visiting[1],
                preferred_element_type=jnp.float32,
            )
            row_total = row_total * factor + jnp.sum(weights, axis=-1)
            return (weighted_sum, new_max, row_total)

        return lax.cond(needed, forward_work, lambda carry: carry, state)

    initial = (
        jnp.zeros((KVH, groups, block_rows, HD), jnp.float32),
        jnp.full((KVH, groups, block_rows), NEG, jnp.float32),
        jnp.zeros((KVH, groups, block_rows), jnp.float32),
    )
    state = forward_step(initial, own_pair, my_block)

    def forward_turn(turn_index, carry):
        visiting, inner = carry
        visiting = shifted(visiting, "blk", 1)
        return (visiting, forward_step(inner, visiting, (my_block - turn_index) % blocks))

    unused_pair, state = lax.fori_loop(1, blocks, forward_turn, (own_pair, state))
    weighted_sum, row_max, row_total = state
    head_out = weighted_sum / row_total[..., None]
    attn_f32 = head_out.transpose(2, 0, 1, 3).reshape(block_rows, width)
    log_total = row_max + jnp.log(row_total)
    attn_low = attn_f32.astype(jnp.bfloat16)
    middle = stream + matmul(attn_low, out_full)
    mlp_shards = (
        w_gate.astype(jnp.bfloat16),
        w_up.astype(jnp.bfloat16),
        w_down.astype(jnp.bfloat16),
        gain_mlp.astype(jnp.bfloat16),
    )
    gate_full, up_full, down_full, mlp_gain = (
        lax.all_gather(mlp_shards[0], ("blk", "pack"), axis=0, tiled=True),
        lax.all_gather(mlp_shards[1], ("blk", "pack"), axis=0, tiled=True),
        lax.all_gather(mlp_shards[2], ("blk", "pack"), axis=0, tiled=True),
        lax.all_gather(mlp_shards[3], ("blk", "pack"), axis=0, tiled=True),
    )
    hidden_low = rms_norm(middle, mlp_gain.astype(jnp.float32)).astype(jnp.bfloat16)
    gate_proj = matmul(hidden_low, gate_full)
    up_proj = matmul(hidden_low, up_full)
    act_low = (jax.nn.silu(gate_proj) * up_proj).astype(jnp.bfloat16)
    result = middle + matmul(act_low, down_full)
    gate_full, up_full, down_full, mlp_gain = (
        lax.all_gather(mlp_shards[0], ("blk", "pack"), axis=0, tiled=True),
        lax.all_gather(mlp_shards[1], ("blk", "pack"), axis=0, tiled=True),
        lax.all_gather(mlp_shards[2], ("blk", "pack"), axis=0, tiled=True),
        lax.all_gather(mlp_shards[3], ("blk", "pack"), axis=0, tiled=True),
    )
    grad_top = out_grad[0]
    grad_down = matmul_tn(act_low, grad_top)
    grad_act = matmul_nt(grad_top, down_full)
    unused_act, act_pull = jax.vjp(
        lambda gate_in, up_in: jax.nn.silu(gate_in) * up_in, gate_proj, up_proj
    )
    grad_gate, grad_up = act_pull(grad_act)
    gate_grad_low = grad_gate.astype(jnp.bfloat16)
    up_grad_low = grad_up.astype(jnp.bfloat16)
    grad_gate_w = matmul_tn(hidden_low, gate_grad_low)
    grad_up_w = matmul_tn(hidden_low, up_grad_low)
    grad_hidden = matmul_nt(gate_grad_low, gate_full) + matmul_nt(up_grad_low, up_full)
    unused_norm, second_pull = jax.vjp(rms_norm, middle, mlp_gain.astype(jnp.float32))
    grad_mid, grad_mlp_gain = second_pull(grad_hidden)
    grad_middle = grad_top.astype(jnp.float32) + grad_mid
    mlp_grads = (
        lax.psum_scatter(grad_gate_w, ("blk", "pack"), scatter_dimension=0, tiled=True),
        lax.psum_scatter(grad_up_w, ("blk", "pack"), scatter_dimension=0, tiled=True),
        lax.psum_scatter(grad_down, ("blk", "pack"), scatter_dimension=0, tiled=True),
        lax.psum_scatter(grad_mlp_gain, ("blk", "pack"), scatter_dimension=0, tiled=True),
    )
    qkv_full, bias_full, out_full, attn_gain = (
        lax.all_gather(attn_shards[0], ("blk", "pack"), axis=0, tiled=True),
        lax.all_gather(attn_shards[1], ("blk", "pack"), axis=0, tiled=True),
        lax.all_gather(attn_shards[2], ("blk", "pack"), axis=0, tiled=True),
        lax.all_gather(attn_shards[3], ("blk", "pack"), axis=0, tiled=True),
    )
    middle_low = grad_middle.astype(jnp.bfloat16)
    grad_out_w = matmul_tn(attn_low, middle_low)
    grad_heads = (
        matmul_nt(middle_low, out_full).astype(jnp.bfloat16).reshape(block_rows, KVH, groups, HD)
    )
    row_delta = jnp.sum(grad_heads.astype(jnp.float32).transpose(1, 2, 0, 3) * head_out, axis=-1)

    def backward_step(query_grads, visiting, source):
        allowed, needed = block_meta(source)

        def backward_work(inner):
            scores = jnp.einsum(
                "tkgd,ukd->kgtu", query_low, visiting[0], preferred_element_type=jnp.float32
            )
            weights = jnp.where(allowed, jnp.exp(scores - log_total[..., None]), 0.0)
            grad_value = jnp.einsum(
                "kgtu,tkgd->ukd",
                weights.astype(jnp.bfloat16),
                grad_heads,
                preferred_element_type=jnp.float32,
            )
            grad_prob = jnp.einsum(
                "tkgd,ukd->kgtu", grad_heads, visiting[1], preferred_element_type=jnp.float32
            )
            grad_score = (weights * (grad_prob - row_delta[..., None])).astype(jnp.bfloat16)
            inner = inner + jnp.einsum(
                "kgtu,ukd->tkgd", grad_score, visiting[0], preferred_element_type=jnp.float32
            )
            grad_key = jnp.einsum(
                "kgtu,tkgd->ukd", grad_score, query_low, preferred_element_type=jnp.float32
            )
            return (inner, jnp.stack([grad_key, grad_value]))

        def skipped(inner):
            return (inner, jnp.zeros((2, block_rows, KVH, HD), jnp.float32))

        return lax.cond(needed, backward_work, skipped, query_grads)

    zero_query = jnp.zeros((block_rows, KVH, groups, HD), jnp.float32)
    query_grads, pair_grads = backward_step(zero_query, own_pair, my_block)

    def backward_turn(turn_index, carry):
        visiting, travelling, inner = carry
        visiting = shifted(visiting, "blk", 1)
        travelling = pass_grads(travelling)
        inner, extra = backward_step(inner, visiting, (my_block - turn_index) % blocks)
        return (visiting, travelling + extra, inner)

    unused_pair, pair_grads, query_grads = lax.fori_loop(
        1, blocks, backward_turn, (own_pair, pair_grads, query_grads)
    )
    pair_grads = pass_grads(pair_grads)
    unused_query, query_pull = jax.vjp(lambda values: rotate(values, position), query)
    unused_key, key_pull = jax.vjp(lambda values: rotate(values, position), key)
    (grad_query,) = query_pull((query_grads * score_scale).reshape(block_rows, H, HD))
    (grad_key,) = key_pull(pair_grads[0])
    grad_proj = jnp.concatenate(
        [
            grad_query.reshape(block_rows, width),
            grad_key.reshape(block_rows, KVH * HD),
            pair_grads[1].reshape(block_rows, KVH * HD),
        ],
        axis=1,
    ).astype(jnp.bfloat16)
    grad_qkv_w = matmul_tn(normed_low, grad_proj)
    grad_qkv_b = jnp.sum(grad_proj.astype(jnp.float32), axis=0)
    grad_normed = matmul_nt(grad_proj, qkv_full)
    unused_first, first_pull = jax.vjp(rms_norm, stream, attn_gain.astype(jnp.float32))
    grad_input, grad_attn_gain = first_pull(grad_normed)
    attn_grads = (
        lax.psum_scatter(grad_qkv_w, ("blk", "pack"), scatter_dimension=0, tiled=True),
        lax.psum_scatter(grad_qkv_b, ("blk", "pack"), scatter_dimension=0, tiled=True),
        lax.psum_scatter(grad_out_w, ("blk", "pack"), scatter_dimension=0, tiled=True),
        lax.psum_scatter(grad_attn_gain, ("blk", "pack"), scatter_dimension=0, tiled=True),
    )
    input_grad = (grad_middle + grad_input).astype(jnp.bfloat16)
    return (
        result.astype(jnp.bfloat16)[None],
        input_grad[None],
        attn_grads[0],
        attn_grads[1],
        attn_grads[2],
        attn_grads[3],
        mlp_grads[0],
        mlp_grads[1],
        mlp_grads[2],
        mlp_grads[3],
    )


def solution(mesh):
    in_specs = (
        P("pack", "blk", None),
        P("pack", None),
        P("pack", "blk", None),
        P(("blk", "pack"), None),
        P(("blk", "pack")),
        P(("blk", "pack"), None),
        P(("blk", "pack")),
        P(("blk", "pack"), None),
        P(("blk", "pack"), None),
        P(("blk", "pack"), None),
        P(("blk", "pack")),
    )
    out_specs = (
        P("pack", "blk", None),
        P("pack", "blk", None),
        P(("blk", "pack"), None),
        P(("blk", "pack")),
        P(("blk", "pack"), None),
        P(("blk", "pack")),
        P(("blk", "pack"), None),
        P(("blk", "pack"), None),
        P(("blk", "pack"), None),
        P(("blk", "pack")),
    )
    return jax.shard_map(
        on_device, mesh=mesh, in_specs=in_specs, out_specs=out_specs, check_vma=False
    )
```

profile of v0, /device:TPU:0, one launch (start us, length us, event | category | flops | bytes accessed | tf_op | source)
XLA Modules:
  0.0 2439.7 jit_solution(11916632775478741978)
XLA Ops:
  17.9 42.4 %all-reduce.12 = (bf16[2048]{0:T(1024)(128)(2,1)S(1)}, bf16[1536]{0:T(1024)(128)(2,1)S(1)}, bf16[1536]{0:T(1024)(128)(2,1)S(1)}) all-reduce(bf16[2048]{0:T(1024)(128)(2,1)S(1)} %dynamic-update-slice.1, bf16[1536]{0:T(1024)(128)(2,1)S(1)} %dynamic-update-slice, ...), channel_id=1, replica_groups=mesh['blk'=8,'pack'=4] {'blk','pack'}, use_global_device_ids=true, to_apply=%add.5 | all-reduce | flops 5120 | bytes 20480
  63.7 20.4 all-gather.6.cloned.1.call-done
  105.5 66.3 %while.49 = (s32[]{:T(128)}, bf16[2,256,2,128]{3,1,2,0:T(8,128)(2,1)S(1)}, f32[2,6,256,128]{3,2,1,0:T(8,128)S(1)}, f32[2,6,256]{2,1,0:T(8,128)}, f32[2,6,256]{2,...) while((s32[]{:T(128)}, ...), condition=%wide.region_14.15_spmd.clone, body=%wide.region_8.14_spmd.clone.sunk | while | flops 411517472 | bytes 15702636 | solution.py:159
  108.9 11.6 collective-permute-start
  129.4 14.3 collective-permute-start
  180.4 145.1 %all-gather.10.cloned.1.call-done = bf16[1536,8960]{1,0:T(8,128)(2,1)} async-done(((bf16[48,8960]{1,0:T(8,128)(2,1)}), bf16[1536,8960]{1,0:T(8,128)(2,1)}) %all-gather.10.cloned.1.call-update) | async-done | bytes 27525136 | tf_op jit(solution)/shard_map/all_gather | solution.py:173
  325.5 15.1 fusion.115
  340.6 152.4 %all-gather.12.cloned.1.call-done = bf16[1536,8960]{1,0:T(8,128)(2,1)} async-done(((bf16[48,8960]{1,0:T(8,128)(2,1)}), bf16[1536,8960]{1,0:T(8,128)(2,1)}) %all-gather.12.cloned.1.call-update) | async-done | bytes 27525136 | tf_op jit(solution)/shard_map/all_gather | solution.py:174
  492.9 15.2 fusion.116
  508.2 151.6 %all-gather.14.cloned.1.call-done = bf16[8960,1536]{1,0:T(8,128)(2,1)} async-done(((bf16[280,1536]{1,0:T(8,128)(2,1)}), bf16[8960,1536]{1,0:T(8,128)(2,1)}) %all-gather.14.cloned.1.call-update) | async-done | bytes 27525136 | tf_op jit(solution)/shard_map/all_gather | solution.py:175
  659.8 21.8 multiply_convert_fusion
  681.6 14.8 fusion.117
  696.4 14.9 multiply_reduce_fusion
  732.1 105.1 %while.50 = (s32[]{:T(128)}, bf16[2,256,2,128]{3,1,2,0:T(8,128)(2,1)}, bf16[2,256,2,128]{3,1,2,0:T(8,128)(2,1)}, f32[256,2,6,128]{3,0,2,1:T(8,128)S(1)}, s32[]{:...) while((s32[]{:T(128)}, ...), condition=%wide.region_24.25_spmd.clone, body=%wide.region_20.24_spmd.clone.sunk | while | flops 1014049280 | bytes 29502112 | solution.py:264
  774.2 10.2 collective-permute-done.2
  844.4 14.6 collective-permute-done.3
  867.7 26.5 %fusion.118 = f32[1536,8960]{1,0:T(8,128)} fusion(bf16[256,1536]{1,0:T(8,128)(2,1)S(1)} %copy-done.9, bf16[256,8960]{1,0:T(8,128)(2,1)} %get-tuple-element.1368), kind=kOutput, calls=%fused_computation.184 | convolution fusion | flops 7046430720 | bytes 60424192 | tf_op jit(solution)/shard_map/dot_general | solution.py:30
  894.5 26.2 %fusion.119 = f32[1536,8960]{1,0:T(8,128)} fusion(bf16[256,1536]{1,0:T(8,128)(2,1)S(1)} %copy-done.9, bf16[256,8960]{1,0:T(8,128)(2,1)} %get-tuple-element.1367), kind=kOutput, calls=%fused_computation.185 | convolution fusion | flops 7046430720 | bytes 60424192 | tf_op jit(solution)/shard_map/dot_general | solution.py:30
  921.9 22.5 fusion.97
  945.8 15.0 fusion.84
  967.4 44.8 %all-reduce.11 = (f32[2048]{0:T(1024)S(1)}, f32[1536]{0:T(1024)S(1)}, f32[1536]{0:T(1024)S(1)}) all-reduce(f32[2048]{0:T(1024)S(1)} %convert_reduce_fusion, f32[1536]{0:T(1024)S(1)} %get-tuple-element.1291, f32[1536]{0:T(1024)S(1)} %copy-done.29), channel_id=3, replica_groups=mesh['blk'=8,'pack'=4] {'blk','pack'}, use_global_device_ids=true, to_apply=%region_28.29.clone | all-reduce | flops 5120 | bytes 40960
  1026.8 468.2 %reduce-scatter.12.cloned.1.call-done = f32[48,8960]{1,0:T(8,128)} async-done(((f32[1536,8960]{1,0:T(8,128)}), f32[48,8960]{1,0:T(8,128)}) %reduce-scatter.12.cloned.1.call-update) | async-done | bytes 1720336 | tf_op jit(solution)/shard_map/reduce_scatter | solution.py:205
  1495.0 469.5 %reduce-scatter.14.cloned.1.call-done = f32[48,8960]{1,0:T(8,128)} async-done(((f32[1536,8960]{1,0:T(8,128)}), f32[48,8960]{1,0:T(8,128)}) %reduce-scatter.14.cloned.1.call-update) | async-done | bytes 1720336 | tf_op jit(solution)/shard_map/reduce_scatter | solution.py:206
  1964.5 468.1 %reduce-scatter.16.cloned.1.call-done = f32[280,1536]{1,0:T(8,128)} async-done(((f32[8960,1536]{1,0:T(8,128)}), f32[280,1536]{1,0:T(8,128)}) %reduce-scatter.16.cloned.1.call-update) | async-done | bytes 1720336
  (301 shorter events, 246.7 us)
Async XLA Ops:
  7.2 77.0 %all-gather.6.cloned.1.call-start = ((), (), s32[]{:S(2)}) async-start(), calls=%async_computation.5 | async-start | bytes 6488064 | tf_op jit(solution)/shard_map/all_gather | solution.py:103
  8.9 166.1 %all-gather.8.cloned.1.call-start = ((), (), s32[]{:S(2)}) async-start(), calls=%async_computation.6 | async-start | bytes 4866048 | tf_op jit(solution)/shard_map/all_gather | solution.py:105
  10.8 314.7 %all-gather.10.cloned.1.call-start = ((), (), s32[]{:S(2)}) async-start(), calls=%async_computation.7 | async-start | bytes 28385280 | tf_op jit(solution)/shard_map/all_gather | solution.py:173
  13.3 479.6 %all-gather.12.cloned.1.call-start = ((), (), s32[]{:S(2)}) async-start(), calls=%async_computation.8 | async-start | bytes 28385280 | tf_op jit(solution)/shard_map/all_gather | solution.py:174
  14.4 645.4 %all-gather.14.cloned.1.call-start = ((), (), s32[]{:S(2)}) async-start(), calls=%async_computation.9 | async-start | bytes 28385280 | tf_op jit(solution)/shard_map/all_gather | solution.py:175
  17.0 999.6 %reduce-scatter.10.cloned.1.call-start = ((), (), s32[]{:S(2)}) async-start(), calls=%async_computation.11 | async-start | bytes 9732096 | tf_op jit(solution)/shard_map/reduce_scatter | solution.py:288
  108.9 12.7 collective-permute-start
  121.6 7.7 collective-permute-start
  129.4 15.5 collective-permute-start
  160.4 11.3 collective-permute-start
  718.1 308.7 %reduce-scatter.8.cloned.1.call-start = ((), (), s32[]{:S(2)}) async-start(), calls=%async_computation.10 | async-start | bytes 12976128 | tf_op jit(solution)/shard_map/reduce_scatter | solution.py:286
  734.2 7.9 collective-permute-start.2
  745.7 7.9 collective-permute-start.2
  757.2 7.9 collective-permute-start.2
  771.0 13.4 collective-permute-start.2
  785.2 10.9 collective-permute-start.1
  793.7 9.5 collective-permute-start.2
  803.9 8.9 collective-permute-start.1
  810.4 8.9 collective-permute-start.2
  823.6 12.8 collective-permute-start.2
  838.3 20.7 collective-permute-start.3
  866.6 628.4 %reduce-scatter.12.cloned.1.call-start = ((), (), s32[]{:S(2)}) async-start(), calls=%async_computation.12 | async-start | bytes 56770560 | tf_op jit(solution)/shard_map/reduce_scatter | solution.py:205
  894.3 1070.3 %reduce-scatter.14.cloned.1.call-start = ((), (), s32[]{:S(2)}) async-start(), calls=%async_computation.13 | async-start | bytes 56770560 | tf_op jit(solution)/shard_map/reduce_scatter | solution.py:206
  920.7 1511.9 %reduce-scatter.16.cloned.1.call-start = ((), (), s32[]{:S(2)}) async-start(), calls=%async_computation.14 | async-start | bytes 56770560
  (42 other events, 1030.5 us)
Sparse Core Ops, SparseCore 0:
  11.5 72.6 all-gather.5
  87.6 62.2 all-gather.7
  153.4 172.0 all-gather.9
  328.8 164.0 all-gather.11
  495.7 164.0 all-gather.13
  718.2 140.6 reduce-scatter.9
  866.7 159.9 reduce-scatter.7
  1033.8 461.2 reduce-scatter.11
  1503.2 461.3 reduce-scatter.13
  1971.4 461.2 reduce-scatter.15
where the time goes:
time: 2450 us; the launch traced here: 2440 us
  waiting for transfers between devices  1950 us (80%)
  matrix products  209 us (9%)
  starting transfers between devices  110 us (4%)
  blocking collectives  87.2 us (4%)
  other arithmetic  32.2 us (1%)
  local copies, waits for them, and re-layouts  29.7 us (1%)
    reduce_scatter x1, waiting for transfers between devices, on_device(): lax.psum_scatter(grad_up_w, ('blk', 'pack'), scatter_dimension=0, tiled=T...  470 us
    unnamed x11, waiting for transfers between devices  468 us
    reduce_scatter x1, waiting for transfers between devices, on_device(): lax.psum_scatter(grad_gate_w, ('blk', 'pack'), scatter_dimension=0, tiled...  468 us
    all_gather x1, waiting for transfers between devices, on_device(): lax.all_gather(mlp_shards[1], ('blk', 'pack'), axis=0, tiled=True)  152 us
    all_gather x1, waiting for transfers between devices, on_device(): lax.all_gather(mlp_shards[2], ('blk', 'pack'), axis=0, tiled=True)  152 us
    all_gather x1, waiting for transfers between devices, on_device(): lax.all_gather(mlp_shards[0], ('blk', 'pack'), axis=0, tiled=True)  145 us
    ppermute x14, starting transfers between devices, shifted(): return lax.ppermute(block, axis, route)  89.5 us
    unnamed x2, blocking collectives  87.2 us
  transfers between devices with their start and end apart: 32, of which 24 were waited for; matrix products, arithmetic and copies ran while one was open for 8% of the time, Pallas kernels for 0%

commit v1 on v0

v1 whole, which is shorter than its diff:
```python
import functools

import jax
import jax.numpy as jnp
from jax import lax
from jax.experimental import pallas as pl
from jax.experimental.pallas import tpu as pltpu
from jax.sharding import PartitionSpec as P

H = 12
KVH = 2
HD = 128
G = H // KVH
NEG = -1e30
BF = jnp.bfloat16
F32 = jnp.float32
VMEM_LIMIT = 56 * 1024 * 1024
BOTH = ("blk", "pack")


def chip_shift(block, by, cyclic=True):
    n = lax.axis_size("blk")
    route = [(i, (i + 2 * by) % n) for i in range(n) if cyclic or 0 <= i + 2 * by < n]
    return lax.ppermute(block, "blk", route)


def core_swap(block):
    n = lax.axis_size("blk")
    return lax.ppermute(block, "blk", [(i, i ^ 1) for i in range(n)])


def gather_line(block):
    chips = lax.axis_size("blk") // 2
    mine = jnp.stack([block] + [chip_shift(block, s) for s in range(1, chips)])
    return jnp.stack([mine, core_swap(mine)], axis=1)


def scatter_line(parts):
    chips = parts.shape[0]
    other = core_swap(parts[:, 1])
    mine = parts[:, 0].astype(F32) + other.astype(F32)
    total = mine[0]
    for s in range(1, chips):
        total = total + chip_shift(mine[s].astype(BF), -s).astype(F32)
    return total


def matmul(left, right):
    return jnp.dot(left, right, preferred_element_type=F32)


def matmul_tn(left, right):
    return lax.dot_general(left, right, (((0,), (0,)), ((), ())), preferred_element_type=F32)


def matmul_nt(left, right):
    return lax.dot_general(left, right, (((1,), (1,)), ((), ())), preferred_element_type=F32)


def rms_norm(values, gain):
    return values * lax.rsqrt(jnp.mean(values * values, axis=-1, keepdims=True) + 1e-06) * gain


def turn(x, cosine, sine):
    return x * cosine + pltpu.roll(x, HD // 2, 1) * sine


def qkv_kernel(xn_ref, w_ref, bias_ref, cos_ref, sin_ref, out_ref):
    step = pl.program_id(0)
    proj = matmul(xn_ref[...], w_ref[...]) + bias_ref[...]
    cosine, sine = cos_ref[...], sin_ref[...]

    @pl.when(step < H // 2)
    def _():
        for i in range(2):
            cut = slice(i * HD, (i + 1) * HD)
            out_ref[:, cut] = (turn(proj[:, cut], cosine, sine) * HD**-0.5).astype(BF)

    @pl.when((step >= H // 2) & (step < (H + KVH) // 2))
    def _():
        for i in range(2):
            cut = slice(i * HD, (i + 1) * HD)
            out_ref[:, cut] = turn(proj[:, cut], cosine, sine).astype(BF)

    @pl.when(step >= (H + KVH) // 2)
    def _():
        out_ref[...] = proj.astype(BF)


def qkv_project(xn, w, bias, cosine, sine):
    rows, depth = xn.shape
    cols = w.shape[1]
    return pl.pallas_call(
        qkv_kernel,
        grid=(cols // 256,),
        in_specs=[
            pl.BlockSpec((rows, depth), lambda i: (0, 0)),
            pl.BlockSpec((depth, 256), lambda i: (0, i)),
            pl.BlockSpec((1, 256), lambda i: (0, i)),
            pl.BlockSpec((rows, HD), lambda i: (0, 0)),
            pl.BlockSpec((rows, HD), lambda i: (0, 0)),
        ],
        out_specs=pl.BlockSpec((rows, 256), lambda i: (0, i)),
        out_shape=jax.ShapeDtypeStruct((rows, cols), BF),
        compiler_params=pltpu.CompilerParams(vmem_limit_bytes=VMEM_LIMIT),
        cost_estimate=pl.CostEstimate(
            flops=2 * rows * depth * cols, bytes_accessed=2 * depth * cols, transcendentals=0
        ),
    )(xn, w, bias, cosine, sine)


def allowed_mask(meta_ref, starts_ref, slot, count):
    rows = starts_ref.shape[1]
    key_index = meta_ref[1 + count + slot] + lax.broadcasted_iota(jnp.int32, (rows, rows), 0)
    query_index = meta_ref[0] + lax.broadcasted_iota(jnp.int32, (rows, rows), 1)
    return (key_index >= starts_ref[...]) & (key_index <= query_index)


def forward_kernel(count, meta_ref, q_ref, starts_ref, k_ref, v_ref, att_ref, lse_ref, m, total, acc):
    slot = pl.program_id(1)

    @pl.when(slot == 0)
    def _():
        m[...] = jnp.full(m.shape, NEG, F32)
        total[...] = jnp.zeros(total.shape, F32)
        acc[...] = jnp.zeros(acc.shape, F32)

    @pl.when(meta_ref[1 + slot] == 1)
    def _():
        allowed = allowed_mask(meta_ref, starts_ref, slot, count)
        keys, values = k_ref[0], v_ref[0]
        for g in range(G):
            scores = matmul_nt(keys, q_ref[:, g * HD : (g + 1) * HD])
            scores = jnp.where(allowed, scores, NEG)
            before = m[g : g + 1, :]
            now = jnp.maximum(before, jnp.max(scores, axis=0, keepdims=True))
            weights = jnp.exp(scores - now)
            fade = jnp.exp(before - now)
            m[g : g + 1, :] = now
            total[g : g + 1, :] = total[g : g + 1, :] * fade + jnp.sum(weights, axis=0, keepdims=True)
            acc[g] = acc[g] * fade + matmul_tn(values, weights.astype(BF))

    @pl.when(slot == count - 1)
    def _():
        for g in range(G):
            att_ref[:, g * HD : (g + 1) * HD] = (acc[g] / total[g : g + 1, :]).T
        lse_ref[0] = m[...] + jnp.log(total[...])


def attention_forward(meta, qkv, starts, kv):
    count, rows = kv.shape[0], kv.shape[1]
    width = G * HD

    def pick(h, j, meta_ref):
        return jnp.where(meta_ref[1 + j] == 1, j, 0)

    return pl.pallas_call(
        functools.partial(forward_kernel, count),
        grid_spec=pltpu.PrefetchScalarGridSpec(
            num_scalar_prefetch=1,
            grid=(KVH, count),
            in_specs=[
                pl.BlockSpec((rows, width), lambda h, j, meta_ref: (0, h)),
                pl.BlockSpec((1, rows), lambda h, j, meta_ref: (0, 0)),
                pl.BlockSpec((1, rows, HD), lambda h, j, meta_ref: (pick(h, j, meta_ref), 0, h)),
                pl.BlockSpec((1, rows, HD), lambda h, j, meta_ref: (pick(h, j, meta_ref), 0, KVH + h)),
            ],
            out_specs=[
                pl.BlockSpec((rows, width), lambda h, j, meta_ref: (0, h)),
                pl.BlockSpec((1, 8, rows), lambda h, j, meta_ref: (h, 0, 0)),
            ],
            scratch_shapes=[
                pltpu.VMEM((8, rows), F32),
                pltpu.VMEM((8, rows), F32),
                pltpu.VMEM((G, HD, rows), F32),
            ],
        ),
        out_shape=[
            jax.ShapeDtypeStruct((rows, H * HD), F32),
            jax.ShapeDtypeStruct((KVH, 8, rows), F32),
        ],
        compiler_params=pltpu.CompilerParams(vmem_limit_bytes=VMEM_LIMIT),
        cost_estimate=pl.CostEstimate(
            flops=4 * rows * rows * count * H * HD,
            bytes_accessed=count * rows * 1024,
            transcendentals=rows * rows * count * H,
        ),
    )(meta, qkv, starts, kv, kv)


def backward_kernel(
    count, meta_ref, q_ref, dout_ref, att_ref, lse_ref, starts_ref, k_ref, v_ref, cos_ref, sin_ref,
    dq_ref, dk_ref, dv_ref, delta, dq_sum,
):
    slot = pl.program_id(1)

    @pl.when(slot == 0)
    def _():
        dq_sum[...] = jnp.zeros(dq_sum.shape, F32)
        for g in range(G):
            cut = slice(g * HD, (g + 1) * HD)
            product = dout_ref[:, cut].astype(F32) * att_ref[:, cut]
            delta[g : g + 1, :] = jnp.sum(product.T, axis=0, keepdims=True)

    @pl.when(meta_ref[1 + slot] == 1)
    def _():
        allowed = allowed_mask(meta_ref, starts_ref, slot, count)
        keys, values = k_ref[0], v_ref[0]
        dk = jnp.zeros(keys.shape, F32)
        dv = jnp.zeros(keys.shape, F32)
        for g in range(G):
            cut = slice(g * HD, (g + 1) * HD)
            query, dout = q_ref[:, cut], dout_ref[:, cut]
            scores = matmul_nt(keys, query)
            weights = jnp.where(allowed, jnp.exp(scores - lse_ref[0, g : g + 1, :]), 0.0)
            dv = dv + matmul(weights.astype(BF), dout)
            slope = matmul_nt(values, dout) - delta[g : g + 1, :]
            dscores = (weights * slope).astype(BF)
            dk = dk + matmul(dscores, query)
            dq_sum[:, cut] = dq_sum[:, cut] + matmul_tn(dscores, keys)
        dk_ref[0] = dk.astype(BF)
        dv_ref[0] = dv.astype(BF)

    @pl.when(meta_ref[1 + slot] == 0)
    def _():
        dk_ref[...] = jnp.zeros(dk_ref.shape, BF)
        dv_ref[...] = jnp.zeros(dv_ref.shape, BF)

    @pl.when(slot == count - 1)
    def _():
        for g in range(G):
            cut = slice(g * HD, (g + 1) * HD)
            back = turn(dq_sum[:, cut] * HD**-0.5, cos_ref[...], -sin_ref[...])
            dq_ref[:, cut] = back.astype(BF)


def attention_backward(meta, qkv, dout, att, lse, starts, kv, cosine, sine):
    count, rows = kv.shape[0], kv.shape[1]
    width = G * HD

    def pick(h, j, meta_ref):
        return jnp.where(meta_ref[1 + j] == 1, j, 0)

    whole = lambda h, j, meta_ref: (0, 0)
    by_head = lambda h, j, meta_ref: (0, h)
    return pl.pallas_call(
        functools.partial(backward_kernel, count),
        grid_spec=pltpu.PrefetchScalarGridSpec(
            num_scalar_prefetch=1,
            grid=(KVH, count),
            in_specs=[
                pl.BlockSpec((rows, width), by_head),
                pl.BlockSpec((rows, width), by_head),
                pl.BlockSpec((rows, width), by_head),
                pl.BlockSpec((1, 8, rows), lambda h, j, meta_ref: (h, 0, 0)),
                pl.BlockSpec((1, rows), whole),
                pl.BlockSpec((1, rows, HD), lambda h, j, meta_ref: (pick(h, j, meta_ref), 0, h)),
                pl.BlockSpec((1, rows, HD), lambda h, j, meta_ref: (pick(h, j, meta_ref), 0, KVH + h)),
                pl.BlockSpec((rows, HD), whole),
                pl.BlockSpec((rows, HD), whole),
            ],
            out_specs=[
                pl.BlockSpec((rows, width), by_head),
                pl.BlockSpec((1, rows, HD), lambda h, j, meta_ref: (j, 0, h)),
                pl.BlockSpec((1, rows, HD), lambda h, j, meta_ref: (j, 0, h)),
            ],
            scratch_shapes=[pltpu.VMEM((8, rows), F32), pltpu.VMEM((rows, width), F32)],
        ),
        out_shape=[
            jax.ShapeDtypeStruct((rows, H * HD), BF),
            jax.ShapeDtypeStruct((count, rows, KVH * HD), BF),
            jax.ShapeDtypeStruct((count, rows, KVH * HD), BF),
        ],
        compiler_params=pltpu.CompilerParams(vmem_limit_bytes=VMEM_LIMIT),
        cost_estimate=pl.CostEstimate(
            flops=10 * rows * rows * count * H * HD,
            bytes_accessed=count * rows * 1024,
            transcendentals=rows * rows * count * H,
        ),
    )(meta, qkv, dout, att, lse, starts, kv, kv, cosine, sine)


def on_device(
    tokens, lengths, out_grad, w_qkv, b_qkv, w_out, gain_attn, w_gate, w_up, w_down, gain_mlp
):
    rows, width = tokens.shape[1:]
    blocks, packs = lax.axis_size("blk"), lax.axis_size("pack")
    chips = blocks // 2
    blk = lax.axis_index("blk")
    chip, core = blk // 2, blk % 2
    depth = w_qkv.shape[0]
    qkv_cols = w_qkv.shape[1]
    ff = w_gate.shape[1] // blocks

    token_index = blk * rows + jnp.arange(rows, dtype=jnp.int32)
    ends = jnp.cumsum(lengths[0])
    doc_starts = ends - lengths[0]
    inside = (token_index[:, None] >= doc_starts[None, :]) & (token_index[:, None] < ends[None, :])
    begin = jnp.sum(jnp.where(inside, doc_starts[None, :], 0), axis=1)
    half = HD // 2
    freq = 10000.0 ** (-2.0 * jnp.arange(half, dtype=F32) / HD)
    angle = (token_index - begin).astype(F32)[:, None] * freq[None, :]
    cosine, sine = jnp.cos(angle), jnp.sin(angle)
    cosine = jnp.concatenate([cosine, cosine], axis=1)
    sine = jnp.concatenate([-sine, sine], axis=1)
    starts = begin[None, :].astype(jnp.int32)

    bias_n, gain_n = b_qkv.shape[0], gain_attn.shape[0]
    vectors = jnp.concatenate([b_qkv, gain_attn, gain_mlp]).astype(BF)
    vectors = jnp.pad(vectors, (0, qkv_cols - vectors.shape[0]))
    spare = jnp.zeros((7, qkv_cols), BF)
    packed = jnp.concatenate([w_qkv.astype(BF), vectors[None], spare])
    packed = lax.all_gather(packed, BOTH, axis=0, tiled=False)
    qkv_full = packed[:, :depth].reshape(width, qkv_cols)
    bias = packed[:, depth, :bias_n].reshape(1, qkv_cols).astype(F32)
    attn_gain = packed[:, depth, bias_n : bias_n + gain_n].reshape(width).astype(F32)
    mlp_gain = packed[:, depth, bias_n + gain_n : bias_n + 2 * gain_n].reshape(width).astype(F32)
    out_full = lax.all_gather(w_out.astype(BF), BOTH, axis=0, tiled=True)

    gate_up = jnp.stack([w_gate, w_up]).astype(BF).reshape(2, depth, blocks, ff)
    gate_up = lax.all_to_all(gate_up.transpose(2, 0, 1, 3), "blk", 0, 0, tiled=True)
    down = lax.all_gather(w_down.astype(BF), "pack", axis=0, tiled=True)
    gate_up = lax.all_gather(gate_up, "pack", axis=0, tiled=False)
    gate_up = gate_up.transpose(2, 1, 0, 3, 4).reshape(2, width, ff)
    gate_w, up_w = gate_up[0], gate_up[1]

    stream = tokens[0].astype(F32)
    normed = rms_norm(stream, attn_gain).astype(BF)
    qkv = qkv_project(normed, qkv_full, bias, cosine, sine)
    own = qkv[:, H * HD :]
    lines = jnp.stack([own] + [chip_shift(own, s, cyclic=False) for s in range(1, chips)])
    kv = jnp.stack([lines, core_swap(lines)], axis=1).reshape(blocks, rows, 2 * KVH * HD)
    back = jnp.arange(chips, dtype=jnp.int32)
    source = jnp.stack([(chip - back) * 2 + core, (chip - back) * 2 + 1 - core], axis=1).reshape(-1)
    valid = ((source >= 0) & (source <= blk)).astype(jnp.int32)
    meta = jnp.concatenate([(blk * rows)[None], valid, source * rows]).astype(jnp.int32)
    att, lse = attention_forward(meta, qkv, starts, kv)
    att_low = att.astype(BF)
    middle = stream + matmul(att_low, out_full)

    grad_top = out_grad[0]
    tops = gather_line(grad_top).reshape(-1, width)
    hidden = rms_norm(middle, mlp_gain).astype(BF)
    hiddens = gather_line(hidden).reshape(-1, width)
    gate = matmul(hiddens, gate_w)
    up = matmul(hiddens, up_w)
    act = (jax.nn.silu(gate) * up).astype(BF)
    partial = matmul(act, down).astype(BF)
    result = middle + scatter_line(partial.reshape(chips, 2, rows, width))

    dact = matmul_nt(tops, down)
    sig = jax.nn.sigmoid(gate)
    dgate = (dact * up * sig * (1 + gate * (1 - sig))).astype(BF)
    dup = (dact * gate * sig).astype(BF)
    dpartial = (matmul_nt(dgate, gate_w) + matmul_nt(dup, up_w)).astype(BF)
    grad_hidden = scatter_line(dpartial.reshape(chips, 2, rows, width))

    grad_down = matmul_tn(act, tops).astype(BF)
    grad_down = lax.psum_scatter(grad_down, "pack", scatter_dimension=0, tiled=True).astype(F32)
    grad_gu = jnp.stack([matmul_tn(hiddens, dgate), matmul_tn(hiddens, dup)]).astype(BF)
    grad_gu = grad_gu.reshape(2, blocks, packs, depth, ff).transpose(2, 1, 0, 3, 4)
    grad_gu = lax.psum_scatter(grad_gu, "pack", scatter_dimension=0, tiled=False)
    grad_gu = lax.all_to_all(grad_gu, "blk", 0, 0, tiled=True)
    grad_gu = grad_gu.transpose(1, 2, 0, 3).reshape(2, depth, blocks * ff).astype(F32)

    _, second_pull = jax.vjp(rms_norm, middle, mlp_gain)
    grad_mid, grad_mlp_gain = second_pull(grad_hidden)
    grad_middle = grad_top.astype(F32) + grad_mid

    middle_low = grad_middle.astype(BF)
    grad_out_w = matmul_tn(att_low, middle_low).astype(BF)
    grad_out_w = lax.psum_scatter(grad_out_w, BOTH, scatter_dimension=0, tiled=True).astype(F32)
    dout = matmul_nt(middle_low, out_full).astype(BF)
    dq, dk, dv = attention_backward(meta, qkv, dout, att, lse, starts, kv, cosine, sine)
    dkv = jnp.concatenate([dk, dv], axis=2).reshape(chips, 2, rows, 2 * KVH * HD)
    mine = dkv[:, 0].astype(F32) + core_swap(dkv[:, 1]).astype(F32)
    pair = mine[0]
    for s in range(1, chips):
        pair = pair + chip_shift(mine[s].astype(BF), -s, cyclic=False).astype(F32)
    dk_own = pair[:, : KVH * HD].reshape(rows, KVH, 2, half)
    swapped = jnp.concatenate([dk_own[:, :, 1:], dk_own[:, :, :1]], axis=2)
    cos4, sin4 = cosine.reshape(rows, 1, 2, half), sine.reshape(rows, 1, 2, half)
    dk_own = (dk_own * cos4 - swapped * sin4).reshape(rows, KVH * HD)
    dproj = jnp.concatenate([dq, dk_own.astype(BF), pair[:, KVH * HD :].astype(BF)], axis=1)

    grad_normed = matmul_nt(dproj, qkv_full)
    _, first_pull = jax.vjp(rms_norm, stream, attn_gain)
    grad_input, grad_attn_gain = first_pull(grad_normed)
    input_grad = (grad_middle + grad_input).astype(BF)
    grad_qkv = matmul_tn(normed, dproj).astype(BF).reshape(blocks * packs, depth, qkv_cols)
    grad_bias = jnp.sum(dproj.astype(F32), axis=0)
    vector_grads = jnp.concatenate(
        [
            grad_bias.reshape(-1, bias_n),
            grad_attn_gain.reshape(-1, gain_n),
            grad_mlp_gain.reshape(-1, gain_n),
        ],
        axis=1,
    ).astype(BF)
    vector_grads = jnp.pad(vector_grads, ((0, 0), (0, qkv_cols - vector_grads.shape[1])))
    spare = jnp.zeros((blocks * packs, 7, qkv_cols), BF)
    attn_grads = jnp.concatenate([grad_qkv, vector_grads[:, None], spare], axis=1)
    attn_grads = lax.psum_scatter(attn_grads, BOTH, scatter_dimension=0, tiled=False).astype(F32)
    tail = attn_grads[depth]
    return (
        result.astype(BF)[None],
        input_grad[None],
        attn_grads[:depth],
        tail[:bias_n],
        grad_out_w,
        tail[bias_n : bias_n + gain_n],
        grad_gu[0],
        grad_gu[1],
        grad_down,
        tail[bias_n + gain_n : bias_n + 2 * gain_n],
    )


def solution(mesh):
    tokens, rows, vector = P("pack", "blk", None), P(BOTH, None), P(BOTH)
    in_specs = (
        tokens, P("pack", None), tokens, rows, vector, rows, vector, rows, rows, rows, vector
    )
    out_specs = (tokens, tokens, rows, vector, rows, vector, rows, rows, rows, vector)
    return jax.shard_map(
        on_device, mesh=mesh, in_specs=in_specs, out_specs=out_specs, check_vma=False
    )
```

time: 2450 us -> 968 us (0.40)
  waiting for transfers between devices: 1950 us -> 488 us
  matrix products: 209 us -> 138 us
  local copies, waits for them, and re-layouts: 29.7 us -> 66.6 us
  other arithmetic: 32.2 us -> 65.8 us
  Pallas kernels: 0 us -> 31.4 us
  starting transfers between devices: 110 us -> 84.2 us
    reduce_scatter x4 -> x2, waiting for transfers between devices: 948 us -> 122 us  [the longest x1 122 us: on_device(): lax.psum_scatter(attn_grads, BOTH, scatter_dimension=0, tiled=False)]
    unnamed x11 -> x10, waiting for transfers between devices: 468 us -> 0.13 us
    all_gather x5 -> x4, waiting for transfers between devices: 470 us -> 20.6 us  [the longest x1 12.2 us: on_device(): packed = lax.all_gather(packed, BOTH, axis=0, tiled=False)]
    ppermute x22 -> x24, waiting for transfers between devices: 68 us -> 303 us  [the longest x18 301 us: chip_shift(): return lax.ppermute(block, 'blk', route)]
    unnamed x2 -> x0, blocking collectives: 87.2 us -> none
    all_to_all x0 -> x1, blocking collectives: none -> 67.8 us  [on_device(): lax.all_to_all(gate_up.transpose(2, 0, 1, 3), 'blk', 0, 0, tiled=True)]
    dot_general x5, matrix products: 86.8 us -> 39.6 us  [matmul_tn(): lax.dot_general(left, right, (((0,), (0,)), ((), ())), preferred_element_...]
    all_to_all x0 -> x1, waiting for transfers between devices: none -> 41.5 us  [on_device(): grad_gu = lax.all_to_all(grad_gu, 'blk', 0, 0, tiled=True)]
  transfers between devices with their start and end apart: 32 -> 33, of which waited for: 24 -> 19; matrix products, arithmetic and copies ran while one was open for 8% -> 22% of each run, Pallas kernels for 0% -> 3%
where the time goes in v1:
time: 968 us; the launch traced here: 957 us
  waiting for transfers between devices  488 us (50%)
  matrix products  138 us (14%)
  starting transfers between devices  84.2 us (9%)
  blocking collectives  67.8 us (7%)
  local copies, waits for them, and re-layouts  66.6 us (7%)
  other arithmetic  65.8 us (7%)
  Pallas kernels  31.4 us (3%)
  between operations  15.4 us (2%)
    ppermute x18, waiting for transfers between devices, chip_shift(): return lax.ppermute(block, 'blk', route)  301 us
    reduce_scatter x1, waiting for transfers between devices, on_device(): lax.psum_scatter(attn_grads, BOTH, scatter_dimension=0, tiled=False)  122 us
    ppermute x18, starting transfers between devices, chip_shift(): return lax.ppermute(block, 'blk', route)  79.2 us
    all_to_all x1, blocking collectives, on_device(): lax.all_to_all(gate_up.transpose(2, 0, 1, 3), 'blk', 0, 0, tiled=True)  67.8 us
    dot_general x5, matrix products, matmul_nt(): lax.dot_general(left, right, (((1,), (1,)), ((), ())), preferred_element_...  58.2 us
    all_to_all x1, waiting for transfers between devices, on_device(): grad_gu = lax.all_to_all(grad_gu, 'blk', 0, 0, tiled=True)  41.5 us
    dot_general x4, matrix products, matmul(): return jnp.dot(left, right, preferred_element_type=F32)  39.9 us
    dot_general x5, matrix products, matmul_tn(): lax.dot_general(left, right, (((0,), (0,)), ((), ())), preferred_element_...  39.6 us
  transfers between devices with their start and end apart: 33, of which 19 were waited for; matrix products, arithmetic and copies ran while one was open for 22% of the time, Pallas kernels for 3%

profile of v1, /device:TPU:0, one launch (start us, length us, event | category | flops | bytes accessed | tf_op | source)
XLA Modules:
  0.0 956.9 jit_solution(4950117659294789895)
XLA Ops:
  20.2 67.8 %all_to_all.10 = bf16[8,2,48,1120]{3,2,1,0:T(8,128)(2,1)} all-to-all(bf16[8,2,48,1120]{3,2,1,0:T(8,128)(2,1)S(1)} %copy.126), channel_id=1, replica_groups=mesh['blk'=8,'pack'=4] {'blk'}, dimensions={0} | all-to-all | bytes 3440640 | tf_op jit(solution)/shard_map/all_to_all | solution.py:321
  91.1 12.2 %all-gather.11.cloned.1.call-done = bf16[1792,2048]{1,0:T(8,128)(2,1)} async-done(((bf16[56,2048]{1,0:T(8,128)(2,1)}), bf16[1792,2048]{1,0:T(8,128)(2,1)}) %all-gather.11.cloned.1.call-update) | async-done | bytes 7340048 | tf_op jit(solution)/shard_map/all_gather | solution.py:313
  152.7 14.8 %collective-permute-done.12 = bf16[256,1536]{1,0:T(8,128)(2,1)S(1)} collective-permute-done((bf16[256,1536]{1,0:T(8,128)(2,1)S(1)}, bf16[256,1536]{1,0:T(8,128)(2,1)S(1)}, u32[]{:S(2)}, u32[]{:S(2)}) %collective-permute-start.12) | collective-permute-done | bytes 786464 | tf_op jit(solution)/shard_map/ppermute | solution.py:24
  167.5 30.8 %collective-permute-done.13 = bf16[256,1536]{1,0:T(8,128)(2,1)S(1)} collective-permute-done((bf16[256,1536]{1,0:T(8,128)(2,1)S(1)}, bf16[256,1536]{1,0:T(8,128)(2,1)S(1)}, u32[]{:S(2)}, u32[]{:S(2)}) %collective-permute-start.13) | collective-permute-done | bytes 786464 | tf_op jit(solution)/shard_map/ppermute | solution.py:24
  198.4 15.0 %collective-permute-done.14 = bf16[256,1536]{1,0:T(8,128)(2,1)S(1)} collective-permute-done((bf16[256,1536]{1,0:T(8,128)(2,1)S(1)}, bf16[256,1536]{1,0:T(8,128)(2,1)S(1)}, u32[]{:S(2)}, u32[]{:S(2)}) %collective-permute-start.14) | collective-permute-done | bytes 786464 | tf_op jit(solution)/shard_map/ppermute | solution.py:24
  235.9 32.3 %collective-permute-start.4 = (bf16[256,1536]{1,0:T(8,128)(2,1)S(1)}, bf16[256,1536]{1,0:T(8,128)(2,1)S(1)}, u32[]{:S(2)}, u32[]{:S(2)}) collective-permute-start(bf16[256,1536]{1,0:T(8,128)(2,1)S(1)} %multiply_convert_fusion.3), channel_id=1, source_target_pairs={{0,8},{4,12},{8,16},{12,20},{16,24},{20,28},{24,0},{28,4},{1,9},{5... | collective-permute-start | bytes 2359304 | tf_op jit(solution)/shard_map/ppermute | solution.py:24
  268.3 16.6 %collective-permute-start.5 = (bf16[256,1536]{1,0:T(8,128)(2,1)S(1)}, bf16[256,1536]{1,0:T(8,128)(2,1)S(1)}, u32[]{:S(2)}, u32[]{:S(2)}) collective-permute-start(bf16[256,1536]{1,0:T(8,128)(2,1)S(1)} %multiply_convert_fusion.3), channel_id=1, source_target_pairs={{0,16},{4,20},{8,24},{12,28},{16,0},{20,4},{24,8},{28,12},{1,17},{... | collective-permute-start | bytes 2359304 | tf_op jit(solution)/shard_map/ppermute | solution.py:24
  285.2 15.6 %collective-permute-done.4 = bf16[256,1536]{1,0:T(8,128)(2,1)S(1)} collective-permute-done((bf16[256,1536]{1,0:T(8,128)(2,1)S(1)}, bf16[256,1536]{1,0:T(8,128)(2,1)S(1)}, u32[]{:S(2)}, u32[]{:S(2)}) %collective-permute-start.4) | collective-permute-done | bytes 786464 | tf_op jit(solution)/shard_map/ppermute | solution.py:24
  300.8 35.5 %collective-permute-done.5 = bf16[256,1536]{1,0:T(8,128)(2,1)S(1)} collective-permute-done((bf16[256,1536]{1,0:T(8,128)(2,1)S(1)}, bf16[256,1536]{1,0:T(8,128)(2,1)S(1)}, u32[]{:S(2)}, u32[]{:S(2)}) %collective-permute-start.5) | collective-permute-done | bytes 786464 | tf_op jit(solution)/shard_map/ppermute | solution.py:24
  370.0 12.8 %fusion.73 = f32[2048,1120]{0,1:T(8,128)} fusion(bf16[2048,1536]{1,0:T(8,128)(2,1)} %bitcast.235, bf16[1536,1120]{1,0:T(8,128)(2,1)} %bitcast.255), kind=kOutput, calls=%fused_computation.157 | convolution fusion | flops 7046430720 | bytes 18907136 | tf_op jit(solution)/shard_map/dot_general | solution.py:49
  401.1 20.2 %multiply_convert_fusion = (bf16[2048,1120]{0,1:T(8,128)(2,1)S(1)}, bf16[2048,1120]{0,1:T(8,128)(2,1)}, bf16[2048,1120]{0,1:T(8,128)(2,1)}) fusion(f32[2048,1120]{0,1:T(8,128)} %fusion.73, f32[2048,1120]{0,1:T(8,128)} %fusion.74, bf16[2048,1536]{1,0:T(8,128)(2,1)} %bitcast.242, bf16[1120,1536]{1,0:T(8,128)(2,1)} %all-gather.9.cloned.1.call-done), kind=kOutput, calls=%fused_computation.1 | convolution fusion | flops 7083130880 | bytes 41844736 | tf_op jit(solution)/shard_map/dot_general | solution.py:57
  421.3 12.2 %fusion.10 = bf16[1,8,4,48,1120]{4,3,2,1,0:T(8,128)(2,1)S(1)} fusion(bf16[8,4,48,2048]{3,2,1,0:T(8,128)(2,1)} %bitcast.246, bf16[2048,1120]{0,1:T(8,128)(2,1)S(1)} %get-tuple-element.27), kind=kOutput, calls=%fused_computation.21 | convolution fusion | flops 7048151040 | bytes 14319616 | tf_op jit(solution)/shard_map/dot_general | solution.py:53
  433.5 10.5 %fusion.13 = bf16[1,8,4,48,1120]{4,3,2,1,0:T(8,128)(2,1)S(1)} fusion(bf16[8,4,48,2048]{3,2,1,0:T(8,128)(2,1)} %bitcast.247, bf16[2048,1120]{0,1:T(8,128)(2,1)S(1)} %copy-done.41), kind=kOutput, calls=%fused_computation.22 | convolution fusion | flops 7048151040 | bytes 14319616 | tf_op jit(solution)/shard_map/dot_general | solution.py:53
  449.7 13.6 %fusion.75 = f32[2048,1536]{1,0:T(8,128)} fusion(bf16[2048,1120]{0,1:T(8,128)(2,1)} %get-tuple-element.28, bf16[1536,1120]{1,0:T(8,128)(2,1)S(1)} %bitcast.256), kind=kOutput, calls=%fused_computation.159 | convolution fusion | flops 7046430720 | bytes 20611072 | tf_op jit(solution)/shard_map/dot_general | solution.py:57
  463.3 13.5 %add_convert_fusion = bf16[2048,1536]{1,0:T(8,128)(2,1)S(1)} fusion(f32[2048,1536]{1,0:T(8,128)} %fusion.75, bf16[2048,1120]{0,1:T(8,128)(2,1)} %copy-done.40, bf16[1536,1120]{1,0:T(8,128)(2,1)} %bitcast.257), kind=kOutput, calls=%fused_computation | convolution fusion | flops 7052722176 | bytes 26902528 | tf_op jit(solution)/shard_map/dot_general | solution.py:57
  479.5 10.3 %convolution_convert_fusion.2 = bf16[1120,1536]{1,0:T(8,128)(2,1)} fusion(bf16[2048,1120]{0,1:T(8,128)(2,1)} %get-tuple-element.29, bf16[2048,1536]{1,0:T(8,128)(2,1)S(1)} %bitcast.245), kind=kOutput, calls=%fused_computation.7 | convolution fusion | flops 7048151040 | bytes 14319616 | tf_op jit(solution)/shard_map/dot_general | solution.py:53
  489.9 11.6 %convolution_convert_fusion = bf16[2048,1536]{1,0:T(8,128)(2,1)S(1)} fusion(bf16[2048,1120]{0,1:T(8,128)(2,1)} %get-tuple-element.29, bf16[1120,1536]{1,0:T(8,128)(2,1)} %all-gather.9.cloned.1.call-done), kind=kOutput, calls=%fused_computation.5 | convolution fusion | flops 7049576448 | bytes 14319616 | tf_op jit(solution)/shard_map/dot_general | solution.py:49
  535.0 85.5 %collective-permute-done.18 = bf16[256,1536]{1,0:T(8,128)(2,1)} collective-permute-done((bf16[256,1536]{1,0:T(8,128)(2,1)S(1)}, bf16[256,1536]{1,0:T(8,128)(2,1)}, u32[]{:S(2)}, u32[]{:S(2)}) %collective-permute-start.18) | collective-permute-done | bytes 786464 | tf_op jit(solution)/shard_map/ppermute | solution.py:24
  622.8 14.3 %collective-permute-done.10 = bf16[256,1536]{1,0:T(8,128)(2,1)S(1)} collective-permute-done((bf16[256,1536]{1,0:T(8,128)(2,1)S(1)}, bf16[256,1536]{1,0:T(8,128)(2,1)S(1)}, u32[]{:S(2)}, u32[]{:S(2)}) %collective-permute-start.10) | collective-permute-done | bytes 786464 | tf_op jit(solution)/shard_map/ppermute | solution.py:24
  655.1 13.8 %shard_map.188 = (bf16[256,1536]{1,0:T(8,128)(2,1)}, bf16[8,256,256]{2,1,0:T(8,128)(2,1)}, bf16[8,256,256]{2,1,0:T(8,128)(2,1)}) custom-call(s32[17]{0:T(128)} %pad_add_fusion.1.meta_ref, bf16[256,2048]{1,0:T(8,128)(2,1)} %shard_map.186.q_ref, bf16[256,1536]{1,0:T(8,128)(2,1)} %convolution_convert_fusion.4.dout_ref, f32[256,1536]{1,0:T(8,128)} %get-tuple-element.15.att_ref, ...), custom_call_target="tpu_custom_call" | custom-call | flops 8053063680 | bytes 2097152 | tf_op jit(solution)/shard_map/pallas_call | solution.py:246
  681.3 22.5 %collective-permute-done.21 = bf16[256,512]{1,0:T(8,128)(2,1)S(1)} collective-permute-done((bf16[256,512]{1,0:T(8,128)(2,1)}, bf16[256,512]{1,0:T(8,128)(2,1)S(1)}, u32[]{:S(2)}, u32[]{:S(2)}) %collective-permute-start.21) | collective-permute-done | bytes 262176 | tf_op jit(solution)/shard_map/ppermute | solution.py:24
  703.8 33.2 %collective-permute-done.22 = bf16[256,512]{1,0:T(8,128)(2,1)S(1)} collective-permute-done((bf16[256,512]{1,0:T(8,128)(2,1)}, bf16[256,512]{1,0:T(8,128)(2,1)S(1)}, u32[]{:S(2)}, u32[]{:S(2)}) %collective-permute-start.22) | collective-permute-done | bytes 262176 | tf_op jit(solution)/shard_map/ppermute | solution.py:24
  776.1 41.5 %all-to-all-done.1 = bf16[8,2,48,1120]{3,2,1,0:T(8,128)(2,1)S(1)} async-done(((bf16[8,2,48,1120]{3,2,1,0:T(8,128)(2,1)}), bf16[8,2,48,1120]{3,2,1,0:T(8,128)(2,1)S(1)}, u32[]{:S(2)}, u32[]{:S(2)}) %all-to-all-start.1) | async-done | bytes 1720352 | tf_op jit(solution)/shard_map/all_to_all | solution.py:363
  824.4 122.4 %reduce-scatter.9.cloned.1.call-done = bf16[1,56,2048]{2,1,0:T(8,128)(2,1)} async-done(((bf16[32,56,2048]{2,1,0:T(8,128)(2,1)}), bf16[1,56,2048]{2,1,0:T(8,128)(2,1)}) %reduce-scatter.9.cloned.1.call-update) | async-done | bytes 229392 | tf_op jit(solution)/shard_map/reduce_scatter | solution.py:403
  (270 shorter events, 262.8 us)
Async XLA Ops:
  7.2 96.2 %all-gather.11.cloned.1.call-start = ((), (), s32[]{:S(2)}) async-start(), calls=%async_computation.9 | async-start | bytes 7569408 | tf_op jit(solution)/shard_map/all_gather | solution.py:313
  11.7 218.4 %all-gather.7.cloned.1.call-start = ((), (), s32[]{:S(2)}) async-start(), calls=%async_computation.5 | async-start | bytes 4866048 | tf_op jit(solution)/shard_map/all_gather | solution.py:318
  13.4 332.8 %all-gather.13.cloned.1.call-start = ((), (), s32[]{:S(2)}) async-start(), calls=%async_computation.10 | async-start | bytes 8847360 | tf_op jit(solution)/shard_map/all_gather | solution.py:323
  88.0 313.0 %all-gather.9.cloned.1.call-start = ((), (), s32[]{:S(2)}) async-start(), calls=%async_computation.6 | async-start | bytes 4300800 | tf_op jit(solution)/shard_map/all_gather | solution.py:322
  130.8 36.7 %collective-permute-start.12 = (bf16[256,1536]{1,0:T(8,128)(2,1)S(1)}, bf16[256,1536]{1,0:T(8,128)(2,1)S(1)}, u32[]{:S(2)}, u32[]{:S(2)}) collective-permute-start(bf16[256,1536]{1,0:T(8,128)(2,1)S(1)} %bitcast.259), channel_id=1, source_target_pairs={{0,8},{4,12},{8,16},{12,20},{16,24},{20,28},{24,0},{28,4},{1,9},{5... | collective-permute-start | bytes 2359304 | tf_op jit(solution)/shard_map/ppermute | solution.py:24
  130.9 67.5 %collective-permute-start.13 = (bf16[256,1536]{1,0:T(8,128)(2,1)S(1)}, bf16[256,1536]{1,0:T(8,128)(2,1)S(1)}, u32[]{:S(2)}, u32[]{:S(2)}) collective-permute-start(bf16[256,1536]{1,0:T(8,128)(2,1)S(1)} %bitcast.260), channel_id=1, source_target_pairs={{0,16},{4,20},{8,24},{12,28},{16,0},{20,4},{24,8},{28,12},{1,17},{... | collective-permute-start | bytes 2359304 | tf_op jit(solution)/shard_map/ppermute | solution.py:24
  135.4 78.0 %collective-permute-start.14 = (bf16[256,1536]{1,0:T(8,128)(2,1)S(1)}, bf16[256,1536]{1,0:T(8,128)(2,1)S(1)}, u32[]{:S(2)}, u32[]{:S(2)}) collective-permute-start(bf16[256,1536]{1,0:T(8,128)(2,1)S(1)} %bitcast.261), channel_id=1, source_target_pairs={{0,24},{4,28},{8,0},{12,4},{16,8},{20,12},{24,16},{28,20},{1,25},{... | collective-permute-start | bytes 2359304 | tf_op jit(solution)/shard_map/ppermute | solution.py:24
  151.8 65.9 %collective-permute-start.3 = (bf16[4,256,512]{2,1,0:T(8,128)(2,1)}, bf16[4,256,512]{2,1,0:T(8,128)(2,1)}, u32[]{:S(2)}, u32[]{:S(2)}) collective-permute-start(bf16[4,256,512]{2,1,0:T(8,128)(2,1)} %get-tuple-element.56), channel_id=1, source_target_pairs={{0,4},{4,0},{8,12},{12,8},{16,20},{20,16},{24,28},{28,24},{1,5},{5... | collective-permute-start | bytes 3145736 | tf_op jit(solution)/shard_map/ppermute | solution.py:29
  217.6 122.8 %collective-permute-start.15 = (bf16[4,256,1536]{2,1,0:T(8,128)(2,1)}, bf16[4,256,1536]{2,1,0:T(8,128)(2,1)}, u32[]{:S(2)}, u32[]{:S(2)}) collective-permute-start(bf16[4,256,1536]{2,1,0:T(8,128)(2,1)} %get-tuple-element.44), channel_id=1, source_target_pairs={{0,4},{4,0},{8,12},{12,8},{16,20},{20,16},{24,28},{28,24},{1,5},{5... | collective-permute-start | bytes 9437192 | tf_op jit(solution)/shard_map/ppermute | solution.py:29
  235.9 64.9 %collective-permute-start.4 = (bf16[256,1536]{1,0:T(8,128)(2,1)S(1)}, bf16[256,1536]{1,0:T(8,128)(2,1)S(1)}, u32[]{:S(2)}, u32[]{:S(2)}) collective-permute-start(bf16[256,1536]{1,0:T(8,128)(2,1)S(1)} %multiply_convert_fusion.3), channel_id=1, source_target_pairs={{0,8},{4,12},{8,16},{12,20},{16,24},{20,28},{24,0},{28,4},{1,9},{5... | collective-permute-start | bytes 2359304 | tf_op jit(solution)/shard_map/ppermute | solution.py:24
  268.3 68.1 %collective-permute-start.5 = (bf16[256,1536]{1,0:T(8,128)(2,1)S(1)}, bf16[256,1536]{1,0:T(8,128)(2,1)S(1)}, u32[]{:S(2)}, u32[]{:S(2)}) collective-permute-start(bf16[256,1536]{1,0:T(8,128)(2,1)S(1)} %multiply_convert_fusion.3), channel_id=1, source_target_pairs={{0,16},{4,20},{8,24},{12,28},{16,0},{20,4},{24,8},{28,12},{1,17},{... | collective-permute-start | bytes 2359304 | tf_op jit(solution)/shard_map/ppermute | solution.py:24
  284.8 51.5 %collective-permute-start.6 = (bf16[256,1536]{1,0:T(8,128)(2,1)S(1)}, bf16[256,1536]{1,0:T(8,128)(2,1)S(1)}, u32[]{:S(2)}, u32[]{:S(2)}) collective-permute-start(bf16[256,1536]{1,0:T(8,128)(2,1)S(1)} %multiply_convert_fusion.3), channel_id=1, source_target_pairs={{0,24},{4,28},{8,0},{12,4},{16,8},{20,12},{24,16},{28,20},{1,25},{... | collective-permute-start | bytes 2359304 | tf_op jit(solution)/shard_map/ppermute | solution.py:24
  340.4 422.7 %all-reduce.6.cloned.1.call-start = ((), (), s32[]{:S(2)}) async-start(), calls=%async_computation.11 | async-start | bytes 14155776
  447.8 325.8 %reduce-scatter.13.cloned.1.call-start = ((), (), s32[]{:S(2)}) async-start(), calls=%async_computation.12 | async-start | bytes 4300800
  489.8 332.9 %reduce-scatter.11.cloned.1.call-start = ((), (), s32[]{:S(2)}) async-start(), calls=%async_computation.8 | async-start | bytes 4866048 | tf_op jit(solution)/shard_map/reduce_scatter | solution.py:372
  509.9 110.5 %collective-permute-start.18 = (bf16[256,1536]{1,0:T(8,128)(2,1)S(1)}, bf16[256,1536]{1,0:T(8,128)(2,1)}, u32[]{:S(2)}, u32[]{:S(2)}) collective-permute-start(bf16[256,1536]{1,0:T(8,128)(2,1)S(1)} %get-tuple-element.42), channel_id=1, source_target_pairs={{0,16},{4,20},{8,24},{12,28},{16,0},{20,4},{24,8},{28,12},{1,17},{... | collective-permute-start | bytes 2359304 | tf_op jit(solution)/shard_map/ppermute | solution.py:24
  517.6 102.8 %collective-permute-start.19 = (bf16[256,1536]{1,0:T(8,128)(2,1)S(1)}, bf16[256,1536]{1,0:T(8,128)(2,1)}, u32[]{:S(2)}, u32[]{:S(2)}) collective-permute-start(bf16[256,1536]{1,0:T(8,128)(2,1)S(1)} %get-tuple-element.41), channel_id=1, source_target_pairs={{0,8},{4,12},{8,16},{12,20},{16,24},{20,28},{24,0},{28,4},{1,9},{5... | collective-permute-start | bytes 2359304 | tf_op jit(solution)/shard_map/ppermute | solution.py:24
  520.9 116.2 %collective-permute-start.10 = (bf16[256,1536]{1,0:T(8,128)(2,1)S(1)}, bf16[256,1536]{1,0:T(8,128)(2,1)S(1)}, u32[]{:S(2)}, u32[]{:S(2)}) collective-permute-start(bf16[256,1536]{1,0:T(8,128)(2,1)S(1)} %get-tuple-element.47), channel_id=1, source_target_pairs={{0,16},{4,20},{8,24},{12,28},{16,0},{20,4},{24,8},{28,12},{1,17},{... | collective-permute-start | bytes 2359304 | tf_op jit(solution)/shard_map/ppermute | solution.py:24
  522.5 114.6 %collective-permute-start.11 = (bf16[256,1536]{1,0:T(8,128)(2,1)S(1)}, bf16[256,1536]{1,0:T(8,128)(2,1)S(1)}, u32[]{:S(2)}, u32[]{:S(2)}) collective-permute-start(bf16[256,1536]{1,0:T(8,128)(2,1)S(1)} %get-tuple-element.46), channel_id=1, source_target_pairs={{0,8},{4,12},{8,16},{12,20},{16,24},{20,28},{24,0},{28,4},{1,9},{5... | collective-permute-start | bytes 2359304 | tf_op jit(solution)/shard_map/ppermute | solution.py:24
  534.0 110.7 %collective-permute-start.9 = (bf16[256,1536]{1,0:T(8,128)(2,1)S(1)}, bf16[256,1536]{1,0:T(8,128)(2,1)S(1)}, u32[]{:S(2)}, u32[]{:S(2)}) collective-permute-start(bf16[256,1536]{1,0:T(8,128)(2,1)S(1)} %get-tuple-element.45), channel_id=1, source_target_pairs={{0,24},{4,28},{8,0},{12,4},{16,8},{20,12},{24,16},{28,20},{1,25},{... | collective-permute-start | bytes 2359304 | tf_op jit(solution)/shard_map/ppermute | solution.py:24
  650.4 296.4 %reduce-scatter.9.cloned.1.call-start = ((), (), s32[]{:S(2)}) async-start(), calls=%async_computation.7 | async-start | bytes 7569408 | tf_op jit(solution)/shard_map/reduce_scatter | solution.py:403
  677.4 59.6 %collective-permute-start.22 = (bf16[256,512]{1,0:T(8,128)(2,1)}, bf16[256,512]{1,0:T(8,128)(2,1)S(1)}, u32[]{:S(2)}, u32[]{:S(2)}) collective-permute-start(bf16[256,512]{1,0:T(8,128)(2,1)} %get-tuple-element.54), channel_id=1, source_target_pairs={{16,0},{20,4},{24,8},{28,12},{17,1},{21,5},{25,9},{29,13},{18,2},{... | collective-permute-start | bytes 786440 | tf_op jit(solution)/shard_map/ppermute | solution.py:24
  678.7 58.4 %collective-permute-start.23 = (bf16[256,512]{1,0:T(8,128)(2,1)}, bf16[256,512]{1,0:T(8,128)(2,1)}, u32[]{:S(2)}, u32[]{:S(2)}) collective-permute-start(bf16[256,512]{1,0:T(8,128)(2,1)} %get-tuple-element.53), channel_id=1, source_target_pairs={{24,0},{28,4},{25,1},{29,5},{26,2},{30,6},{27,3},{31,7}} | collective-permute-start | bytes 786440 | tf_op jit(solution)/shard_map/ppermute | solution.py:24
  766.7 50.9 %all-to-all-start.1 = ((bf16[8,2,48,1120]{3,2,1,0:T(8,128)(2,1)}), bf16[8,2,48,1120]{3,2,1,0:T(8,128)(2,1)S(1)}, u32[]{:S(2)}, u32[]{:S(2)}) async-start(bf16[8,2,48,1120]{3,2,1,0:T(8,128)(2,1)} %copy.141), calls=%async_computation.3 | async-start | bytes 3538944 | tf_op jit(solution)/shard_map/all_to_all | solution.py:363
  (55 other events, 1357.3 us)
Sparse Core Ops, SparseCore 0:
  11.9 91.4 all-gather.10
  106.8 106.1 all-gather.6
  214.9 86.3 all-gather.12
  340.5 60.5 all-gather.8
  447.9 157.7 all-reduce.5
  608.6 46.3 reduce-scatter.12
  660.5 118.7 reduce-scatter.10
  781.7 165.0 reduce-scatter.8

commit v2 on v1

v2 whole, which is shorter than its diff:
```python
import functools

import jax
import jax.numpy as jnp
from jax import lax
from jax.experimental import pallas as pl
from jax.experimental.pallas import tpu as pltpu
from jax.sharding import PartitionSpec as P

H = 12
KVH = 2
HD = 128
G = H // KVH
NEG = -1e30
BF = jnp.bfloat16
F32 = jnp.float32
VMEM_LIMIT = 56 * 1024 * 1024
BOTH = ("blk", "pack")


def chip_shift(block, by, cyclic=True):
    n = lax.axis_size("blk")
    route = [(i, (i + 2 * by) % n) for i in range(n) if cyclic or 0 <= i + 2 * by < n]
    return lax.ppermute(block, "blk", route)


def core_swap(block):
    n = lax.axis_size("blk")
    return lax.ppermute(block, "blk", [(i, i ^ 1) for i in range(n)])


def pack_swap(block, k):
    n = lax.axis_size("pack")
    return lax.ppermute(block, "pack", [(i, i ^ k) for i in range(n)])


def put(buffer, piece, *index):
    piece = piece.reshape((1,) * len(index) + piece.shape)
    zeros = (0,) * (buffer.ndim - len(index))
    return lax.dynamic_update_slice(buffer, piece, tuple(index) + zeros)


def take(array, axis, index):
    return lax.dynamic_index_in_dim(array, index, axis, keepdims=False)


class Place:
    def __init__(self):
        self.blocks, self.packs = lax.axis_size("blk"), lax.axis_size("pack")
        self.chips = self.blocks // 2
        self.blk, self.pack = lax.axis_index("blk"), lax.axis_index("pack")
        self.chip, self.core = self.blk // 2, self.blk % 2

    def chip_at(self, by):
        return lax.rem(self.chip + by + self.chips, self.chips)


def in_core_order(place, mine, other):
    first = jnp.where(place.core == 0, mine, other)
    second = jnp.where(place.core == 0, other, mine)
    return jnp.stack([first, second], axis=1)


def after(value, *before):
    return lax.optimization_barrier((value, before))[0]


def gather_line(block):
    chips = lax.axis_size("blk") // 2
    return jnp.stack([block] + [chip_shift(block, s) for s in range(1, chips)])


def exchange_packs(place, parts):
    got = [take(parts, 0, place.pack)]
    for k in range(1, place.packs):
        got.append(pack_swap(take(parts, 0, place.pack ^ k), k))
    return got


def reduce_line(place, parts):
    other = core_swap(take(parts, 1, 1 - place.core))
    mine = take(parts, 1, place.core).astype(F32) + other.astype(F32)
    line = mine.astype(BF)
    total = take(mine, 0, place.chip)
    for s in range(1, place.chips):
        total = total + chip_shift(take(line, 0, place.chip_at(s)), s).astype(F32)
    return total


def by_columns(matrix, packs):
    return jnp.stack(jnp.split(matrix, packs, axis=1))


def in_pack_order(place, pieces):
    ordered = []
    for q in range(place.packs):
        chosen = pieces[q]
        for p in range(1, place.packs):
            chosen = jnp.where(place.pack == p, pieces[q ^ p], chosen)
        ordered.append(chosen)
    return ordered


def to_shard(place, grad, depth):
    pieces = exchange_packs(place, grad.reshape(place.packs, depth, -1))
    return jnp.concatenate(in_pack_order(place, pieces), axis=1).astype(F32)


def exchange_line(place, parts, beside=()):
    got = jnp.zeros(parts.shape, parts.dtype)
    got = put(got, take(parts, 0, place.chip), place.chip)
    for s in range(1, place.chips):
        got = put(got, chip_shift(take(parts, 0, place.chip_at(s)), s), place.chip_at(-s))
    got = after(got, beside)
    other = core_swap(take(got, 1, 1 - place.core))
    return in_core_order(place, take(got, 1, place.core), other)


def matmul(left, right):
    return jnp.dot(left, right, preferred_element_type=F32)


def matmul_tn(left, right):
    return lax.dot_general(left, right, (((0,), (0,)), ((), ())), preferred_element_type=F32)


def matmul_nt(left, right):
    return lax.dot_general(left, right, (((1,), (1,)), ((), ())), preferred_element_type=F32)


def rms_norm(values, gain):
    return values * lax.rsqrt(jnp.mean(values * values, axis=-1, keepdims=True) + 1e-06) * gain


def turn(x, cosine, sine):
    return x * cosine + pltpu.roll(x, HD // 2, 1) * sine


def qkv_kernel(xn_ref, w_ref, bias_ref, cos_ref, sin_ref, out_ref):
    step = pl.program_id(0)
    proj = matmul(xn_ref[...], w_ref[...]) + bias_ref[...]
    cosine, sine = cos_ref[...], sin_ref[...]

    @pl.when(step < H // 2)
    def _():
        for i in range(2):
            cut = slice(i * HD, (i + 1) * HD)
            out_ref[:, cut] = (turn(proj[:, cut], cosine, sine) * HD**-0.5).astype(BF)

    @pl.when((step >= H // 2) & (step < (H + KVH) // 2))
    def _():
        for i in range(2):
            cut = slice(i * HD, (i + 1) * HD)
            out_ref[:, cut] = turn(proj[:, cut], cosine, sine).astype(BF)

    @pl.when(step >= (H + KVH) // 2)
    def _():
        out_ref[...] = proj.astype(BF)


def qkv_project(xn, w, bias, cosine, sine):
    rows, depth = xn.shape
    cols = w.shape[1]
    return pl.pallas_call(
        qkv_kernel,
        grid=(cols // 256,),
        in_specs=[
            pl.BlockSpec((rows, depth), lambda i: (0, 0)),
            pl.BlockSpec((depth, 256), lambda i: (0, i)),
            pl.BlockSpec((1, 256), lambda i: (0, i)),
            pl.BlockSpec((rows, HD), lambda i: (0, 0)),
            pl.BlockSpec((rows, HD), lambda i: (0, 0)),
        ],
        out_specs=pl.BlockSpec((rows, 256), lambda i: (0, i)),
        out_shape=jax.ShapeDtypeStruct((rows, cols), BF),
        compiler_params=pltpu.CompilerParams(vmem_limit_bytes=VMEM_LIMIT),
        cost_estimate=pl.CostEstimate(
            flops=2 * rows * depth * cols, bytes_accessed=2 * depth * cols, transcendentals=0
        ),
    )(xn, w, bias, cosine, sine)


def allowed_mask(meta_ref, starts_ref, slot, count):
    rows, lanes = starts_ref.shape[1], G * starts_ref.shape[1]
    starts = jnp.concatenate([starts_ref[...]] * G, axis=1)
    key_index = meta_ref[1 + count + slot] + lax.broadcasted_iota(jnp.int32, (rows, lanes), 0)
    query = lax.rem(lax.broadcasted_iota(jnp.int32, (1, lanes), 1), rows)
    return (key_index >= starts) & (key_index <= meta_ref[0] + query)


def stack_heads(target, source_ref):
    rows = source_ref.shape[0]
    for g in range(G):
        target[g * rows : (g + 1) * rows, :] = source_ref[:, g * HD : (g + 1) * HD]


def when_needed(meta_ref, count, work, pieces):
    slot = pl.program_id(1)
    state = meta_ref[1 + slot]
    for core, (k_ref, v_ref) in enumerate(pieces):
        here = slot < count // 2 if core == 0 else slot >= count // 2
        for masked in (True, False):

            @pl.when(here & (state == (1 if masked else 2)))
            def _(k_ref=k_ref, v_ref=v_ref, masked=masked):
                work(k_ref[0], v_ref[0], masked)


def forward_kernel(
    count, meta_ref, q_ref, starts_ref, k0_ref, v0_ref, k1_ref, v1_ref,
    att_ref, low_ref, lse_ref, q, m, total, acc,
):
    slot = pl.program_id(1)
    rows = q_ref.shape[0]

    @pl.when(slot == 0)
    def _():
        stack_heads(q, q_ref)
        m[...] = jnp.full(m.shape, NEG, F32)
        total[...] = jnp.zeros(total.shape, F32)
        acc[...] = jnp.zeros(acc.shape, F32)

    def work(keys, values, masked):
        scores = matmul_nt(keys, q[...])
        if masked:
            scores = jnp.where(allowed_mask(meta_ref, starts_ref, slot, count), scores, NEG)
        before = m[...]
        now = jnp.maximum(before, jnp.max(scores, axis=0, keepdims=True))
        weights = jnp.exp(scores - now)
        fade = jnp.exp(before - now)
        m[...] = now
        total[...] = total[...] * fade + jnp.sum(weights, axis=0, keepdims=True)
        acc[...] = acc[...] * fade + matmul_tn(values, weights.astype(BF))

    when_needed(meta_ref, count, work, ((k0_ref, v0_ref), (k1_ref, v1_ref)))

    @pl.when(slot == count - 1)
    def _():
        out = acc[...] / total[...]
        for g in range(G):
            head = out[:, g * rows : (g + 1) * rows].T
            att_ref[:, g * HD : (g + 1) * HD] = head
            low_ref[:, g * HD : (g + 1) * HD] = head.astype(BF)
        lse_ref[0] = m[...] + jnp.log(total[...])


def kv_specs(count, rows):
    half = count // 2
    specs = []
    for core in range(2):
        for first in (0, KVH):

            def where(h, j, meta_ref, core=core, first=first):
                here = (j < half) if core == 0 else (j >= half)
                index = jnp.where(here & (meta_ref[1 + j] > 0), j - core * half, 0)
                return (index, 0, first + h)

            specs.append(pl.BlockSpec((1, rows, HD), where))
    return specs


def attention_forward(meta, qkv, starts, line, other):
    count, rows = 2 * line.shape[0], line.shape[1]
    width = G * HD
    by_head = lambda h, j, meta_ref: (0, h)
    return pl.pallas_call(
        functools.partial(forward_kernel, count),
        grid_spec=pltpu.PrefetchScalarGridSpec(
            num_scalar_prefetch=1,
            grid=(KVH, count),
            in_specs=[
                pl.BlockSpec((rows, width), by_head),
                pl.BlockSpec((1, rows), lambda h, j, meta_ref: (0, 0)),
            ]
            + kv_specs(count, rows),
            out_specs=[
                pl.BlockSpec((rows, width), by_head),
                pl.BlockSpec((rows, width), by_head),
                pl.BlockSpec((1, 1, G * rows), lambda h, j, meta_ref: (h, 0, 0)),
            ],
            scratch_shapes=[
                pltpu.VMEM((G * rows, HD), BF),
                pltpu.VMEM((1, G * rows), F32),
                pltpu.VMEM((1, G * rows), F32),
                pltpu.VMEM((HD, G * rows), F32),
            ],
        ),
        out_shape=[
            jax.ShapeDtypeStruct((rows, H * HD), F32),
            jax.ShapeDtypeStruct((rows, H * HD), BF),
            jax.ShapeDtypeStruct((KVH, 1, G * rows), F32),
        ],
        compiler_params=pltpu.CompilerParams(vmem_limit_bytes=VMEM_LIMIT),
        cost_estimate=pl.CostEstimate(
            flops=16 * rows * rows * count * H * HD,
            bytes_accessed=count * rows * 1024,
            transcendentals=rows * rows * count * H,
        ),
    )(meta, qkv, starts, line, line, other, other)


def backward_kernel(
    count, meta_ref, q_ref, dout_ref, att_ref, lse_ref, starts_ref, k0_ref, v0_ref, k1_ref, v1_ref,
    cos_ref, sin_ref, dq_ref, dk0_ref, dv0_ref, dk1_ref, dv1_ref, q, dout, delta, dq_sum,
):
    slot = pl.program_id(1)
    rows = q_ref.shape[0]
    half = count // 2

    @pl.when(slot == 0)
    def _():
        stack_heads(q, q_ref)
        stack_heads(dout, dout_ref)
        dq_sum[...] = jnp.zeros(dq_sum.shape, F32)
        for g in range(G):
            cut = slice(g * HD, (g + 1) * HD)
            product = dout_ref[:, cut].astype(F32) * att_ref[:, cut]
            delta[:, g * rows : (g + 1) * rows] = jnp.sum(product.T, axis=0, keepdims=True)

    def work(keys, values, masked):
        weights = jnp.exp(matmul_nt(keys, q[...]) - lse_ref[0])
        if masked:
            weights = jnp.where(allowed_mask(meta_ref, starts_ref, slot, count), weights, 0.0)
        dv = matmul(weights.astype(BF), dout[...]).astype(BF)
        dscores = (weights * (matmul_nt(values, dout[...]) - delta[...])).astype(BF)
        dk = matmul(dscores, q[...]).astype(BF)
        dq_sum[...] = dq_sum[...] + matmul_tn(keys, dscores)

        @pl.when(slot < half)
        def _():
            dk0_ref[0], dv0_ref[0] = dk, dv

        @pl.when(slot >= half)
        def _():
            dk1_ref[0], dv1_ref[0] = dk, dv

    @pl.when((meta_ref[1 + slot] == 0) & (slot < half))
    def _():
        dk0_ref[...] = jnp.zeros(dk0_ref.shape, BF)
        dv0_ref[...] = jnp.zeros(dv0_ref.shape, BF)

    @pl.when((meta_ref[1 + slot] == 0) & (slot >= half))
    def _():
        dk1_ref[...] = jnp.zeros(dk1_ref.shape, BF)
        dv1_ref[...] = jnp.zeros(dv1_ref.shape, BF)

    when_needed(meta_ref, count, work, ((k0_ref, v0_ref), (k1_ref, v1_ref)))

    @pl.when(slot == count - 1)
    def _():
        for g in range(G):
            back = dq_sum[:, g * rows : (g + 1) * rows].T * HD**-0.5
            dq_ref[:, g * HD : (g + 1) * HD] = turn(back, cos_ref[...], -sin_ref[...]).astype(BF)


def attention_backward(meta, qkv, dout, att, lse, starts, line, other, cosine, sine):
    chips, rows = line.shape[:2]
    count = 2 * chips
    width = G * HD
    whole = lambda h, j, meta_ref: (0, 0)
    by_head = lambda h, j, meta_ref: (0, h)
    own = pl.BlockSpec((1, rows, HD), lambda h, j, meta_ref: (jnp.minimum(j, chips - 1), 0, h))
    far = pl.BlockSpec((1, rows, HD), lambda h, j, meta_ref: (jnp.maximum(j - chips, 0), 0, h))
    return pl.pallas_call(
        functools.partial(backward_kernel, count),
        grid_spec=pltpu.PrefetchScalarGridSpec(
            num_scalar_prefetch=1,
            grid=(KVH, count),
            in_specs=[
                pl.BlockSpec((rows, width), by_head),
                pl.BlockSpec((rows, width), by_head),
                pl.BlockSpec((rows, width), by_head),
                pl.BlockSpec((1, 1, G * rows), lambda h, j, meta_ref: (h, 0, 0)),
                pl.BlockSpec((1, rows), whole),
            ]
            + kv_specs(count, rows)
            + [pl.BlockSpec((rows, HD), whole)] * 2,
            out_specs=[pl.BlockSpec((rows, width), by_head), own, own, far, far],
            scratch_shapes=[
                pltpu.VMEM((G * rows, HD), BF),
                pltpu.VMEM((G * rows, HD), BF),
                pltpu.VMEM((1, G * rows), F32),
                pltpu.VMEM((HD, G * rows), F32),
            ],
        ),
        out_shape=[jax.ShapeDtypeStruct((rows, H * HD), BF)]
        + [jax.ShapeDtypeStruct((chips, rows, KVH * HD), BF)] * 4,
        compiler_params=pltpu.CompilerParams(vmem_limit_bytes=VMEM_LIMIT),
        cost_estimate=pl.CostEstimate(
            flops=100 * rows * rows * count * H * HD,
            bytes_accessed=count * rows * 1024,
            transcendentals=rows * rows * count * H,
        ),
    )(meta, qkv, dout, att, lse, starts, line, line, other, other, cosine, sine)


def assemble_kernel(packs, depth, at_ref, *refs):
    *sources, out_ref, sems = refs
    chips = sources[0].shape[0]
    chip, core, pack = at_ref[0], at_ref[1], at_ref[2]
    copies = []
    for n, source in enumerate(sources):
        k, other = n // 2, n % 2
        for s in range(chips):
            place = lax.rem(chip - s + chips, chips) * 2 + (core ^ other)
            start = pl.multiple_of((place * packs + (pack ^ k)) * depth, depth)
            copies.append(
                pltpu.make_async_copy(
                    source.at[s, pl.ds(0, depth)],
                    out_ref.at[pl.ds(start, depth)],
                    sems.at[len(copies)],
                )
            )
    for copy in copies:
        copy.start()
    for copy in copies:
        copy.wait()


def assemble(place, lines, depth):
    chips, _, cols = lines[0].shape
    count = len(lines) * chips
    if depth % 16:
        out = jnp.zeros((count, depth, cols), lines[0].dtype)
        for n, line in enumerate(lines):
            for s in range(chips):
                where = (place.chip_at(-s) * 2 + (place.core ^ (n % 2))) * place.packs
                out = put(out, line[s, :depth], where + (place.pack ^ (n // 2)))
        return out.reshape(count * depth, cols)
    at = jnp.stack([place.chip, place.core, place.pack]).astype(jnp.int32)
    return pl.pallas_call(
        functools.partial(assemble_kernel, place.packs, depth),
        grid_spec=pltpu.PrefetchScalarGridSpec(
            num_scalar_prefetch=1,
            grid=(1,),
            in_specs=[pl.BlockSpec(memory_space=pl.ANY)] * len(lines),
            out_specs=pl.BlockSpec((count * depth, cols), lambda i, at_ref: (0, 0)),
            scratch_shapes=[pltpu.SemaphoreType.DMA((count,))],
        ),
        out_shape=jax.ShapeDtypeStruct((count * depth, cols), lines[0].dtype),
        compiler_params=pltpu.CompilerParams(vmem_limit_bytes=VMEM_LIMIT),
        cost_estimate=pl.CostEstimate(
            flops=0, bytes_accessed=4 * count * depth * cols, transcendentals=0
        ),
    )(at, *lines)


def feed_kernel(
    h0_ref, h1_ref, t0_ref, t1_ref, gate_ref, up_ref, down_ref, *refs
):
    act0_ref, dgate0_ref, dup0_ref, act1_ref, dgate1_ref, dup1_ref, own_ref, other_ref, h, t = refs[-10:]
    rows = h0_ref.shape[1]
    h[:rows], h[rows:] = h0_ref[0], h1_ref[0]
    t[:rows], t[rows:] = t0_ref[0], t1_ref[0]
    gate = matmul(h[...], gate_ref[...])
    up = matmul(h[...], up_ref[...])
    dact = matmul_nt(t[...], down_ref[...])
    sig = 1.0 / (1.0 + jnp.exp(-gate))
    silu = gate * sig
    act = (silu * up).astype(BF)
    dgate = (dact * up * (sig * (1.0 + gate * (1.0 - sig)))).astype(BF)
    dup = (dact * silu).astype(BF)
    act0_ref[0], act1_ref[0] = act[:rows], act[rows:]
    dgate0_ref[0], dgate1_ref[0] = dgate[:rows], dgate[rows:]
    dup0_ref[0], dup1_ref[0] = dup[:rows], dup[rows:]
    part = matmul_nt(dgate, gate_ref[...]) + matmul_nt(dup, up_ref[...])
    own_ref[0] = part[:rows]
    other_ref[0] = part[rows:].astype(BF)


def feed(hs, ts, gate_w, up_w, down):
    count, rows, width = hs[0].shape
    ff = gate_w.shape[1]
    entry = lambda i: (i, 0, 0)
    whole = lambda i: (0, 0)
    once = pl.Buffered(1)
    tokens = pl.BlockSpec((1, rows, width), entry)
    column = pl.BlockSpec((1, rows, ff), entry)
    return pl.pallas_call(
        feed_kernel,
        grid=(count,),
        in_specs=[tokens] * 4
        + [
            pl.BlockSpec((width, ff), whole, pipeline_mode=once),
            pl.BlockSpec((width, ff), whole, pipeline_mode=once),
            pl.BlockSpec((ff, width), whole, pipeline_mode=once),
        ],
        out_specs=[column] * 6 + [tokens] * 2,
        out_shape=[jax.ShapeDtypeStruct((count, rows, ff), BF)] * 6
        + [
            jax.ShapeDtypeStruct((count, rows, width), F32),
            jax.ShapeDtypeStruct((count, rows, width), BF),
        ],
        scratch_shapes=[pltpu.VMEM((2 * rows, width), BF)] * 2,
        compiler_params=pltpu.CompilerParams(vmem_limit_bytes=VMEM_LIMIT),
        cost_estimate=pl.CostEstimate(
            flops=25 * count * rows * width * ff,
            bytes_accessed=6 * width * ff,
            transcendentals=2 * count * rows * ff,
        ),
    )(*hs, *ts, gate_w, up_w, down)


def grads_kernel(packs, n, *refs):
    *refs, out_ref = refs
    _, near, _, depth, ff = out_ref.shape
    for i in range(2):
        grad = sum(matmul_tn(refs[j][...], refs[n + i * n + j][...]) for j in range(n))
        grad = grad.astype(BF).reshape(near, packs, depth, ff)
        for p in range(packs):
            out_ref[p, :, i] = grad[:, p]


def gate_up_grads(blocks, packs, depth, ff, hs, dgates, dups):
    width = hs[0].shape[1]
    tile = width // 4
    if depth % 16 or tile % (packs * depth):
        grads = [sum(matmul_tn(h, d) for h, d in zip(hs, ds)).astype(BF) for ds in (dgates, dups)]
        return jnp.stack(grads).reshape(2, blocks, packs, depth, ff).transpose(2, 1, 0, 3, 4)
    near = tile // (packs * depth)
    columns = [pl.BlockSpec((h.shape[0], tile), lambda j: (0, j)) for h in hs]
    once = pl.Buffered(1)
    kept = [pl.BlockSpec(d.shape, lambda j: (0, 0), pipeline_mode=once) for d in dgates + dups]
    rows = sum(h.shape[0] for h in hs)
    return pl.pallas_call(
        functools.partial(grads_kernel, packs, len(hs)),
        grid=(4,),
        in_specs=columns + kept,
        out_specs=pl.BlockSpec((packs, near, 2, depth, ff), lambda j: (0, j, 0, 0, 0)),
        out_shape=jax.ShapeDtypeStruct((packs, blocks, 2, depth, ff), BF),
        compiler_params=pltpu.CompilerParams(vmem_limit_bytes=VMEM_LIMIT),
        cost_estimate=pl.CostEstimate(
            flops=7 * rows * width * ff, bytes_accessed=6 * rows * ff, transcendentals=0
        ),
    )(*hs, *dgates, *dups)


def on_device(
    tokens, lengths, out_grad, w_qkv, b_qkv, w_out, gain_attn, w_gate, w_up, w_down, gain_mlp
):
    rows, width = tokens.shape[1:]
    place = Place()
    blocks, packs, chips = place.blocks, place.packs, place.chips
    blk, chip, core = place.blk, place.chip, place.core
    depth = w_qkv.shape[0]
    qkv_cols = w_qkv.shape[1]
    ff = w_gate.shape[1] // blocks
    q_cols = H * HD

    token_index = blk * rows + jnp.arange(rows, dtype=jnp.int32)
    ends = jnp.cumsum(lengths[0])
    doc_starts = ends - lengths[0]
    inside = (token_index[:, None] >= doc_starts[None, :]) & (token_index[:, None] < ends[None, :])
    begin = jnp.sum(jnp.where(inside, doc_starts[None, :], 0), axis=1)
    half = HD // 2
    freq = 10000.0 ** (-2.0 * jnp.arange(half, dtype=F32) / HD)
    angle = (token_index - begin).astype(F32)[:, None] * freq[None, :]
    cosine, sine = jnp.cos(angle), jnp.sin(angle)
    cosine = jnp.concatenate([cosine, cosine], axis=1)
    sine = jnp.concatenate([-sine, sine], axis=1)
    starts = begin[None, :].astype(jnp.int32)

    bias_n, gain_n = b_qkv.shape[0], gain_attn.shape[0]
    shard = blk * packs + place.pack

    def placed(vector):
        row = jnp.zeros((qkv_cols,), BF)
        return lax.dynamic_update_slice(row, vector.astype(BF), (shard * vector.shape[0],))

    spare = jnp.stack([placed(b_qkv), placed(gain_attn), placed(gain_mlp)])
    spare = jnp.pad(spare, ((0, 5), (0, 0)))
    line = gather_line(jnp.concatenate([w_qkv.astype(BF), spare]))
    grad_top = out_grad[0]
    gate_up = jnp.stack([w_gate, w_up]).astype(BF).reshape(2, depth, chips, 2, ff)
    gate_up = after(gate_up.transpose(2, 3, 0, 1, 4), line)
    lines = [line] + [pack_swap(line, k) for k in range(1, packs)]
    lines = [piece for line in lines for piece in (line, core_swap(after(line, lines[1])))]
    gate_up = exchange_line(place, gate_up, lines).reshape(blocks, 2, depth, ff)
    vectors = sum(jnp.sum(piece[:, depth:].astype(F32), axis=0) for piece in lines)
    bias = vectors[:1]
    attn_gain, mlp_gain = vectors[1, :width], vectors[2, :width]
    out_line = gather_line(after(w_out.astype(BF), gate_up))
    qkv_full = assemble(place, lines, depth)

    down = lax.all_gather(after(w_down, lines[2]).astype(BF), "pack", axis=0, tiled=True)
    out_lines = [out_line] + [pack_swap(out_line, k) for k in range(1, packs)]

    def whole(part):
        part = lax.all_gather(part.reshape(blocks * depth, ff), "pack", axis=0, tiled=True)
        part = part.reshape(packs, blocks, depth, ff).transpose(1, 0, 2, 3)
        return part.reshape(width, ff)

    gate_w, up_w = whole(gate_up[:, 0]), whole(gate_up[:, 1])

    stream = tokens[0].astype(F32)
    normed = rms_norm(stream, attn_gain).astype(BF)
    qkv = qkv_project(normed, qkv_full, bias, cosine, sine)
    own = qkv[:, q_cols:]
    kv_line = jnp.stack([own] + [chip_shift(own, s, cyclic=False) for s in range(1, chips)])
    top = after(out_grad[0], gate_up)
    t = {0: grad_top, 1: chip_shift(top, 1)}
    if chips > 2:
        t[chips - 1] = chip_shift(top, -1)
    kv_other = core_swap(after(kv_line, out_lines, t[1]))
    back = jnp.arange(chips, dtype=jnp.int32)
    source = jnp.concatenate([(chip - back) * 2 + core, (chip - back) * 2 + 1 - core])
    valid = ((source >= 0) & (source <= blk)).astype(jnp.int32)
    clear = ((source < blk) & (source * rows >= jnp.max(begin))).astype(jnp.int32)
    meta = jnp.concatenate([(blk * rows)[None], valid * (1 + clear), source * rows])
    meta = meta.astype(jnp.int32)
    att, att_low, lse = attention_forward(meta, qkv, starts, kv_line, kv_other)
    out_lines = after(out_lines, att_low)
    out_lines = [piece for line in out_lines for piece in (line, core_swap(line))]
    out_full = assemble(place, out_lines, depth)
    att_low = after(att_low, t[chips - 1])
    middle = stream + matmul(att_low, out_full)

    hidden = rms_norm(middle, mlp_gain).astype(BF)

    normed_all = lax.all_gather(after(normed, up_w, down), "pack", axis=0, tiled=True)
    att_all = lax.all_gather(after(att_low, up_w, down), "pack", axis=0, tiled=True)

    def both(blocks):
        line = jnp.stack(blocks)
        return line, core_swap(line)

    def pass_back(parts):
        parts = dict(parts)
        for s in reversed(range(2, chips - 1)):
            parts[s - 1] = parts[s - 1] + chip_shift(parts[s].astype(BF), -1).astype(F32)
        return parts

    def give_back(parts):
        total = parts[0] + chip_shift(parts[1].astype(BF), -1).astype(F32)
        if chips > 2:
            total = total + chip_shift(parts[chips - 1].astype(BF), 1).astype(F32)
        return total

    h = {0: hidden, 1: chip_shift(hidden, 1)}
    if chips > 2:
        h[chips - 1] = chip_shift(hidden, -1)
    for s in range(2, chips - 1):
        h[s], t[s] = chip_shift(h[s - 1], 1), chip_shift(t[s - 1], 1)
    h[0], h[chips - 1] = after((h[0], h[chips - 1]), h[chips - 1])
    h[1] = after(h[1], h[chips - 1])
    first, second = (list(range(chips - 2, 0, -1)), [chips - 1, 0]) if chips > 2 else ([1, 0], [])
    hs, ts, fed, partials = [], [], [], {}
    for part in (first, second):
        if not part:
            continue
        h_pair, t_pair = both([h[s] for s in part]), both([t[s] for s in part])
        if partials:
            h_pair = after(h_pair, other)
        *kept, mine, other = feed(h_pair, t_pair, gate_w, up_w, down)
        mine = mine + core_swap(other).astype(F32)
        partials.update({s: mine[i] for i, s in enumerate(part)})
        flat = lambda arrays: [one.reshape(len(part) * rows, -1) for one in arrays]
        hs, ts = hs + flat(h_pair), ts + flat(t_pair)
        fed.append(flat(kept))
    acts, dgates, dups = ([one for kept in fed for one in kept[i::3]] for i in range(3))
    partials = pass_back(partials)
    hs = after(hs, partials)
    grad_hidden = give_back(partials)

    grad_gu = gate_up_grads(blocks, packs, depth, ff, hs, dgates, dups)
    out_parts, outs = [matmul(act, down) for act in after(acts, grad_gu)], {}
    for i, part in enumerate((first, second)):
        if part:
            other = core_swap(out_parts[2 * i + 1].astype(BF))
            mine = (out_parts[2 * i] + other.astype(F32)).reshape(len(part), rows, width)
            outs.update({s: mine[n] for n, s in enumerate(part)})
    grad_hidden = after(grad_hidden, grad_gu)

    grad_gu = after(grad_gu, normed_all, att_all).reshape(packs * blocks * 2 * depth, ff)
    grad_gu = lax.psum_scatter(grad_gu, "pack", scatter_dimension=0, tiled=True)
    gu_here = exchange_line(place, grad_gu.reshape(chips, 2, 2, depth, ff))

    _, second_pull = jax.vjp(rms_norm, middle, mlp_gain)
    grad_mid, grad_mlp_gain = second_pull(grad_hidden)
    grad_middle = grad_top.astype(F32) + grad_mid

    middle_low = grad_middle.astype(BF)

    dout = matmul_nt(middle_low, out_full).astype(BF).reshape(rows, q_cols)
    dout, outs = after((dout, outs), dout, outs)
    outs = pass_back(outs)
    if chips > 2:
        outs[chips - 1] = chip_shift(outs[chips - 1].astype(BF), 1)
    dq, dk0, dv0, dk1, dv1 = attention_backward(
        meta, qkv, dout, att, lse, starts, kv_line, kv_other, cosine, sine
    )
    dk1, dv1, outs = after((dk1, dv1, outs), outs)
    result = middle + outs[0] + chip_shift(outs[1].astype(BF), -1).astype(F32)
    if chips > 2:
        result = result + outs[chips - 1].astype(F32)
    result = result.astype(BF)
    other = core_swap(jnp.concatenate([dk1, dv1], axis=2))
    mine = jnp.concatenate([dk0, dv0], axis=2).astype(F32) + other.astype(F32)
    sent = [by_columns(middle_low, packs), by_columns(after(dq, mine), packs)]
    got = exchange_packs(place, jnp.concatenate(sent, axis=2))
    got = jnp.concatenate(in_pack_order(place, got))
    part = width // packs
    parts = [matmul_tn(att_all, got[:, :part]), matmul_tn(normed_all, got[:, part:])]
    parts = jnp.concatenate(parts, axis=1).astype(BF)
    acts, ts = after((acts, ts), parts)
    pair = mine[0]
    for s in range(1, chips):
        pair = pair + chip_shift(mine[s].astype(BF), -s, cyclic=False).astype(F32)
    turned = []
    for j in range(KVH):
        one = pair[:, j * HD : (j + 1) * HD]
        swapped = jnp.concatenate([one[:, half:], one[:, :half]], axis=1)
        turned.append(one * cosine - swapped * sine)
    dkv = jnp.concatenate(turned + [pair[:, KVH * HD :]], axis=1).astype(BF)
    parts = reduce_line(place, parts.reshape(chips, 2, packs * depth, -1)).astype(BF)
    parts = after(parts, dkv, result)
    got = exchange_packs(place, parts.reshape(packs, depth, -1))
    got = in_pack_order(place, got)
    grad_out_w = jnp.concatenate([piece[:, :part] for piece in got], axis=1).astype(F32)
    grad_q = jnp.concatenate([piece[:, part:] for piece in got], axis=1).astype(F32)
    grad_down = sum(matmul_tn(act, top) for act, top in zip(acts, ts)).astype(BF)
    grad_down = lax.psum_scatter(grad_down, "pack", scatter_dimension=0, tiled=True).astype(F32)
    grad_gu = gu_here.reshape(blocks, 2, depth, ff).transpose(1, 2, 0, 3).reshape(2, depth, -1)
    grad_gate_w, grad_up_w = grad_gu[0].astype(F32), grad_gu[1].astype(F32)
    dkv = after(dkv, gu_here)
    dproj = jnp.concatenate([dq, dkv], axis=1)

    grad_normed = matmul_nt(dproj, qkv_full)
    _, first_pull = jax.vjp(rms_norm, stream, attn_gain)
    grad_input, grad_attn_gain = first_pull(grad_normed)
    input_grad = (grad_middle + grad_input).astype(BF)
    grad_bias = jnp.sum(dproj.astype(F32), axis=0)
    vector_grads = jnp.concatenate(
        [
            grad_bias.reshape(-1, bias_n),
            grad_attn_gain.reshape(-1, gain_n),
            grad_mlp_gain.reshape(-1, gain_n),
        ],
        axis=1,
    ).astype(BF)
    part = (qkv_cols - q_cols) // packs
    lines = -(-vector_grads.shape[1] // part)
    lines += -(blocks * lines) % 16 // blocks
    vector_grads = jnp.pad(vector_grads, ((0, 0), (0, lines * part - vector_grads.shape[1])))
    vector_grads = vector_grads.reshape(blocks, packs, lines, part).transpose(1, 0, 2, 3)
    vector_grads = vector_grads.reshape(packs, blocks * lines, part)
    got = exchange_packs(place, jnp.concatenate([by_columns(dkv, packs), vector_grads], axis=1))
    kv_all = jnp.concatenate(in_pack_order(place, [piece[:rows] for piece in got]))
    grad_kv = matmul_tn(normed_all, kv_all).astype(BF)
    vector_sum = sum(piece[rows:].astype(F32) for piece in got).astype(BF)
    grad_kv = jnp.concatenate(
        [grad_kv.reshape(blocks, packs * depth, part), vector_sum.reshape(blocks, lines, part)],
        axis=1,
    )
    grad_kv = reduce_line(place, grad_kv.reshape(chips, 2, -1, part))
    tail = grad_kv[packs * depth :].reshape(-1)
    grad_kv = to_shard(place, grad_kv[: packs * depth].astype(BF), depth)
    return (
        result[None],
        input_grad[None],
        jnp.concatenate([grad_q, grad_kv], axis=1),
        tail[:bias_n],
        grad_out_w,
        tail[bias_n : bias_n + gain_n],
        grad_gate_w,
        grad_up_w,
        grad_down,
        tail[bias_n + gain_n : bias_n + 2 * gain_n],
    )


def solution(mesh):
    tokens, rows, vector = P("pack", "blk", None), P(BOTH, None), P(BOTH)
    in_specs = (
        tokens, P("pack", None), tokens, rows, vector, rows, vector, rows, rows, rows, vector
    )
    out_specs = (tokens, tokens, rows, vector, rows, vector, rows, rows, rows, vector)
    return jax.shard_map(
        on_device, mesh=mesh, in_specs=in_specs, out_specs=out_specs, check_vma=False
    )
```

time: 968 us -> 723 us (0.75)
  waiting for transfers between devices: 488 us -> 314 us
  Pallas kernels: 31.4 us -> 130 us
  matrix products: 138 us -> 46.7 us
  blocking collectives: 67.8 us -> 0 us
  local copies, waits for them, and re-layouts: 66.6 us -> 52.9 us
    reduce_scatter x2 -> x1, waiting for transfers between devices: 122 us -> 0.02 us  [on_device(): grad_gu = lax.psum_scatter(grad_gu, 'pack', scatter_dimension=0, tiled=True)]
    pallas_call x0 -> x5, Pallas kernels: none -> 99.5 us  [the longest x2 64.2 us: feed(): pl.pallas_call(feed_kernel, grid=(count,), in_specs=[tokens] * 4 + [pl.Bl...]
    all_to_all x1 -> x0, blocking collectives: 67.8 us -> none  [on_device(): lax.all_to_all(gate_up.transpose(2, 0, 1, 3), 'blk', 0, 0, tiled=True)]
    dot_general x5 -> x2, matrix products: 58.2 us -> 4.48 us  [matmul_nt(): lax.dot_general(left, right, (((1,), (1,)), ((), ())), preferred_element_...]
    ppermute x0 -> x18, waiting for transfers between devices: none -> 53.2 us  [pack_swap(): return lax.ppermute(block, 'pack', [(i, i ^ k) for i in range(n)])]
    ppermute x18 -> x36, waiting for transfers between devices: 301 us -> 253 us  [chip_shift(): return lax.ppermute(block, 'blk', route)]
    all_to_all x1 -> x0, waiting for transfers between devices: 41.5 us -> none  [on_device(): grad_gu = lax.all_to_all(grad_gu, 'blk', 0, 0, tiled=True)]
    dot_general x4 -> x5, matrix products: 39.9 us -> 15.1 us  [matmul(): return jnp.dot(left, right, preferred_element_type=F32)]
  transfers between devices with their start and end apart: 33 -> 83, of which waited for: 19 -> 36; matrix products, arithmetic and copies ran while one was open for 22% -> 18% of each run, Pallas kernels for 3% -> 18%
where the time goes in v2:
time: 723 us; the launch traced here: 713 us
  waiting for transfers between devices  314 us (43%)
  Pallas kernels  130 us (18%)
  starting transfers between devices  91.9 us (13%)
  other arithmetic  60.9 us (8%)
  local copies, waits for them, and re-layouts  52.9 us (7%)
  matrix products  46.7 us (6%)
  between operations  16.3 us (2%)
    ppermute x36, waiting for transfers between devices, chip_shift(): return lax.ppermute(block, 'blk', route)  253 us
    ppermute x36, starting transfers between devices, chip_shift(): return lax.ppermute(block, 'blk', route)  66.9 us
    pallas_call x2, Pallas kernels, feed(): pl.pallas_call(feed_kernel, grid=(count,), in_specs=[tokens] * 4 + [pl.Bl...  64.2 us
    ppermute x18, waiting for transfers between devices, pack_swap(): return lax.ppermute(block, 'pack', [(i, i ^ k) for i in range(n)])  53.2 us
    dot_general x7, matrix products, matmul_tn(): lax.dot_general(left, right, (((0,), (0,)), ((), ())), preferred_element_...  27 us
    pallas_call x1, Pallas kernels, gate_up_grads(): pl.pallas_call(functools.partial(grads_kernel, packs, len(hs)), grid=(4,)...  22.8 us
    ppermute x18, starting transfers between devices, pack_swap(): return lax.ppermute(block, 'pack', [(i, i ^ k) for i in range(n)])  18.2 us
    unnamed x163, local copies, waits for them, and re-layouts  15.3 us
  transfers between devices with their start and end apart: 83, of which 36 were waited for; matrix products, arithmetic and copies ran while one was open for 18% of the time, Pallas kernels for 18%

profile of v2, /device:TPU:0, one launch (start us, length us, event | category | flops | bytes accessed | tf_op | source)
XLA Modules:
  0.0 713.1 jit_solution(5494146279343646302)
XLA Ops:
  26.4 10.3 %collective-permute-done.1 = bf16[56,2048]{1,0:T(8,128)(2,1)} collective-permute-done((bf16[56,2048]{1,0:T(8,128)(2,1)}, bf16[56,2048]{1,0:T(8,128)(2,1)}, u32[]{:S(2)}, u32[]{:S(2)}) %collective-permute-start.1) | collective-permute-done | bytes 229408 | tf_op jit(solution)/shard_map/ppermute | solution.py:24
  46.2 11.8 %collective-permute-done.13 = bf16[2,2,48,1120]{3,2,1,0:T(8,128)(2,1)S(1)} collective-permute-done((bf16[2,2,48,1120]{3,2,1,0:T(8,128)(2,1)S(1)}, bf16[2,2,48,1120]{3,2,1,0:T(8,128)(2,1)S(1)}, u32[]{:S(2)}, u32[]{:S(2)}) %collective-permute-start.13) | collective-permute-done | bytes 430112 | tf_op jit(solution)/shard_map/ppermute | solution.py:24
  62.4 17.6 %collective-permute-done.3.refs_2_ = bf16[4,56,2048]{2,1,0:T(8,128)(2,1)S(1)} collective-permute-done((bf16[4,56,2048]{2,1,0:T(8,128)(2,1)S(1)}, bf16[4,56,2048]{2,1,0:T(8,128)(2,1)S(1)}, u32[]{:S(2)}, u32[]{:S(2)}) %collective-permute-start.3) | collective-permute-done | bytes 917536 | tf_op jit(solution)/shard_map/ppermute | solution.py:34
  116.7 8.5 %shard_map.187.q_ref = bf16[256,2048]{1,0:T(8,128)(2,1)} custom-call(bf16[256,1536]{1,0:T(8,128)(2,1)} %fusion.3.xn_ref, bf16[1536,2048]{1,0:T(8,128)(2,1)} %shard_map.186.w_ref, f32[1,2048]{1,0:T(1,128)} %slice.261.bias_ref, f32[256,128]{1,0:T(8,128)} %get-tuple-element.270.cos_ref, f32[256,128]{1,0:T(8,128)} %get-tuple-element.271.sin_ref), custom_call_target="tpu_custom_call" | custom-call | flops 1610612736 | bytes 6291456 | tf_op jit(solution)/shard_map/pallas_call | solution.py:164
  137.3 21.7 %collective-permute-done.18 = bf16[48,1536]{1,0:T(8,128)(2,1)S(1)} collective-permute-done((bf16[48,1536]{1,0:T(8,128)(2,1)S(1)}, bf16[48,1536]{1,0:T(8,128)(2,1)S(1)}, u32[]{:S(2)}, u32[]{:S(2)}) %collective-permute-start.18) | collective-permute-done | bytes 147488 | tf_op jit(solution)/shard_map/ppermute | solution.py:24
  177.0 14.6 %collective-permute-done.22.refs_6_ = bf16[4,48,1536]{2,1,0:T(8,128)(2,1)S(1)} collective-permute-done((bf16[4,48,1536]{2,1,0:T(8,128)(2,1)S(1)}, bf16[4,48,1536]{2,1,0:T(8,128)(2,1)S(1)}, u32[]{:S(2)}, u32[]{:S(2)}) %collective-permute-start.22) | collective-permute-done | bytes 589856 | tf_op jit(solution)/shard_map/ppermute | solution.py:34
  195.4 8.8 %shard_map.188 = (f32[256,1536]{1,0:T(8,128)}, bf16[256,1536]{1,0:T(8,128)(2,1)}, f32[2,1,1536]{2,1,0:T(1,128)}) custom-call(s32[17]{0:T(128)} %pad_add_fusion.1.meta_ref, bf16[256,2048]{1,0:T(8,128)(2,1)} %shard_map.187.q_ref, s32[1,256]{1,0:T(1,128)} %bitcast.431, bf16[4,256,512]{2,1,0:T(8,128)(2,1)} %copy-done.41, bf16[4,256,512]{2,1,0:T(8,128)(2,1)} %copy-done.41, ...), custom_call_target="tpu_custom_call" | custom-call | flops 12884901888 | bytes 2097152 | tf_op jit(solution)/shard_map/pallas_call | solution.py:266
  237.1 17.1 %collective-permute-done.32 = bf16[256,1536]{1,0:T(8,128)(2,1)S(1)} collective-permute-done((bf16[256,1536]{1,0:T(8,128)(2,1)S(1)}, bf16[256,1536]{1,0:T(8,128)(2,1)S(1)}, u32[]{:S(2)}, u32[]{:S(2)}) %collective-permute-start.32) | collective-permute-done | bytes 786464 | tf_op jit(solution)/shard_map/ppermute | solution.py:24
  254.3 16.7 %collective-permute-done.35 = bf16[256,1536]{1,0:T(8,128)(2,1)S(1)} collective-permute-done((bf16[256,1536]{1,0:T(8,128)(2,1)S(1)}, bf16[256,1536]{1,0:T(8,128)(2,1)S(1)}, u32[]{:S(2)}, u32[]{:S(2)}) %collective-permute-start.35) | collective-permute-done | bytes 786464 | tf_op jit(solution)/shard_map/ppermute | solution.py:24
  272.3 15.5 %collective-permute-done.30 = bf16[256,1536]{1,0:T(8,128)(2,1)S(1)} collective-permute-done((bf16[256,1536]{1,0:T(8,128)(2,1)S(1)}, bf16[256,1536]{1,0:T(8,128)(2,1)S(1)}, u32[]{:S(2)}, u32[]{:S(2)}) %collective-permute-start.30) | collective-permute-done | bytes 786464 | tf_op jit(solution)/shard_map/ppermute | solution.py:24
  287.8 16.7 %collective-permute-done.33 = bf16[256,1536]{1,0:T(8,128)(2,1)S(1)} collective-permute-done((bf16[256,1536]{1,0:T(8,128)(2,1)S(1)}, bf16[256,1536]{1,0:T(8,128)(2,1)S(1)}, u32[]{:S(2)}, u32[]{:S(2)}) %collective-permute-start.33) | collective-permute-done | bytes 786464 | tf_op jit(solution)/shard_map/ppermute | solution.py:24
  313.6 32.1 %shard_map.190 = (bf16[2,256,1120]{2,1,0:T(8,128)(2,1)}, bf16[2,256,1120]{2,1,0:T(8,128)(2,1)}, bf16[2,256,1120]{2,1,0:T(8,128)(2,1)}, bf16[2,256,1120]{2,1,0:T(...) custom-call(bf16[2,256,1536]{2,1,0:T(8,128)(2,1)} %pad_maximum_fusio, ...), custom_call_target="tpu_custom_call" | custom-call | flops 22020096000 | bytes 10321920 | tf_op jit(solution)/shard_map/pallas_call | solution.py:479
  346.3 32.0 %shard_map.191 = (bf16[2,256,1120]{2,1,0:T(8,128)(2,1)}, bf16[2,256,1120]{2,1,0:T(8,128)(2,1)}, bf16[2,256,1120]{2,1,0:T(8,128)(2,1)}, bf16[2,256,1120]{2,1,0:T(...) custom-call(bf16[2,256,1536]{2,1,0:T(8,128)(2,1)} %pad_maximum_fusio, ...), custom_call_target="tpu_custom_call" | custom-call | flops 22020096000 | bytes 10321920 | tf_op jit(solution)/shard_map/pallas_call | solution.py:479
  395.9 10.2 %collective-permute-done.40 = bf16[256,1536]{1,0:T(8,128)(2,1)S(1)} collective-permute-done((bf16[256,1536]{1,0:T(8,128)(2,1)S(1)}, bf16[256,1536]{1,0:T(8,128)(2,1)S(1)}, u32[]{:S(2)}, u32[]{:S(2)}) %collective-permute-start.40) | collective-permute-done | bytes 786464 | tf_op jit(solution)/shard_map/ppermute | solution.py:24
  407.1 22.8 %shard_map.192 = bf16[4,8,2,48,1120]{4,3,2,1,0:T(8,128)(2,1)} custom-call(bf16[512,1536]{1,0:T(8,128)(2,1)} %bitcast.61.refs_0_, bf16[512,1536]{1,0:T(8,128)(2,1)} %bitcast.62.refs_1_, bf16[512,1536]{1,0:T(8,128)(2,1)} %bitcast.63.refs_2_, bf16[512,1536]{1,0:T(8,128)(2,1)} %bitcast.64.refs_3_, bf16[512,1120]{1,0:T(8,128)(2,1)} %bitcast.439, ...), custom_call_target="tpu_custom_call" | custom-call | flops 24662507520 | bytes 13762560 | tf_op jit(solution)/shard_map/pallas_call | solution.py:525
  443.5 10.5 %collective-permute-done.42 = bf16[256,1536]{1,0:T(8,128)(2,1)S(1)} collective-permute-done((bf16[256,1536]{1,0:T(8,128)(2,1)S(1)}, bf16[256,1536]{1,0:T(8,128)(2,1)S(1)}, u32[]{:S(2)}, u32[]{:S(2)}) %collective-permute-start.42) | collective-permute-done | bytes 786464 | tf_op jit(solution)/shard_map/ppermute | solution.py:24
  453.9 14.3 %collective-permute-done.41 = bf16[256,1536]{1,0:T(8,128)(2,1)S(1)} collective-permute-done((bf16[256,1536]{1,0:T(8,128)(2,1)}, bf16[256,1536]{1,0:T(8,128)(2,1)S(1)}, u32[]{:S(2)}, u32[]{:S(2)}) %collective-permute-start.41) | collective-permute-done | bytes 786464 | tf_op jit(solution)/shard_map/ppermute | solution.py:24
  485.3 13.3 %shard_map.193 = (bf16[256,1536]{1,0:T(8,128)(2,1)}, bf16[4,256,256]{2,1,0:T(8,128)(2,1)}, bf16[4,256,256]{2,1,0:T(8,128)(2,1)}, bf16[4,256,256]{2,1,0:T(8,128)(2,1)}, bf16[4,256,256]{2,1,0:T(8,128)(2,1)}) custom-call(s32[17]{0:T(128)} %pad_add_fusion.1.meta_ref, bf16[256,2048]{1,0:T(8,128)(2,1)} %shard_map.187.q_ref, ...), custom_call_target="tpu_custom_call" | custom-call | flops 80530636800 | bytes 2097152 | tf_op jit(solution)/shard_map/pallas_call | solution.py:364
  507.0 12.7 %collective-permute-done.46 = bf16[256,1536]{1,0:T(8,128)(2,1)} collective-permute-done((bf16[256,1536]{1,0:T(8,128)(2,1)}, bf16[256,1536]{1,0:T(8,128)(2,1)}, u32[]{:S(2)}, u32[]{:S(2)}) %collective-permute-start.46) | collective-permute-done | bytes 786464 | tf_op jit(solution)/shard_map/ppermute | solution.py:24
  536.5 21.3 %collective-permute-done.51 = bf16[256,512]{1,0:T(8,128)(2,1)S(1)} collective-permute-done((bf16[256,512]{1,0:T(8,128)(2,1)S(1)}, bf16[256,512]{1,0:T(8,128)(2,1)S(1)}, u32[]{:S(2)}, u32[]{:S(2)}) %collective-permute-start.51) | collective-permute-done | bytes 262176 | tf_op jit(solution)/shard_map/ppermute | solution.py:24
  557.9 12.0 %collective-permute-done.50 = bf16[256,512]{1,0:T(8,128)(2,1)S(1)} collective-permute-done((bf16[256,512]{1,0:T(8,128)(2,1)S(1)}, bf16[256,512]{1,0:T(8,128)(2,1)S(1)}, u32[]{:S(2)}, u32[]{:S(2)}) %collective-permute-start.50) | collective-permute-done | bytes 262176 | tf_op jit(solution)/shard_map/ppermute | solution.py:24
  597.9 18.0 %collective-permute-done.53 = bf16[2,2,48,1120]{3,2,1,0:T(8,128)(2,1)S(1)} collective-permute-done((bf16[2,2,48,1120]{3,2,1,0:T(8,128)(2,1)S(1)}, bf16[2,2,48,1120]{3,2,1,0:T(8,128)(2,1)S(1)}, u32[]{:S(2)}, u32[]{:S(2)}) %collective-permute-start.53) | collective-permute-done | bytes 430112 | tf_op jit(solution)/shard_map/ppermute | solution.py:24
  620.8 9.5 %collective-permute-start.62 = (bf16[192,768]{1,0:T(8,128)(2,1)}, bf16[192,768]{1,0:T(8,128)(2,1)}, u32[]{:S(2)}, u32[]{:S(2)}) collective-permute-start(bf16[192,768]{1,0:T(8,128)(2,1)} %get-tuple-element.201), channel_id=1, source_target_pairs={{0,24},{4,28},{8,0},{12,4},{16,8},{20,12},{24,16},{28,20},{1,25},{... | collective-permute-start | bytes 884744 | tf_op jit(solution)/shard_map/ppermute | solution.py:24
  638.7 20.1 %collective-permute-done.61 = bf16[192,768]{1,0:T(8,128)(2,1)} collective-permute-done((bf16[192,768]{1,0:T(8,128)(2,1)}, bf16[192,768]{1,0:T(8,128)(2,1)}, u32[]{:S(2)}, u32[]{:S(2)}) %collective-permute-start.61) | collective-permute-done | bytes 294944 | tf_op jit(solution)/shard_map/ppermute | solution.py:24
  (493 shorter events, 308.5 us)
Async XLA Ops:
  7.2 199.7 %all-gather.8.cloned.1.call-start = ((), (), s32[]{:S(2)}) async-start(), calls=%async_computation.3 | async-start | bytes 4423680 | tf_op jit(solution)/shard_map/all_gather | solution.py:589
  40.7 39.3 %collective-permute-start.3 = (bf16[4,56,2048]{2,1,0:T(8,128)(2,1)S(1)}, bf16[4,56,2048]{2,1,0:T(8,128)(2,1)S(1)}, u32[]{:S(2)}, u32[]{:S(2)}) collective-permute-start(bf16[4,56,2048]{2,1,0:T(8,128)(2,1)S(1)} %pad_maximum_fusion.9.refs_0_), channel_id=1, source_target_pairs={{0,1},{1,0},{2,3},{3,2},{4,5},{5,4},{6,7},{7,6},{8,9},{9,8},{10,11... | collective-permute-start | bytes 2752520 | tf_op jit(solution)/shard_map/ppermute | solution.py:34
  41.1 39.0 %collective-permute-start.6 = (bf16[4,56,2048]{2,1,0:T(8,128)(2,1)S(1)}, bf16[4,56,2048]{2,1,0:T(8,128)(2,1)S(1)}, u32[]{:S(2)}, u32[]{:S(2)}) collective-permute-start(bf16[4,56,2048]{2,1,0:T(8,128)(2,1)S(1)} %pad_maximum_fusion.9.refs_0_), channel_id=1, source_target_pairs={{0,2},{1,3},{2,0},{3,1},{4,6},{5,7},{6,4},{7,5},{8,10},{9,11},{10,... | collective-permute-start | bytes 2752520 | tf_op jit(solution)/shard_map/ppermute | solution.py:34
  43.9 36.8 %collective-permute-start.14 = (bf16[2,2,48,1120]{3,2,1,0:T(8,128)(2,1)S(1)}, bf16[2,2,48,1120]{3,2,1,0:T(8,128)(2,1)S(1)}, u32[]{:S(2)}, u32[]{:S(2)}) collective-permute-start(bf16[2,2,48,1120]{3,2,1,0:T(8,128)(2,1)S(1)} %bitcast.414), channel_id=1, source_target_pairs={{0,16},{4,20},{8,24},{12,28},{16,0},{20,4},{24,8},{28,12},{1,17},{... | collective-permute-start | bytes 1290248 | tf_op jit(solution)/shard_map/ppermute | solution.py:24
  94.5 116.6 %all-gather.10.cloned.1.call-start = ((), (), s32[]{:S(2)}) async-start(), calls=%async_computation.4 | async-start | bytes 4300800 | tf_op jit(solution)/shard_map/all_gather | solution.py:585
  96.1 212.8 %all-gather.6.cloned.1.call-start = ((), (), s32[]{:S(2)}) async-start(), calls=%async_computation.2 | async-start | bytes 4423680 | tf_op jit(solution)/shard_map/all_gather | solution.py:589
  107.4 322.6 %all-gather.12.cloned.1.call-start = ((), (), s32[]{:S(2)}) async-start(), calls=%async_computation.5 | async-start | bytes 3932160 | tf_op jit(solution)/shard_map/all_gather | solution.py:620
  136.7 55.0 %collective-permute-start.23 = (bf16[256,1536]{1,0:T(8,128)(2,1)S(1)}, bf16[256,1536]{1,0:T(8,128)(2,1)S(1)}, u32[]{:S(2)}, u32[]{:S(2)}) collective-permute-start(bf16[256,1536]{1,0:T(8,128)(2,1)S(1)} %bitcast.378), channel_id=1, source_target_pairs={{0,8},{4,12},{8,16},{12,20},{16,24},{20,28},{24,0},{28,4},{1,9},{5... | collective-permute-start | bytes 2359304 | tf_op jit(solution)/shard_map/ppermute | solution.py:24
  211.1 218.9 %all-gather.14.cloned.1.call-start = ((), (), s32[]{:S(2)}) async-start(), calls=%async_computation.6 | async-start | bytes 3932160 | tf_op jit(solution)/shard_map/all_gather | solution.py:621
  226.5 44.5 %collective-permute-start.35 = (bf16[256,1536]{1,0:T(8,128)(2,1)S(1)}, bf16[256,1536]{1,0:T(8,128)(2,1)S(1)}, u32[]{:S(2)}, u32[]{:S(2)}) collective-permute-start(bf16[256,1536]{1,0:T(8,128)(2,1)S(1)} %copy-done.44), channel_id=1, source_target_pairs={{0,8},{4,12},{8,16},{12,20},{16,24},{20,28},{24,0},{28,4},{1,9},{5... | collective-permute-start | bytes 2359304 | tf_op jit(solution)/shard_map/ppermute | solution.py:24
  231.5 56.3 %collective-permute-start.30 = (bf16[256,1536]{1,0:T(8,128)(2,1)S(1)}, bf16[256,1536]{1,0:T(8,128)(2,1)S(1)}, u32[]{:S(2)}, u32[]{:S(2)}) collective-permute-start(bf16[256,1536]{1,0:T(8,128)(2,1)S(1)} %multiply_convert_fusion), channel_id=1, source_target_pairs={{0,24},{4,28},{8,0},{12,4},{16,8},{20,12},{24,16},{28,20},{1,25},{... | collective-permute-start | bytes 2359304 | tf_op jit(solution)/shard_map/ppermute | solution.py:24
  254.3 50.2 %collective-permute-start.33 = (bf16[256,1536]{1,0:T(8,128)(2,1)S(1)}, bf16[256,1536]{1,0:T(8,128)(2,1)S(1)}, u32[]{:S(2)}, u32[]{:S(2)}) collective-permute-start(bf16[256,1536]{1,0:T(8,128)(2,1)S(1)} %collective-permute-done.32), channel_id=1, source_target_pairs={{0,8},{4,12},{8,16},{12,20},{16,24},{20,28},{24,0},{28,4},{1,9},{5... | collective-permute-start | bytes 2359304 | tf_op jit(solution)/shard_map/ppermute | solution.py:24
  272.3 41.3 %collective-permute-start.36 = (bf16[2,256,1536]{2,1,0:T(8,128)(2,1)}, bf16[2,256,1536]{2,1,0:T(8,128)(2,1)}, u32[]{:S(2)}, u32[]{:S(2)}) collective-permute-start(bf16[2,256,1536]{2,1,0:T(8,128)(2,1)} %pad_maximum_fusion.4.t0_ref), channel_id=1, source_target_pairs={{0,4},{4,0},{8,12},{12,8},{16,20},{20,16},{24,28},{28,24},{1,5},{5... | collective-permute-start | bytes 4718600 | tf_op jit(solution)/shard_map/ppermute | solution.py:29
  307.1 39.2 %collective-permute-start.37 = (bf16[2,256,1536]{2,1,0:T(8,128)(2,1)}, bf16[2,256,1536]{2,1,0:T(8,128)(2,1)}, u32[]{:S(2)}, u32[]{:S(2)}) collective-permute-start(bf16[2,256,1536]{2,1,0:T(8,128)(2,1)} %pad_maximum_fusion.5.t0_ref), channel_id=1, source_target_pairs={{0,4},{4,0},{8,12},{12,8},{16,20},{20,16},{24,28},{28,24},{1,5},{5... | collective-permute-start | bytes 4718600 | tf_op jit(solution)/shard_map/ppermute | solution.py:29
  308.8 37.4 %collective-permute-start.31 = (bf16[2,256,1536]{2,1,0:T(8,128)(2,1)}, bf16[2,256,1536]{2,1,0:T(8,128)(2,1)}, u32[]{:S(2)}, u32[]{:S(2)}) collective-permute-start(bf16[2,256,1536]{2,1,0:T(8,128)(2,1)} %pad_maximum_fusion.2.h0_ref), channel_id=1, source_target_pairs={{0,4},{4,0},{8,12},{12,8},{16,20},{20,16},{24,28},{28,24},{1,5},{5... | collective-permute-start | bytes 4718600 | tf_op jit(solution)/shard_map/ppermute | solution.py:29
  313.1 271.8 %reduce-scatter.5.cloned.1.call-start = ((), (), s32[]{:S(2)}) async-start(), calls=%async_computation.7 | async-start | bytes 8847360 | tf_op jit(solution)/shard_map/reduce_scatter | solution.py:675
  345.7 39.8 %collective-permute-start.39 = (bf16[2,256,1536]{2,1,0:T(8,128)(2,1)}, bf16[2,256,1536]{2,1,0:T(8,128)(2,1)S(1)}, u32[]{:S(2)}, u32[]{:S(2)}) collective-permute-start(bf16[2,256,1536]{2,1,0:T(8,128)(2,1)} %get-tuple-element.106), channel_id=1, source_target_pairs={{0,4},{4,0},{8,12},{12,8},{16,20},{20,16},{24,28},{28,24},{1,5},{5... | collective-permute-start | bytes 4718600 | tf_op jit(solution)/shard_map/ppermute | solution.py:29
  430.0 202.5 %reduce-scatter.7.cloned.1.call-start = ((), (), s32[]{:S(2)}) async-start(), calls=%async_computation.8 | async-start | bytes 4300800
  431.6 36.6 %collective-permute-start.41 = (bf16[256,1536]{1,0:T(8,128)(2,1)}, bf16[256,1536]{1,0:T(8,128)(2,1)S(1)}, u32[]{:S(2)}, u32[]{:S(2)}) collective-permute-start(bf16[256,1536]{1,0:T(8,128)(2,1)} %fusion.10), channel_id=1, source_target_pairs={{0,24},{4,28},{8,0},{12,4},{16,8},{20,12},{24,16},{28,20},{1,25},{... | collective-permute-start | bytes 2359304 | tf_op jit(solution)/shard_map/ppermute | solution.py:24
  440.6 37.3 %collective-permute-start.43 = (bf16[512,1536]{1,0:T(8,128)(2,1)S(1)}, bf16[512,1536]{1,0:T(8,128)(2,1)S(1)}, u32[]{:S(2)}, u32[]{:S(2)}) collective-permute-start(bf16[512,1536]{1,0:T(8,128)(2,1)S(1)} %convolution_convert_fusion.1), channel_id=1, source_target_pairs={{0,4},{4,0},{8,12},{12,8},{16,20},{20,16},{24,28},{28,24},{1,5},{5... | collective-permute-start | bytes 4718600 | tf_op jit(solution)/shard_map/ppermute | solution.py:29
  528.3 138.4 %collective-permute-start.47 = (bf16[256,1536]{1,0:T(8,128)(2,1)}, bf16[256,1536]{1,0:T(8,128)(2,1)}, u32[]{:S(2)}, u32[]{:S(2)}) collective-permute-start(bf16[256,1536]{1,0:T(8,128)(2,1)} %convert_add_fusion.7), channel_id=1, source_target_pairs={{0,24},{4,28},{8,0},{12,4},{16,8},{20,12},{24,16},{28,20},{1,25},{... | collective-permute-start | bytes 2359304 | tf_op jit(solution)/shard_map/ppermute | solution.py:24
  533.3 36.5 %collective-permute-start.50 = (bf16[256,512]{1,0:T(8,128)(2,1)S(1)}, bf16[256,512]{1,0:T(8,128)(2,1)S(1)}, u32[]{:S(2)}, u32[]{:S(2)}) collective-permute-start(bf16[256,512]{1,0:T(8,128)(2,1)S(1)} %get-tuple-element.205), channel_id=1, source_target_pairs={{16,0},{20,4},{24,8},{28,12},{17,1},{21,5},{25,9},{29,13},{18,2},{... | collective-permute-start | bytes 786440 | tf_op jit(solution)/shard_map/ppermute | solution.py:24
  536.3 35.6 %collective-permute-start.56 = (bf16[256,768]{1,0:T(8,128)(2,1)S(1)}, bf16[256,768]{1,0:T(8,128)(2,1)S(1)}, u32[]{:S(2)}, u32[]{:S(2)}) collective-permute-start(bf16[256,768]{1,0:T(8,128)(2,1)S(1)} %get-tuple-element.195), channel_id=1, source_target_pairs={{0,3},{1,2},{2,1},{3,0},{4,7},{5,6},{6,5},{7,4},{8,11},{9,10},{10,... | collective-permute-start | bytes 1179656 | tf_op jit(solution)/shard_map/ppermute | solution.py:34
  618.1 42.2 %collective-permute-start.55 = (bf16[4,2,48,1120]{3,2,1,0:T(8,128)(2,1)}, bf16[4,2,48,1120]{3,2,1,0:T(8,128)(2,1)}, u32[]{:S(2)}, u32[]{:S(2)}) collective-permute-start(bf16[4,2,48,1120]{3,2,1,0:T(8,128)(2,1)} %dynamic-slice_bitcast_fusion), channel_id=1, source_target_pairs={{0,4},{4,0},{8,12},{12,8},{16,20},{20,16},{24,28},{28,24},{1,5},{5... | collective-permute-start | bytes 2580488 | tf_op jit(solution)/shard_map/ppermute | solution.py:29
  (141 other events, 2191.9 us)
Sparse Core Ops, SparseCore 0:
  94.6 47.1 all-gather.7
  143.6 65.2 all-gather.9
  210.7 45.8 all-gather.5
  258.9 43.9 all-gather.11
  313.2 41.6 all-gather.13
  430.1 75.6 reduce-scatter.4
  526.2 63.3 reduce-scatter.6

commit v3 on v2

--- a/solution.py
+++ b/solution.py
@@ -77,9 +77,9 @@
     return got
 
 
-def reduce_line(place, parts):
+def reduce_line(place, parts, before=()):
     other = core_swap(take(parts, 1, 1 - place.core))
-    mine = take(parts, 1, place.core).astype(F32) + other.astype(F32)
+    mine = after(take(parts, 1, place.core).astype(F32) + other.astype(F32), before)
     line = mine.astype(BF)
     total = take(mine, 0, place.chip)
     for s in range(1, place.chips):
@@ -106,12 +106,15 @@
     return jnp.concatenate(in_pack_order(place, pieces), axis=1).astype(F32)
 
 
-def exchange_line(place, parts, beside=()):
+def exchange_chips(place, parts):
     got = jnp.zeros(parts.shape, parts.dtype)
     got = put(got, take(parts, 0, place.chip), place.chip)
     for s in range(1, place.chips):
         got = put(got, chip_shift(take(parts, 0, place.chip_at(s)), s), place.chip_at(-s))
-    got = after(got, beside)
+    return got
+
+
+def exchange_cores(place, got):
     other = core_swap(take(got, 1, 1 - place.core))
     return in_core_order(place, take(got, 1, place.core), other)
 
@@ -387,7 +390,7 @@
         + [jax.ShapeDtypeStruct((chips, rows, KVH * HD), BF)] * 4,
         compiler_params=pltpu.CompilerParams(vmem_limit_bytes=VMEM_LIMIT),
         cost_estimate=pl.CostEstimate(
-            flops=100 * rows * rows * count * H * HD,
+            flops=400 * rows * rows * count * H * HD,
             bytes_accessed=count * rows * 1024,
             transcendentals=rows * rows * count * H,
         ),
@@ -494,7 +497,7 @@
         scratch_shapes=[pltpu.VMEM((2 * rows, width), BF)] * 2,
         compiler_params=pltpu.CompilerParams(vmem_limit_bytes=VMEM_LIMIT),
         cost_estimate=pl.CostEstimate(
-            flops=25 * count * rows * width * ff,
+            flops=75 * count * rows * width * ff,
             bytes_accessed=6 * width * ff,
             transcendentals=2 * count * rows * ff,
         ),
@@ -535,6 +538,30 @@
     )(*hs, *dgates, *dups)
 
 
+def down_grads_kernel(n, *refs):
+    *refs, out_ref = refs
+    out_ref[...] = sum(matmul_tn(refs[j][...], refs[n + j][...]) for j in range(n)).astype(BF)
+
+
+def down_grads(acts, tops):
+    ff, width = acts[0].shape[1], tops[0].shape[1]
+    tile = width // 4
+    rows = sum(act.shape[0] for act in acts)
+    once = pl.Buffered(1)
+    return pl.pallas_call(
+        functools.partial(down_grads_kernel, len(acts)),
+        grid=(4,),
+        in_specs=[pl.BlockSpec(act.shape, lambda j: (0, 0), pipeline_mode=once) for act in acts]
+        + [pl.BlockSpec((top.shape[0], tile), lambda j: (0, j)) for top in tops],
+        out_specs=pl.BlockSpec((ff, tile), lambda j: (0, j)),
+        out_shape=jax.ShapeDtypeStruct((ff, width), BF),
+        compiler_params=pltpu.CompilerParams(vmem_limit_bytes=VMEM_LIMIT),
+        cost_estimate=pl.CostEstimate(
+            flops=2 * rows * width * ff, bytes_accessed=4 * rows * width, transcendentals=0
+        ),
+    )(*acts, *tops)
+
+
 def on_device(
     tokens, lengths, out_grad, w_qkv, b_qkv, w_out, gain_attn, w_gate, w_up, w_down, gain_mlp
 ):
@@ -575,8 +602,9 @@
     gate_up = after(gate_up.transpose(2, 3, 0, 1, 4), line)
     lines = [line] + [pack_swap(line, k) for k in range(1, packs)]
     lines = [piece for line in lines for piece in (line, core_swap(after(line, lines[1])))]
-    gate_up = exchange_line(place, gate_up, lines).reshape(blocks, 2, depth, ff)
-    vectors = sum(jnp.sum(piece[:, depth:].astype(F32), axis=0) for piece in lines)
+    gate_up = exchange_cores(place, after(exchange_chips(place, gate_up), lines))
+    gate_up = gate_up.reshape(blocks, 2, depth, ff)
+    vectors = jnp.sum(sum(piece[:, depth:].astype(F32) for piece in lines), axis=0)
     bias = vectors[:1]
     attn_gain, mlp_gain = vectors[1, :width], vectors[2, :width]
     out_line = gather_line(after(w_out.astype(BF), gate_up))
@@ -601,7 +629,7 @@
     t = {0: grad_top, 1: chip_shift(top, 1)}
     if chips > 2:
         t[chips - 1] = chip_shift(top, -1)
-    kv_other = core_swap(after(kv_line, out_lines, t[1]))
+    kv_other = core_swap(after(kv_line, out_lines))
     back = jnp.arange(chips, dtype=jnp.int32)
     source = jnp.concatenate([(chip - back) * 2 + core, (chip - back) * 2 + 1 - core])
     valid = ((source >= 0) & (source <= blk)).astype(jnp.int32)
@@ -612,7 +640,9 @@
     out_lines = after(out_lines, att_low)
     out_lines = [piece for line in out_lines for piece in (line, core_swap(line))]
     out_full = assemble(place, out_lines, depth)
-    att_low = after(att_low, t[chips - 1])
+    for s in range(2, chips - 1):
+        t[s] = chip_shift(t[s - 1], 1)
+    att_low = after(att_low, t)
     middle = stream + matmul(att_low, out_full)
 
     hidden = rms_norm(middle, mlp_gain).astype(BF)
@@ -640,7 +670,7 @@
     if chips > 2:
         h[chips - 1] = chip_shift(hidden, -1)
     for s in range(2, chips - 1):
-        h[s], t[s] = chip_shift(h[s - 1], 1), chip_shift(t[s - 1], 1)
+        h[s] = chip_shift(h[s - 1], 1)
     h[0], h[chips - 1] = after((h[0], h[chips - 1]), h[chips - 1])
     h[1] = after(h[1], h[chips - 1])
     first, second = (list(range(chips - 2, 0, -1)), [chips - 1, 0]) if chips > 2 else ([1, 0], [])
@@ -650,7 +680,7 @@
             continue
         h_pair, t_pair = both([h[s] for s in part]), both([t[s] for s in part])
         if partials:
-            h_pair = after(h_pair, other)
+            h_pair = after(h_pair, mine)
         *kept, mine, other = feed(h_pair, t_pair, gate_w, up_w, down)
         mine = mine + core_swap(other).astype(F32)
         partials.update({s: mine[i] for i, s in enumerate(part)})
@@ -673,7 +703,6 @@
 
     grad_gu = after(grad_gu, normed_all, att_all).reshape(packs * blocks * 2 * depth, ff)
     grad_gu = lax.psum_scatter(grad_gu, "pack", scatter_dimension=0, tiled=True)
-    gu_here = exchange_line(place, grad_gu.reshape(chips, 2, 2, depth, ff))
 
     _, second_pull = jax.vjp(rms_norm, middle, mlp_gain)
     grad_mid, grad_mlp_gain = second_pull(grad_hidden)
@@ -696,13 +725,14 @@
     result = result.astype(BF)
     other = core_swap(jnp.concatenate([dk1, dv1], axis=2))
     mine = jnp.concatenate([dk0, dv0], axis=2).astype(F32) + other.astype(F32)
-    sent = [by_columns(middle_low, packs), by_columns(after(dq, mine), packs)]
+    acts, ts = after((acts, ts), mine)
+    grad_down = down_grads(acts, ts)
+    sent = [by_columns(middle_low, packs), by_columns(after(dq, grad_down), packs)]
     got = exchange_packs(place, jnp.concatenate(sent, axis=2))
     got = jnp.concatenate(in_pack_order(place, got))
     part = width // packs
     parts = [matmul_tn(att_all, got[:, :part]), matmul_tn(normed_all, got[:, part:])]
     parts = jnp.concatenate(parts, axis=1).astype(BF)
-    acts, ts = after((acts, ts), parts)
     pair = mine[0]
     for s in range(1, chips):
         pair = pair + chip_shift(mine[s].astype(BF), -s, cyclic=False).astype(F32)
@@ -712,17 +742,17 @@
         swapped = jnp.concatenate([one[:, half:], one[:, :half]], axis=1)
         turned.append(one * cosine - swapped * sine)
     dkv = jnp.concatenate(turned + [pair[:, KVH * HD :]], axis=1).astype(BF)
-    parts = reduce_line(place, parts.reshape(chips, 2, packs * depth, -1)).astype(BF)
+    gu_here = exchange_chips(place, grad_gu.reshape(chips, 2, 2, depth, ff))
+    parts = reduce_line(place, parts.reshape(chips, 2, packs * depth, -1), gu_here).astype(BF)
+    gu_here = exchange_cores(place, gu_here)
     parts = after(parts, dkv, result)
     got = exchange_packs(place, parts.reshape(packs, depth, -1))
     got = in_pack_order(place, got)
     grad_out_w = jnp.concatenate([piece[:, :part] for piece in got], axis=1).astype(F32)
     grad_q = jnp.concatenate([piece[:, part:] for piece in got], axis=1).astype(F32)
-    grad_down = sum(matmul_tn(act, top) for act, top in zip(acts, ts)).astype(BF)
     grad_down = lax.psum_scatter(grad_down, "pack", scatter_dimension=0, tiled=True).astype(F32)
     grad_gu = gu_here.reshape(blocks, 2, depth, ff).transpose(1, 2, 0, 3).reshape(2, depth, -1)
     grad_gate_w, grad_up_w = grad_gu[0].astype(F32), grad_gu[1].astype(F32)
-    dkv = after(dkv, gu_here)
     dproj = jnp.concatenate([dq, dkv], axis=1)
 
     grad_normed = matmul_nt(dproj, qkv_full)

time: 723 us -> 673 us (0.931)
  waiting for transfers between devices: 314 us -> 269 us
  matrix products: 46.7 us -> 30.2 us
  Pallas kernels: 130 us -> 145 us
    ppermute x36, waiting for transfers between devices: 253 us -> 207 us  [chip_shift(): return lax.ppermute(block, 'blk', route)]
    dot_general x7 -> x3, matrix products: 27 us -> 7.15 us  [matmul_tn(): lax.dot_general(left, right, (((0,), (0,)), ((), ())), preferred_element_...]
    pallas_call x0 -> x1, Pallas kernels: none -> 14.6 us  [down_grads(): pl.pallas_call(functools.partial(down_grads_kernel, len(acts)), grid=(4,)...]
    unnamed x163 -> x150, local copies, waits for them, and re-layouts: 15.3 us -> 10.7 us
  transfers between devices with their start and end apart: 83 -> 83, of which waited for: 36 -> 36; matrix products, arithmetic and copies ran while one was open for 18% -> 16% of each run, Pallas kernels for 18% -> 22%
where the time goes in v3:
time: 673 us; the launch traced here: 663 us
  waiting for transfers between devices  269 us (40%)
  Pallas kernels  145 us (22%)
  starting transfers between devices  97.9 us (15%)
  other arithmetic  56.7 us (8%)
  local copies, waits for them, and re-layouts  48.5 us (7%)
  matrix products  30.2 us (4%)
  between operations  16 us (2%)
    ppermute x36, waiting for transfers between devices, chip_shift(): return lax.ppermute(block, 'blk', route)  207 us
    ppermute x36, starting transfers between devices, chip_shift(): return lax.ppermute(block, 'blk', route)  70.3 us
    pallas_call x2, Pallas kernels, feed(): pl.pallas_call(feed_kernel, grid=(count,), in_specs=[tokens] * 4 + [pl.Bl...  64.4 us
    ppermute x18, waiting for transfers between devices, pack_swap(): return lax.ppermute(block, 'pack', [(i, i ^ k) for i in range(n)])  52.3 us
    pallas_call x1, Pallas kernels, gate_up_grads(): pl.pallas_call(functools.partial(grads_kernel, packs, len(hs)), grid=(4,)...  22.9 us
    ppermute x18, starting transfers between devices, pack_swap(): return lax.ppermute(block, 'pack', [(i, i ^ k) for i in range(n)])  20.9 us
    dot_general x5, matrix products, matmul(): return jnp.dot(left, right, preferred_element_type=F32)  14.7 us
    pallas_call x1, Pallas kernels, down_grads(): pl.pallas_call(functools.partial(down_grads_kernel, len(acts)), grid=(4,)...  14.6 us
  transfers between devices with their start and end apart: 83, of which 36 were waited for; matrix products, arithmetic and copies ran while one was open for 16% of the time, Pallas kernels for 22%

profile of v3, /device:TPU:0, one launch (start us, length us, event | category | flops | bytes accessed | tf_op | source)
XLA Modules:
  0.0 663.1 jit_solution(9990251385015893057)
XLA Ops:
  26.4 10.3 %collective-permute-done.1 = bf16[56,2048]{1,0:T(8,128)(2,1)} collective-permute-done((bf16[56,2048]{1,0:T(8,128)(2,1)}, bf16[56,2048]{1,0:T(8,128)(2,1)}, u32[]{:S(2)}, u32[]{:S(2)}) %collective-permute-start.1) | collective-permute-done | bytes 229408 | tf_op jit(solution)/shard_map/ppermute | solution.py:24
  46.2 11.8 %collective-permute-done.13 = bf16[2,2,48,1120]{3,2,1,0:T(8,128)(2,1)S(1)} collective-permute-done((bf16[2,2,48,1120]{3,2,1,0:T(8,128)(2,1)S(1)}, bf16[2,2,48,1120]{3,2,1,0:T(8,128)(2,1)S(1)}, u32[]{:S(2)}, u32[]{:S(2)}) %collective-permute-start.13) | collective-permute-done | bytes 430112 | tf_op jit(solution)/shard_map/ppermute | solution.py:24
  62.4 17.6 %collective-permute-done.3.refs_2_ = bf16[4,56,2048]{2,1,0:T(8,128)(2,1)S(1)} collective-permute-done((bf16[4,56,2048]{2,1,0:T(8,128)(2,1)S(1)}, bf16[4,56,2048]{2,1,0:T(8,128)(2,1)S(1)}, u32[]{:S(2)}, u32[]{:S(2)}) %collective-permute-start.3) | collective-permute-done | bytes 917536 | tf_op jit(solution)/shard_map/ppermute | solution.py:34
  108.4 8.4 %shard_map.187.q_ref = bf16[256,2048]{1,0:T(8,128)(2,1)} custom-call(bf16[256,1536]{1,0:T(8,128)(2,1)} %fusion.2.xn_ref, bf16[1536,2048]{1,0:T(8,128)(2,1)} %shard_map.186.w_ref, f32[1,2048]{1,0:T(1,128)} %slice.265.bias_ref, f32[256,128]{1,0:T(8,128)} %get-tuple-element.266.cos_ref, f32[256,128]{1,0:T(8,128)} %get-tuple-element.267.sin_ref), custom_call_target="tpu_custom_call" | custom-call | flops 1610612736 | bytes 6291456 | tf_op jit(solution)/shard_map/pallas_call | solution.py:167
  155.4 15.2 %collective-permute-done.22.refs_6_ = bf16[4,48,1536]{2,1,0:T(8,128)(2,1)S(1)} collective-permute-done((bf16[4,48,1536]{2,1,0:T(8,128)(2,1)S(1)}, bf16[4,48,1536]{2,1,0:T(8,128)(2,1)S(1)}, u32[]{:S(2)}, u32[]{:S(2)}) %collective-permute-start.22) | collective-permute-done | bytes 589856 | tf_op jit(solution)/shard_map/ppermute | solution.py:34
  175.8 17.1 %collective-permute-done.24 = bf16[256,1536]{1,0:T(8,128)(2,1)} collective-permute-done((bf16[256,1536]{1,0:T(8,128)(2,1)S(1)}, bf16[256,1536]{1,0:T(8,128)(2,1)}, u32[]{:S(2)}, u32[]{:S(2)}) %collective-permute-start.24) | collective-permute-done | bytes 786464 | tf_op jit(solution)/shard_map/ppermute | solution.py:24
  193.9 8.8 %shard_map.188 = (f32[256,1536]{1,0:T(8,128)}, bf16[256,1536]{1,0:T(8,128)(2,1)}, f32[2,1,1536]{2,1,0:T(1,128)}) custom-call(s32[17]{0:T(128)} %pad_add_fusion.1.meta_ref, bf16[256,2048]{1,0:T(8,128)(2,1)} %shard_map.187.q_ref, s32[1,256]{1,0:T(1,128)} %bitcast.413, bf16[4,256,512]{2,1,0:T(8,128)(2,1)} %copy-done.30, bf16[4,256,512]{2,1,0:T(8,128)(2,1)} %copy-done.30, ...), custom_call_target="tpu_custom_call" | custom-call | flops 12884901888 | bytes 2097152 | tf_op jit(solution)/shard_map/pallas_call | solution.py:269
  212.4 13.8 %collective-permute-done.25 = bf16[256,1536]{1,0:T(8,128)(2,1)} collective-permute-done((bf16[256,1536]{1,0:T(8,128)(2,1)}, bf16[256,1536]{1,0:T(8,128)(2,1)}, u32[]{:S(2)}, u32[]{:S(2)}) %collective-permute-start.25) | collective-permute-done | bytes 786464 | tf_op jit(solution)/shard_map/ppermute | solution.py:24
  239.6 18.4 %collective-permute-done.33 = bf16[256,1536]{1,0:T(8,128)(2,1)S(1)} collective-permute-done((bf16[256,1536]{1,0:T(8,128)(2,1)S(1)}, bf16[256,1536]{1,0:T(8,128)(2,1)S(1)}, u32[]{:S(2)}, u32[]{:S(2)}) %collective-permute-start.33) | collective-permute-done | bytes 786464 | tf_op jit(solution)/shard_map/ppermute | solution.py:24
  259.7 12.3 %collective-permute-done.31 = bf16[256,1536]{1,0:T(8,128)(2,1)S(1)} collective-permute-done((bf16[256,1536]{1,0:T(8,128)(2,1)S(1)}, bf16[256,1536]{1,0:T(8,128)(2,1)S(1)}, u32[]{:S(2)}, u32[]{:S(2)}) %collective-permute-start.31) | collective-permute-done | bytes 786464 | tf_op jit(solution)/shard_map/ppermute | solution.py:24
  272.8 17.7 %collective-permute-done.34 = bf16[256,1536]{1,0:T(8,128)(2,1)S(1)} collective-permute-done((bf16[256,1536]{1,0:T(8,128)(2,1)S(1)}, bf16[256,1536]{1,0:T(8,128)(2,1)S(1)}, u32[]{:S(2)}, u32[]{:S(2)}) %collective-permute-start.34) | collective-permute-done | bytes 786464 | tf_op jit(solution)/shard_map/ppermute | solution.py:24
  300.7 32.6 %shard_map.190 = (bf16[2,256,1120]{2,1,0:T(8,128)(2,1)}, bf16[2,256,1120]{2,1,0:T(8,128)(2,1)}, bf16[2,256,1120]{2,1,0:T(8,128)(2,1)}, bf16[2,256,1120]{2,1,0:T(...) custom-call(bf16[2,256,1536]{2,1,0:T(8,128)(2,1)} %pad_maximum_fusio, ...), custom_call_target="tpu_custom_call" | custom-call | flops 66060288000 | bytes 10321920 | tf_op jit(solution)/shard_map/pallas_call | solution.py:482
  342.1 31.8 %shard_map.191 = (bf16[2,256,1120]{2,1,0:T(8,128)(2,1)}, bf16[2,256,1120]{2,1,0:T(8,128)(2,1)}, bf16[2,256,1120]{2,1,0:T(8,128)(2,1)}, bf16[2,256,1120]{2,1,0:T(...) custom-call(bf16[2,256,1536]{2,1,0:T(8,128)(2,1)} %pad_maximum_fusio, ...), custom_call_target="tpu_custom_call" | custom-call | flops 66060288000 | bytes 10321920 | tf_op jit(solution)/shard_map/pallas_call | solution.py:482
  375.9 22.9 %shard_map.192 = bf16[4,8,2,48,1120]{4,3,2,1,0:T(8,128)(2,1)} custom-call(bf16[512,1536]{1,0:T(8,128)(2,1)} %bitcast.61.refs_0_, bf16[512,1536]{1,0:T(8,128)(2,1)} %bitcast.62.refs_1_, bf16[512,1536]{1,0:T(8,128)(2,1)} %bitcast.63.refs_2_, bf16[512,1536]{1,0:T(8,128)(2,1)} %bitcast.64.refs_3_, bf16[512,1120]{1,0:T(8,128)(2,1)} %bitcast.425, ...), custom_call_target="tpu_custom_call" | custom-call | flops 24662507520 | bytes 13762560 | tf_op jit(solution)/shard_map/pallas_call | solution.py:528
  418.0 10.1 %collective-permute-done.42 = bf16[256,1536]{1,0:T(8,128)(2,1)S(1)} collective-permute-done((bf16[256,1536]{1,0:T(8,128)(2,1)S(1)}, bf16[256,1536]{1,0:T(8,128)(2,1)S(1)}, u32[]{:S(2)}, u32[]{:S(2)}) %collective-permute-start.42) | collective-permute-done | bytes 786464 | tf_op jit(solution)/shard_map/ppermute | solution.py:24
  435.9 13.3 %shard_map.193 = (bf16[256,1536]{1,0:T(8,128)(2,1)}, bf16[4,256,256]{2,1,0:T(8,128)(2,1)}, bf16[4,256,256]{2,1,0:T(8,128)(2,1)}, bf16[4,256,256]{2,1,0:T(8,128)(2,1)}, bf16[4,256,256]{2,1,0:T(8,128)(2,1)}) custom-call(s32[17]{0:T(128)} %pad_add_fusion.1.meta_ref, bf16[256,2048]{1,0:T(8,128)(2,1)} %shard_map.187.q_ref, ...), custom_call_target="tpu_custom_call" | custom-call | flops 322122547200 | bytes 2097152 | tf_op jit(solution)/shard_map/pallas_call | solution.py:367
  455.6 14.5 %collective-permute-done.46 = bf16[256,1536]{1,0:T(8,128)(2,1)} collective-permute-done((bf16[256,1536]{1,0:T(8,128)(2,1)}, bf16[256,1536]{1,0:T(8,128)(2,1)}, u32[]{:S(2)}, u32[]{:S(2)}) %collective-permute-start.46) | collective-permute-done | bytes 786464 | tf_op jit(solution)/shard_map/ppermute | solution.py:24
  480.9 14.6 %shard_map.194 = bf16[1120,1536]{1,0:T(8,128)(2,1)} custom-call(bf16[512,1120]{1,0:T(8,128)(2,1)} %bitcast.417, bf16[512,1120]{1,0:T(8,128)(2,1)} %bitcast.419, bf16[512,1120]{1,0:T(8,128)(2,1)} %bitcast.421, bf16[512,1120]{1,0:T(8,128)(2,1)} %bitcast.423, bf16[512,1536]{1,0:T(8,128)(2,1)} %bitcast.381, bf16[512,1536]{1,0:T(8,128)(2,1)} %bitcast.88.refs_5_, ...), custom_call_target="tpu_custom_call" | custom-call | flops 7046430720 | bytes 12582912 | tf_op jit(solution)/shard_map/pallas_call | solution.py:551
  497.9 10.9 %collective-permute-done.50 = bf16[256,512]{1,0:T(8,128)(2,1)} collective-permute-done((bf16[256,512]{1,0:T(8,128)(2,1)}, bf16[256,512]{1,0:T(8,128)(2,1)}, u32[]{:S(2)}, u32[]{:S(2)}) %collective-permute-start.50) | collective-permute-done | bytes 262176 | tf_op jit(solution)/shard_map/ppermute | solution.py:24
  528.7 10.5 %collective-permute-done.53 = bf16[256,768]{1,0:T(8,128)(2,1)S(1)} collective-permute-done((bf16[256,768]{1,0:T(8,128)(2,1)}, bf16[256,768]{1,0:T(8,128)(2,1)S(1)}, u32[]{:S(2)}, u32[]{:S(2)}) %collective-permute-start.53) | collective-permute-done | bytes 393248 | tf_op jit(solution)/shard_map/ppermute | solution.py:34
  549.0 10.5 %collective-permute-start.70 = (bf16[194,128]{1,0:T(8,128)(2,1)S(1)}, bf16[194,128]{1,0:T(8,128)(2,1)S(1)}, u32[]{:S(2)}, u32[]{:S(2)}) collective-permute-start(bf16[194,128]{1,0:T(8,128)(2,1)S(1)} %get-tuple-element.240), channel_id=1, source_target_pairs={{0,16},{4,20},{8,24},{12,28},{16,0},{20,4},{24,8},{28,12},{1,17},{... | collective-permute-start | bytes 149000 | tf_op jit(solution)/shard_map/ppermute | solution.py:24
  583.5 16.0 %collective-permute-done.57 = bf16[2,2,48,1120]{3,2,1,0:T(8,128)(2,1)S(1)} collective-permute-done((bf16[2,2,48,1120]{3,2,1,0:T(8,128)(2,1)S(1)}, bf16[2,2,48,1120]{3,2,1,0:T(8,128)(2,1)S(1)}, u32[]{:S(2)}, u32[]{:S(2)}) %collective-permute-start.57) | collective-permute-done | bytes 430112 | tf_op jit(solution)/shard_map/ppermute | solution.py:24
  601.3 8.9 %collective-permute-start.61 = (bf16[192,768]{1,0:T(8,128)(2,1)S(1)}, bf16[192,768]{1,0:T(8,128)(2,1)}, u32[]{:S(2)}, u32[]{:S(2)}) collective-permute-start(bf16[192,768]{1,0:T(8,128)(2,1)S(1)} %get-tuple-element.199), channel_id=1, source_target_pairs={{0,24},{4,28},{8,0},{12,4},{16,8},{20,12},{24,16},{28,20},{1,25},{... | collective-permute-start | bytes 884744 | tf_op jit(solution)/shard_map/ppermute | solution.py:24
  618.5 19.4 %collective-permute-done.60 = bf16[192,768]{1,0:T(8,128)(2,1)} collective-permute-done((bf16[192,768]{1,0:T(8,128)(2,1)S(1)}, bf16[192,768]{1,0:T(8,128)(2,1)}, u32[]{:S(2)}, u32[]{:S(2)}) %collective-permute-start.60) | collective-permute-done | bytes 294944 | tf_op jit(solution)/shard_map/ppermute | solution.py:24
  (468 shorter events, 279.6 us)
Async XLA Ops:
  7.2 284.7 %all-gather.6.cloned.1.call-start = ((), (), s32[]{:S(2)}) async-start(), calls=%async_computation.2 | async-start | bytes 4423680 | tf_op jit(solution)/shard_map/all_gather | solution.py:617
  40.7 39.3 %collective-permute-start.3 = (bf16[4,56,2048]{2,1,0:T(8,128)(2,1)S(1)}, bf16[4,56,2048]{2,1,0:T(8,128)(2,1)S(1)}, u32[]{:S(2)}, u32[]{:S(2)}) collective-permute-start(bf16[4,56,2048]{2,1,0:T(8,128)(2,1)S(1)} %pad_maximum_fusion.10.refs_0_), channel_id=1, source_target_pairs={{0,1},{1,0},{2,3},{3,2},{4,5},{5,4},{6,7},{7,6},{8,9},{9,8},{10,11... | collective-permute-start | bytes 2752520 | tf_op jit(solution)/shard_map/ppermute | solution.py:34
  41.1 39.0 %collective-permute-start.6 = (bf16[4,56,2048]{2,1,0:T(8,128)(2,1)S(1)}, bf16[4,56,2048]{2,1,0:T(8,128)(2,1)S(1)}, u32[]{:S(2)}, u32[]{:S(2)}) collective-permute-start(bf16[4,56,2048]{2,1,0:T(8,128)(2,1)S(1)} %pad_maximum_fusion.10.refs_0_), channel_id=1, source_target_pairs={{0,2},{1,3},{2,0},{3,1},{4,6},{5,7},{6,4},{7,5},{8,10},{9,11},{10,... | collective-permute-start | bytes 2752520 | tf_op jit(solution)/shard_map/ppermute | solution.py:34
  43.9 36.8 %collective-permute-start.14 = (bf16[2,2,48,1120]{3,2,1,0:T(8,128)(2,1)S(1)}, bf16[2,2,48,1120]{3,2,1,0:T(8,128)(2,1)S(1)}, u32[]{:S(2)}, u32[]{:S(2)}) collective-permute-start(bf16[2,2,48,1120]{3,2,1,0:T(8,128)(2,1)S(1)} %bitcast.396), channel_id=1, source_target_pairs={{0,16},{4,20},{8,24},{12,28},{16,0},{20,4},{24,8},{28,12},{1,17},{... | collective-permute-start | bytes 1290248 | tf_op jit(solution)/shard_map/ppermute | solution.py:24
  94.4 201.6 %all-gather.8.cloned.1.call-start = ((), (), s32[]{:S(2)}) async-start(), calls=%async_computation.3 | async-start | bytes 4423680 | tf_op jit(solution)/shard_map/all_gather | solution.py:617
  95.5 204.7 %all-gather.10.cloned.1.call-start = ((), (), s32[]{:S(2)}) async-start(), calls=%async_computation.4 | async-start | bytes 4300800 | tf_op jit(solution)/shard_map/all_gather | solution.py:613
  135.6 34.9 %collective-permute-start.22 = (bf16[4,48,1536]{2,1,0:T(8,128)(2,1)S(1)}, bf16[4,48,1536]{2,1,0:T(8,128)(2,1)S(1)}, u32[]{:S(2)}, u32[]{:S(2)}) collective-permute-start(bf16[4,48,1536]{2,1,0:T(8,128)(2,1)S(1)} %pad_maximum_fusion.11.refs_0_), channel_id=1, source_target_pairs={{0,3},{1,2},{2,1},{3,0},{4,7},{5,6},{6,5},{7,4},{8,11},{9,10},{10,... | collective-permute-start | bytes 1769480 | tf_op jit(solution)/shard_map/ppermute | solution.py:34
  173.3 36.2 %collective-permute-start.26 = (bf16[256,1536]{1,0:T(8,128)(2,1)S(1)}, bf16[256,1536]{1,0:T(8,128)(2,1)S(1)}, u32[]{:S(2)}, u32[]{:S(2)}) collective-permute-start(bf16[256,1536]{1,0:T(8,128)(2,1)S(1)} %bitcast.363), channel_id=1, source_target_pairs={{0,24},{4,28},{8,0},{12,4},{16,8},{20,12},{24,16},{28,20},{1,25},{... | collective-permute-start | bytes 2359304 | tf_op jit(solution)/shard_map/ppermute | solution.py:24
  192.9 33.3 %collective-permute-start.25 = (bf16[256,1536]{1,0:T(8,128)(2,1)}, bf16[256,1536]{1,0:T(8,128)(2,1)}, u32[]{:S(2)}, u32[]{:S(2)}) collective-permute-start(bf16[256,1536]{1,0:T(8,128)(2,1)} %collective-permute-done.24), channel_id=1, source_target_pairs={{0,8},{4,12},{8,16},{12,20},{16,24},{20,28},{24,0},{28,4},{1,9},{5... | collective-permute-start | bytes 2359304 | tf_op jit(solution)/shard_map/ppermute | solution.py:24
  212.4 223.0 %all-gather.12.cloned.1.call-start = ((), (), s32[]{:S(2)}) async-start(), calls=%async_computation.5 | async-start | bytes 3932160 | tf_op jit(solution)/shard_map/all_gather | solution.py:651
  235.9 36.1 %collective-permute-start.31 = (bf16[256,1536]{1,0:T(8,128)(2,1)S(1)}, bf16[256,1536]{1,0:T(8,128)(2,1)S(1)}, u32[]{:S(2)}, u32[]{:S(2)}) collective-permute-start(bf16[256,1536]{1,0:T(8,128)(2,1)S(1)} %multiply_convert_fusion), channel_id=1, source_target_pairs={{0,24},{4,28},{8,0},{12,4},{16,8},{20,12},{24,16},{28,20},{1,25},{... | collective-permute-start | bytes 2359304 | tf_op jit(solution)/shard_map/ppermute | solution.py:24
  258.0 32.5 %collective-permute-start.34 = (bf16[256,1536]{1,0:T(8,128)(2,1)S(1)}, bf16[256,1536]{1,0:T(8,128)(2,1)S(1)}, u32[]{:S(2)}, u32[]{:S(2)}) collective-permute-start(bf16[256,1536]{1,0:T(8,128)(2,1)S(1)} %collective-permute-done.33), channel_id=1, source_target_pairs={{0,8},{4,12},{8,16},{12,20},{16,24},{20,28},{24,0},{28,4},{1,9},{5... | collective-permute-start | bytes 2359304 | tf_op jit(solution)/shard_map/ppermute | solution.py:24
  259.6 41.1 %collective-permute-start.36 = (bf16[2,256,1536]{2,1,0:T(8,128)(2,1)S(1)}, bf16[2,256,1536]{2,1,0:T(8,128)(2,1)}, u32[]{:S(2)}, u32[]{:S(2)}) collective-permute-start(bf16[2,256,1536]{2,1,0:T(8,128)(2,1)S(1)} %pad_maximum_fusion.4.t0_ref), channel_id=1, source_target_pairs={{0,4},{4,0},{8,12},{12,8},{16,20},{20,16},{24,28},{28,24},{1,5},{5... | collective-permute-start | bytes 4718600 | tf_op jit(solution)/shard_map/ppermute | solution.py:29
  300.2 135.2 %all-gather.14.cloned.1.call-start = ((), (), s32[]{:S(2)}) async-start(), calls=%async_computation.6 | async-start | bytes 3932160 | tf_op jit(solution)/shard_map/all_gather | solution.py:650
  335.9 230.1 %reduce-scatter.5.cloned.1.call-start = ((), (), s32[]{:S(2)}) async-start(), calls=%async_computation.7 | async-start | bytes 8847360 | tf_op jit(solution)/shard_map/reduce_scatter | solution.py:705
  341.8 32.5 %collective-permute-start.40 = (bf16[256,1536]{1,0:T(8,128)(2,1)S(1)}, bf16[256,1536]{1,0:T(8,128)(2,1)}, u32[]{:S(2)}, u32[]{:S(2)}) collective-permute-start(bf16[256,1536]{1,0:T(8,128)(2,1)S(1)} %fusion.82), channel_id=1, source_target_pairs={{0,24},{4,28},{8,0},{12,4},{16,8},{20,12},{24,16},{28,20},{1,25},{... | collective-permute-start | bytes 2359304 | tf_op jit(solution)/shard_map/ppermute | solution.py:24
  373.9 32.1 %collective-permute-start.39 = (bf16[2,256,1536]{2,1,0:T(8,128)(2,1)}, bf16[2,256,1536]{2,1,0:T(8,128)(2,1)S(1)}, u32[]{:S(2)}, u32[]{:S(2)}) collective-permute-start(bf16[2,256,1536]{2,1,0:T(8,128)(2,1)} %get-tuple-element.111), channel_id=1, source_target_pairs={{0,4},{4,0},{8,12},{12,8},{16,20},{20,16},{24,28},{28,24},{1,5},{5... | collective-permute-start | bytes 4718600 | tf_op jit(solution)/shard_map/ppermute | solution.py:29
  375.6 42.4 %collective-permute-start.41 = (bf16[256,1536]{1,0:T(8,128)(2,1)S(1)}, bf16[256,1536]{1,0:T(8,128)(2,1)S(1)}, u32[]{:S(2)}, u32[]{:S(2)}) collective-permute-start(bf16[256,1536]{1,0:T(8,128)(2,1)S(1)} %fusion.9), channel_id=1, source_target_pairs={{0,24},{4,28},{8,0},{12,4},{16,8},{20,12},{24,16},{28,20},{1,25},{... | collective-permute-start | bytes 2359304 | tf_op jit(solution)/shard_map/ppermute | solution.py:24
  434.4 35.7 %collective-permute-start.46 = (bf16[256,1536]{1,0:T(8,128)(2,1)}, bf16[256,1536]{1,0:T(8,128)(2,1)}, u32[]{:S(2)}, u32[]{:S(2)}) collective-permute-start(bf16[256,1536]{1,0:T(8,128)(2,1)} %slice.277), channel_id=1, source_target_pairs={{0,8},{4,12},{8,16},{12,20},{16,24},{20,28},{24,0},{28,4},{1,9},{5... | collective-permute-start | bytes 2359304 | tf_op jit(solution)/shard_map/ppermute | solution.py:24
  435.4 180.5 %reduce-scatter.7.cloned.1.call-start = ((), (), s32[]{:S(2)}) async-start(), calls=%async_computation.8 | async-start | bytes 4300800
  471.2 88.3 %collective-permute-start.47 = (bf16[256,1536]{1,0:T(8,128)(2,1)}, bf16[256,1536]{1,0:T(8,128)(2,1)}, u32[]{:S(2)}, u32[]{:S(2)}) collective-permute-start(bf16[256,1536]{1,0:T(8,128)(2,1)} %convert_add_fusion.7), channel_id=1, source_target_pairs={{0,24},{4,28},{8,0},{12,4},{16,8},{20,12},{24,16},{28,20},{1,25},{... | collective-permute-start | bytes 2359304 | tf_op jit(solution)/shard_map/ppermute | solution.py:24
  497.8 30.9 %collective-permute-start.52 = (bf16[256,768]{1,0:T(8,128)(2,1)}, bf16[256,768]{1,0:T(8,128)(2,1)}, u32[]{:S(2)}, u32[]{:S(2)}) collective-permute-start(bf16[256,768]{1,0:T(8,128)(2,1)} %get-tuple-element.193), channel_id=1, source_target_pairs={{0,3},{1,2},{2,1},{3,0},{4,7},{5,6},{6,5},{7,4},{8,11},{9,10},{10,... | collective-permute-start | bytes 1179656 | tf_op jit(solution)/shard_map/ppermute | solution.py:34
  612.0 34.7 %collective-permute-start.72 = (bf16[48,128]{1,0:T(8,128)(2,1)S(1)}, bf16[48,128]{1,0:T(8,128)(2,1)S(1)}, u32[]{:S(2)}, u32[]{:S(2)}) collective-permute-start(bf16[48,128]{1,0:T(8,128)(2,1)S(1)} %get-tuple-element.251), channel_id=1, source_target_pairs={{0,3},{1,2},{2,1},{3,0},{4,7},{5,6},{6,5},{7,4},{8,11},{9,10},{10,... | collective-permute-start | bytes 36872 | tf_op jit(solution)/shard_map/ppermute | solution.py:34
  613.5 33.2 %collective-permute-start.73 = (bf16[48,128]{1,0:T(8,128)(2,1)S(1)}, bf16[48,128]{1,0:T(8,128)(2,1)S(1)}, u32[]{:S(2)}, u32[]{:S(2)}) collective-permute-start(bf16[48,128]{1,0:T(8,128)(2,1)S(1)} %get-tuple-element.250), channel_id=1, source_target_pairs={{0,2},{1,3},{2,0},{3,1},{4,6},{5,7},{6,4},{7,5},{8,10},{9,11},{10,... | collective-permute-start | bytes 36872 | tf_op jit(solution)/shard_map/ppermute | solution.py:34
  (136 other events, 1931.4 us)
Sparse Core Ops, SparseCore 0:
  94.5 52.4 all-gather.5
  148.8 54.3 all-gather.7
  212.5 51.5 all-gather.9
  300.3 40.6 all-gather.11
  343.3 43.9 all-gather.13
  435.5 83.3 reduce-scatter.4
  522.0 50.9 reduce-scatter.6

commit v4 on v3

--- a/solution.py
+++ b/solution.py
@@ -622,13 +622,13 @@
 
     stream = tokens[0].astype(F32)
     normed = rms_norm(stream, attn_gain).astype(BF)
-    qkv = qkv_project(normed, qkv_full, bias, cosine, sine)
-    own = qkv[:, q_cols:]
-    kv_line = jnp.stack([own] + [chip_shift(own, s, cyclic=False) for s in range(1, chips)])
     top = after(out_grad[0], gate_up)
     t = {0: grad_top, 1: chip_shift(top, 1)}
     if chips > 2:
         t[chips - 1] = chip_shift(top, -1)
+    qkv = qkv_project(after(normed, t[1]), qkv_full, bias, cosine, sine)
+    own = qkv[:, q_cols:]
+    kv_line = jnp.stack([own] + [chip_shift(own, s, cyclic=False) for s in range(1, chips)])
     kv_other = core_swap(after(kv_line, out_lines))
     back = jnp.arange(chips, dtype=jnp.int32)
     source = jnp.concatenate([(chip - back) * 2 + core, (chip - back) * 2 + 1 - core])
@@ -671,7 +671,7 @@
         h[chips - 1] = chip_shift(hidden, -1)
     for s in range(2, chips - 1):
         h[s] = chip_shift(h[s - 1], 1)
-    h[0], h[chips - 1] = after((h[0], h[chips - 1]), h[chips - 1])
+    h[0], h[chips - 1] = after((h[0], h[chips - 1]), h[chips - 1], gate_w, up_w)
     h[1] = after(h[1], h[chips - 1])
     first, second = (list(range(chips - 2, 0, -1)), [chips - 1, 0]) if chips > 2 else ([1, 0], [])
     hs, ts, fed, partials = [], [], [], {}

time: 673 us -> 662 us (0.984)
  waiting for transfers between devices: 269 us -> 253 us
    ppermute x36, waiting for transfers between devices: 207 us -> 181 us  [chip_shift(): return lax.ppermute(block, 'blk', route)]
  transfers between devices with their start and end apart: 83 -> 83, of which waited for: 36 -> 38; matrix products, arithmetic and copies ran while one was open for 16% -> 18% of each run, Pallas kernels for 22% -> 22%
where the time goes in v4:
time: 662 us; the launch traced here: 653 us
  waiting for transfers between devices  253 us (38%)
  Pallas kernels  145 us (22%)
  starting transfers between devices  94.1 us (14%)
  other arithmetic  61.6 us (9%)
  local copies, waits for them, and re-layouts  50.3 us (8%)
  matrix products  33.1 us (5%)
  between operations  16 us (2%)
    ppermute x36, waiting for transfers between devices, chip_shift(): return lax.ppermute(block, 'blk', route)  181 us
    ppermute x36, starting transfers between devices, chip_shift(): return lax.ppermute(block, 'blk', route)  67.5 us
    pallas_call x2, Pallas kernels, feed(): pl.pallas_call(feed_kernel, grid=(count,), in_specs=[tokens] * 4 + [pl.Bl...  64.5 us
    ppermute x18, waiting for transfers between devices, pack_swap(): return lax.ppermute(block, 'pack', [(i, i ^ k) for i in range(n)])  57.7 us
    pallas_call x1, Pallas kernels, gate_up_grads(): pl.pallas_call(functools.partial(grads_kernel, packs, len(hs)), grid=(4,)...  23 us
    ppermute x18, starting transfers between devices, pack_swap(): return lax.ppermute(block, 'pack', [(i, i ^ k) for i in range(n)])  20 us
    dot_general x5, matrix products, matmul(): return jnp.dot(left, right, preferred_element_type=F32)  18.2 us
    pallas_call x1, Pallas kernels, down_grads(): pl.pallas_call(functools.partial(down_grads_kernel, len(acts)), grid=(4,)...  14.5 us
  transfers between devices with their start and end apart: 83, of which 38 were waited for; matrix products, arithmetic and copies ran while one was open for 18% of the time, Pallas kernels for 22%

profile of v4, /device:TPU:0, one launch (start us, length us, event | category | flops | bytes accessed | tf_op | source)
XLA Modules:
  0.0 653.0 jit_solution(17424357407796386102)
XLA Ops:
  26.4 10.3 %collective-permute-done.1 = bf16[56,2048]{1,0:T(8,128)(2,1)} collective-permute-done((bf16[56,2048]{1,0:T(8,128)(2,1)}, bf16[56,2048]{1,0:T(8,128)(2,1)}, u32[]{:S(2)}, u32[]{:S(2)}) %collective-permute-start.1) | collective-permute-done | bytes 229408 | tf_op jit(solution)/shard_map/ppermute | solution.py:24
  46.2 11.8 %collective-permute-done.10 = bf16[2,2,48,1120]{3,2,1,0:T(8,128)(2,1)S(1)} collective-permute-done((bf16[2,2,48,1120]{3,2,1,0:T(8,128)(2,1)S(1)}, bf16[2,2,48,1120]{3,2,1,0:T(8,128)(2,1)S(1)}, u32[]{:S(2)}, u32[]{:S(2)}) %collective-permute-start.10) | collective-permute-done | bytes 430112 | tf_op jit(solution)/shard_map/ppermute | solution.py:24
  62.4 17.6 %collective-permute-done.3.refs_2_ = bf16[4,56,2048]{2,1,0:T(8,128)(2,1)S(1)} collective-permute-done((bf16[4,56,2048]{2,1,0:T(8,128)(2,1)S(1)}, bf16[4,56,2048]{2,1,0:T(8,128)(2,1)S(1)}, u32[]{:S(2)}, u32[]{:S(2)}) %collective-permute-start.3) | collective-permute-done | bytes 917536 | tf_op jit(solution)/shard_map/ppermute | solution.py:34
  101.2 6.9 %shard_map.186.w_ref = bf16[1536,2048]{1,0:T(8,128)(2,1)} custom-call(s32[3]{0:T(128)} %pad_add_fusion.2.at_ref, bf16[4,56,2048]{2,1,0:T(8,128)(2,1)} %copy-done.13, bf16[4,56,2048]{2,1,0:T(8,128)(2,1)} %collective-permute-done.4.refs_1_, bf16[4,56,2048]{2,1,0:T(8,128)(2,1)} %copy-done.22, bf16[4,56,2048]{2,1,0:T(8,128)(2,1)} %copy-done.26, ...), custom_call_target="tpu_custom_call" | custom-call | bytes 12582912 | tf_op jit(solution)/shard_map/pallas_call | solution.py:434
  113.5 6.9 %collective-permute-done.14 = bf16[256,1536]{1,0:T(8,128)(2,1)} collective-permute-done((bf16[256,1536]{1,0:T(8,128)(2,1)S(1)}, bf16[256,1536]{1,0:T(8,128)(2,1)}, u32[]{:S(2)}, u32[]{:S(2)}) %collective-permute-start.14) | collective-permute-done | bytes 786464 | tf_op jit(solution)/shard_map/ppermute | solution.py:24
  120.4 8.5 %shard_map.187.q_ref = bf16[256,2048]{1,0:T(8,128)(2,1)} custom-call(bf16[256,1536]{1,0:T(8,128)(2,1)} %fusion.2.xn_ref, bf16[1536,2048]{1,0:T(8,128)(2,1)} %shard_map.186.w_ref, f32[1,2048]{1,0:T(1,128)} %slice.265.bias_ref, f32[256,128]{1,0:T(8,128)} %get-tuple-element.268.cos_ref, f32[256,128]{1,0:T(8,128)} %get-tuple-element.269.sin_ref), custom_call_target="tpu_custom_call" | custom-call | flops 1610612736 | bytes 6291456 | tf_op jit(solution)/shard_map/pallas_call | solution.py:167
  155.3 15.5 %collective-permute-done.23.refs_6_ = bf16[4,48,1536]{2,1,0:T(8,128)(2,1)S(1)} collective-permute-done((bf16[4,48,1536]{2,1,0:T(8,128)(2,1)S(1)}, bf16[4,48,1536]{2,1,0:T(8,128)(2,1)S(1)}, u32[]{:S(2)}, u32[]{:S(2)}) %collective-permute-start.23) | collective-permute-done | bytes 589856 | tf_op jit(solution)/shard_map/ppermute | solution.py:34
  176.6 8.8 %shard_map.188 = (f32[256,1536]{1,0:T(8,128)}, bf16[256,1536]{1,0:T(8,128)(2,1)}, f32[2,1,1536]{2,1,0:T(1,128)}) custom-call(s32[17]{0:T(128)} %pad_add_fusion.1.meta_ref, bf16[256,2048]{1,0:T(8,128)(2,1)} %shard_map.187.q_ref, s32[1,256]{1,0:T(1,128)} %bitcast.411, bf16[4,256,512]{2,1,0:T(8,128)(2,1)} %copy-done.30, bf16[4,256,512]{2,1,0:T(8,128)(2,1)} %copy-done.30, ...), custom_call_target="tpu_custom_call" | custom-call | flops 12884901888 | bytes 2097152 | tf_op jit(solution)/shard_map/pallas_call | solution.py:269
  196.4 14.5 %collective-permute-done.25 = bf16[256,1536]{1,0:T(8,128)(2,1)} collective-permute-done((bf16[256,1536]{1,0:T(8,128)(2,1)}, bf16[256,1536]{1,0:T(8,128)(2,1)}, u32[]{:S(2)}, u32[]{:S(2)}) %collective-permute-start.25) | collective-permute-done | bytes 786464 | tf_op jit(solution)/shard_map/ppermute | solution.py:24
  225.2 18.5 %collective-permute-done.33 = bf16[256,1536]{1,0:T(8,128)(2,1)S(1)} collective-permute-done((bf16[256,1536]{1,0:T(8,128)(2,1)S(1)}, bf16[256,1536]{1,0:T(8,128)(2,1)S(1)}, u32[]{:S(2)}, u32[]{:S(2)}) %collective-permute-start.33) | collective-permute-done | bytes 786464 | tf_op jit(solution)/shard_map/ppermute | solution.py:24
  260.4 15.8 %collective-permute-done.34 = bf16[256,1536]{1,0:T(8,128)(2,1)} collective-permute-done((bf16[256,1536]{1,0:T(8,128)(2,1)S(1)}, bf16[256,1536]{1,0:T(8,128)(2,1)}, u32[]{:S(2)}, u32[]{:S(2)}) %collective-permute-start.34) | collective-permute-done | bytes 786464 | tf_op jit(solution)/shard_map/ppermute | solution.py:24
  282.4 32.4 %shard_map.190 = (bf16[2,256,1120]{2,1,0:T(8,128)(2,1)}, bf16[2,256,1120]{2,1,0:T(8,128)(2,1)}, bf16[2,256,1120]{2,1,0:T(8,128)(2,1)}, bf16[2,256,1120]{2,1,0:T(...) custom-call(bf16[2,256,1536]{2,1,0:T(8,128)(2,1)} %pad_maximum_fusio, ...), custom_call_target="tpu_custom_call" | custom-call | flops 66060288000 | bytes 10321920 | tf_op jit(solution)/shard_map/pallas_call | solution.py:482
  326.9 32.0 %shard_map.191 = (bf16[2,256,1120]{2,1,0:T(8,128)(2,1)}, bf16[2,256,1120]{2,1,0:T(8,128)(2,1)}, bf16[2,256,1120]{2,1,0:T(8,128)(2,1)}, bf16[2,256,1120]{2,1,0:T(...) custom-call(bf16[2,256,1536]{2,1,0:T(8,128)(2,1)} %pad_maximum_fusio, ...), custom_call_target="tpu_custom_call" | custom-call | flops 66060288000 | bytes 10321920 | tf_op jit(solution)/shard_map/pallas_call | solution.py:482
  361.9 23.0 %shard_map.192 = bf16[4,8,2,48,1120]{4,3,2,1,0:T(8,128)(2,1)} custom-call(bf16[512,1536]{1,0:T(8,128)(2,1)} %bitcast.61.refs_0_, bf16[512,1536]{1,0:T(8,128)(2,1)} %bitcast.62.refs_1_, bf16[512,1536]{1,0:T(8,128)(2,1)} %bitcast.63.refs_2_, bf16[512,1536]{1,0:T(8,128)(2,1)} %bitcast.64.refs_3_, bf16[512,1120]{1,0:T(8,128)(2,1)} %bitcast.423, ...), custom_call_target="tpu_custom_call" | custom-call | flops 24662507520 | bytes 13762560 | tf_op jit(solution)/shard_map/pallas_call | solution.py:528
  396.0 12.1 %collective-permute-done.42 = bf16[256,1536]{1,0:T(8,128)(2,1)} collective-permute-done((bf16[256,1536]{1,0:T(8,128)(2,1)}, bf16[256,1536]{1,0:T(8,128)(2,1)}, u32[]{:S(2)}, u32[]{:S(2)}) %collective-permute-start.42) | collective-permute-done | bytes 786464 | tf_op jit(solution)/shard_map/ppermute | solution.py:24
  429.2 13.4 %shard_map.193 = (bf16[256,1536]{1,0:T(8,128)(2,1)}, bf16[4,256,256]{2,1,0:T(8,128)(2,1)}, bf16[4,256,256]{2,1,0:T(8,128)(2,1)}, bf16[4,256,256]{2,1,0:T(8,128)(2,1)}, bf16[4,256,256]{2,1,0:T(8,128)(2,1)}) custom-call(s32[17]{0:T(128)} %pad_add_fusion.1.meta_ref, bf16[256,2048]{1,0:T(8,128)(2,1)} %shard_map.187.q_ref, ...), custom_call_target="tpu_custom_call" | custom-call | flops 322122547200 | bytes 2097152 | tf_op jit(solution)/shard_map/pallas_call | solution.py:367
  442.6 20.2 %collective-permute-done.45 = bf16[256,1536]{1,0:T(8,128)(2,1)} collective-permute-done((bf16[256,1536]{1,0:T(8,128)(2,1)}, bf16[256,1536]{1,0:T(8,128)(2,1)}, u32[]{:S(2)}, u32[]{:S(2)}) %collective-permute-start.45) | collective-permute-done | bytes 786464 | tf_op jit(solution)/shard_map/ppermute | solution.py:24
  475.7 14.5 %shard_map.194 = bf16[1120,1536]{1,0:T(8,128)(2,1)} custom-call(bf16[512,1120]{1,0:T(8,128)(2,1)} %bitcast.415, bf16[512,1120]{1,0:T(8,128)(2,1)} %bitcast.417, bf16[512,1120]{1,0:T(8,128)(2,1)} %bitcast.419, bf16[512,1120]{1,0:T(8,128)(2,1)} %bitcast.421, bf16[512,1536]{1,0:T(8,128)(2,1)} %bitcast.87.refs_4_, bf16[512,1536]{1,0:T(8,128)(2,1)} %bitcast.88.refs_5_, ...), custom_call_target="tpu_custom_call" | custom-call | flops 7046430720 | bytes 12582912 | tf_op jit(solution)/shard_map/pallas_call | solution.py:551
  492.5 11.2 %collective-permute-done.50 = bf16[256,512]{1,0:T(8,128)(2,1)} collective-permute-done((bf16[256,512]{1,0:T(8,128)(2,1)}, bf16[256,512]{1,0:T(8,128)(2,1)}, u32[]{:S(2)}, u32[]{:S(2)}) %collective-permute-start.50) | collective-permute-done | bytes 262176 | tf_op jit(solution)/shard_map/ppermute | solution.py:24
  506.6 6.0 fusion.3
  525.6 10.6 %collective-permute-done.53 = bf16[256,768]{1,0:T(8,128)(2,1)S(1)} collective-permute-done((bf16[256,768]{1,0:T(8,128)(2,1)}, bf16[256,768]{1,0:T(8,128)(2,1)S(1)}, u32[]{:S(2)}, u32[]{:S(2)}) %collective-permute-start.53) | collective-permute-done | bytes 393248 | tf_op jit(solution)/shard_map/ppermute | solution.py:34
  572.7 16.4 %collective-permute-done.57 = bf16[2,2,48,1120]{3,2,1,0:T(8,128)(2,1)S(1)} collective-permute-done((bf16[2,2,48,1120]{3,2,1,0:T(8,128)(2,1)S(1)}, bf16[2,2,48,1120]{3,2,1,0:T(8,128)(2,1)S(1)}, u32[]{:S(2)}, u32[]{:S(2)}) %collective-permute-start.57) | collective-permute-done | bytes 430112 | tf_op jit(solution)/shard_map/ppermute | solution.py:24
  591.0 10.6 %collective-permute-start.61 = (bf16[192,768]{1,0:T(8,128)(2,1)S(1)}, bf16[192,768]{1,0:T(8,128)(2,1)}, u32[]{:S(2)}, u32[]{:S(2)}) collective-permute-start(bf16[192,768]{1,0:T(8,128)(2,1)S(1)} %get-tuple-element.201), channel_id=1, source_target_pairs={{0,24},{4,28},{8,0},{12,4},{16,8},{20,12},{24,16},{28,20},{1,25},{... | collective-permute-start | bytes 884744 | tf_op jit(solution)/shard_map/ppermute | solution.py:24
  609.1 18.5 %collective-permute-done.60 = bf16[192,768]{1,0:T(8,128)(2,1)} collective-permute-done((bf16[192,768]{1,0:T(8,128)(2,1)S(1)}, bf16[192,768]{1,0:T(8,128)(2,1)}, u32[]{:S(2)}, u32[]{:S(2)}) %collective-permute-start.60) | collective-permute-done | bytes 294944 | tf_op jit(solution)/shard_map/ppermute | solution.py:24
  (466 shorter events, 281.0 us)
Async XLA Ops:
  7.2 240.6 %all-gather.6.cloned.1.call-start = ((), (), s32[]{:S(2)}) async-start(), calls=%async_computation.2 | async-start | bytes 4423680 | tf_op jit(solution)/shard_map/all_gather | solution.py:617
  40.7 39.3 %collective-permute-start.3 = (bf16[4,56,2048]{2,1,0:T(8,128)(2,1)S(1)}, bf16[4,56,2048]{2,1,0:T(8,128)(2,1)S(1)}, u32[]{:S(2)}, u32[]{:S(2)}) collective-permute-start(bf16[4,56,2048]{2,1,0:T(8,128)(2,1)S(1)} %pad_maximum_fusion.10.refs_0_), channel_id=1, source_target_pairs={{0,1},{1,0},{2,3},{3,2},{4,5},{5,4},{6,7},{7,6},{8,9},{9,8},{10,11... | collective-permute-start | bytes 2752520 | tf_op jit(solution)/shard_map/ppermute | solution.py:34
  41.1 39.0 %collective-permute-start.6 = (bf16[4,56,2048]{2,1,0:T(8,128)(2,1)S(1)}, bf16[4,56,2048]{2,1,0:T(8,128)(2,1)S(1)}, u32[]{:S(2)}, u32[]{:S(2)}) collective-permute-start(bf16[4,56,2048]{2,1,0:T(8,128)(2,1)S(1)} %pad_maximum_fusion.10.refs_0_), channel_id=1, source_target_pairs={{0,2},{1,3},{2,0},{3,1},{4,6},{5,7},{6,4},{7,5},{8,10},{9,11},{10,... | collective-permute-start | bytes 2752520 | tf_op jit(solution)/shard_map/ppermute | solution.py:34
  43.9 36.8 %collective-permute-start.11 = (bf16[2,2,48,1120]{3,2,1,0:T(8,128)(2,1)S(1)}, bf16[2,2,48,1120]{3,2,1,0:T(8,128)(2,1)S(1)}, u32[]{:S(2)}, u32[]{:S(2)}) collective-permute-start(bf16[2,2,48,1120]{3,2,1,0:T(8,128)(2,1)S(1)} %bitcast.394), channel_id=1, source_target_pairs={{0,16},{4,20},{8,24},{12,28},{16,0},{20,4},{24,8},{28,12},{1,17},{... | collective-permute-start | bytes 1290248 | tf_op jit(solution)/shard_map/ppermute | solution.py:24
  94.3 157.5 %all-gather.8.cloned.1.call-start = ((), (), s32[]{:S(2)}) async-start(), calls=%async_computation.3 | async-start | bytes 4423680 | tf_op jit(solution)/shard_map/all_gather | solution.py:617
  95.4 183.3 %all-gather.10.cloned.1.call-start = ((), (), s32[]{:S(2)}) async-start(), calls=%async_computation.4 | async-start | bytes 4300800 | tf_op jit(solution)/shard_map/all_gather | solution.py:613
  137.3 33.5 %collective-permute-start.23 = (bf16[4,48,1536]{2,1,0:T(8,128)(2,1)S(1)}, bf16[4,48,1536]{2,1,0:T(8,128)(2,1)S(1)}, u32[]{:S(2)}, u32[]{:S(2)}) collective-permute-start(bf16[4,48,1536]{2,1,0:T(8,128)(2,1)S(1)} %pad_maximum_fusion.11.refs_0_), channel_id=1, source_target_pairs={{0,3},{1,2},{2,1},{3,0},{4,7},{5,6},{6,5},{7,4},{8,11},{9,10},{10,... | collective-permute-start | bytes 1769480 | tf_op jit(solution)/shard_map/ppermute | solution.py:34
  175.7 35.3 %collective-permute-start.25 = (bf16[256,1536]{1,0:T(8,128)(2,1)}, bf16[256,1536]{1,0:T(8,128)(2,1)}, u32[]{:S(2)}, u32[]{:S(2)}) collective-permute-start(bf16[256,1536]{1,0:T(8,128)(2,1)} %collective-permute-done.14), channel_id=1, source_target_pairs={{0,8},{4,12},{8,16},{12,20},{16,24},{20,28},{24,0},{28,4},{1,9},{5... | collective-permute-start | bytes 2359304 | tf_op jit(solution)/shard_map/ppermute | solution.py:24
  196.3 199.6 %all-gather.12.cloned.1.call-start = ((), (), s32[]{:S(2)}) async-start(), calls=%async_computation.5 | async-start | bytes 3932160 | tf_op jit(solution)/shard_map/all_gather | solution.py:651
  224.7 35.8 %collective-permute-start.31 = (bf16[256,1536]{1,0:T(8,128)(2,1)S(1)}, bf16[256,1536]{1,0:T(8,128)(2,1)S(1)}, u32[]{:S(2)}, u32[]{:S(2)}) collective-permute-start(bf16[256,1536]{1,0:T(8,128)(2,1)S(1)} %multiply_convert_fusion), channel_id=1, source_target_pairs={{0,24},{4,28},{8,0},{12,4},{16,8},{20,12},{24,16},{28,20},{1,25},{... | collective-permute-start | bytes 2359304 | tf_op jit(solution)/shard_map/ppermute | solution.py:24
  243.6 32.6 %collective-permute-start.34 = (bf16[256,1536]{1,0:T(8,128)(2,1)S(1)}, bf16[256,1536]{1,0:T(8,128)(2,1)}, u32[]{:S(2)}, u32[]{:S(2)}) collective-permute-start(bf16[256,1536]{1,0:T(8,128)(2,1)S(1)} %collective-permute-done.33), channel_id=1, source_target_pairs={{0,8},{4,12},{8,16},{12,20},{16,24},{20,28},{24,0},{28,4},{1,9},{5... | collective-permute-start | bytes 2359304 | tf_op jit(solution)/shard_map/ppermute | solution.py:24
  247.7 31.4 %collective-permute-start.36 = (bf16[2,256,1536]{2,1,0:T(8,128)(2,1)}, bf16[2,256,1536]{2,1,0:T(8,128)(2,1)}, u32[]{:S(2)}, u32[]{:S(2)}) collective-permute-start(bf16[2,256,1536]{2,1,0:T(8,128)(2,1)} %pad_maximum_fusion.4.t0_ref), channel_id=1, source_target_pairs={{0,4},{4,0},{8,12},{12,8},{16,20},{20,16},{24,28},{28,24},{1,5},{5... | collective-permute-start | bytes 4718600 | tf_op jit(solution)/shard_map/ppermute | solution.py:29
  278.7 117.2 %all-gather.14.cloned.1.call-start = ((), (), s32[]{:S(2)}) async-start(), calls=%async_computation.6 | async-start | bytes 3932160 | tf_op jit(solution)/shard_map/all_gather | solution.py:650
  317.1 238.0 %reduce-scatter.5.cloned.1.call-start = ((), (), s32[]{:S(2)}) async-start(), calls=%async_computation.7 | async-start | bytes 8847360 | tf_op jit(solution)/shard_map/reduce_scatter | solution.py:705
  323.3 35.7 %collective-permute-start.40 = (bf16[256,1536]{1,0:T(8,128)(2,1)S(1)}, bf16[256,1536]{1,0:T(8,128)(2,1)}, u32[]{:S(2)}, u32[]{:S(2)}) collective-permute-start(bf16[256,1536]{1,0:T(8,128)(2,1)S(1)} %fusion.82), channel_id=1, source_target_pairs={{0,24},{4,28},{8,0},{12,4},{16,8},{20,12},{24,16},{28,20},{1,25},{... | collective-permute-start | bytes 2359304 | tf_op jit(solution)/shard_map/ppermute | solution.py:24
  361.2 34.8 %collective-permute-start.41 = (bf16[256,1536]{1,0:T(8,128)(2,1)}, bf16[256,1536]{1,0:T(8,128)(2,1)S(1)}, u32[]{:S(2)}, u32[]{:S(2)}) collective-permute-start(bf16[256,1536]{1,0:T(8,128)(2,1)} %fusion.9), channel_id=1, source_target_pairs={{0,24},{4,28},{8,0},{12,4},{16,8},{20,12},{24,16},{28,20},{1,25},{... | collective-permute-start | bytes 2359304 | tf_op jit(solution)/shard_map/ppermute | solution.py:24
  396.0 209.9 %reduce-scatter.7.cloned.1.call-start = ((), (), s32[]{:S(2)}) async-start(), calls=%async_computation.8 | async-start | bytes 4300800
  426.7 36.1 %collective-permute-start.45 = (bf16[256,1536]{1,0:T(8,128)(2,1)}, bf16[256,1536]{1,0:T(8,128)(2,1)}, u32[]{:S(2)}, u32[]{:S(2)}) collective-permute-start(bf16[256,1536]{1,0:T(8,128)(2,1)} %slice.276), channel_id=1, source_target_pairs={{0,24},{4,28},{8,0},{12,4},{16,8},{20,12},{24,16},{28,20},{1,25},{... | collective-permute-start | bytes 2359304 | tf_op jit(solution)/shard_map/ppermute | solution.py:24
  426.8 38.3 %collective-permute-start.46 = (bf16[256,1536]{1,0:T(8,128)(2,1)}, bf16[256,1536]{1,0:T(8,128)(2,1)}, u32[]{:S(2)}, u32[]{:S(2)}) collective-permute-start(bf16[256,1536]{1,0:T(8,128)(2,1)} %slice.277), channel_id=1, source_target_pairs={{0,8},{4,12},{8,16},{12,20},{16,24},{20,28},{24,0},{28,4},{1,9},{5... | collective-permute-start | bytes 2359304 | tf_op jit(solution)/shard_map/ppermute | solution.py:24
  467.0 83.5 %collective-permute-start.47 = (bf16[256,1536]{1,0:T(8,128)(2,1)}, bf16[256,1536]{1,0:T(8,128)(2,1)}, u32[]{:S(2)}, u32[]{:S(2)}) collective-permute-start(bf16[256,1536]{1,0:T(8,128)(2,1)} %convert_add_fusion.7), channel_id=1, source_target_pairs={{0,24},{4,28},{8,0},{12,4},{16,8},{20,12},{24,16},{28,20},{1,25},{... | collective-permute-start | bytes 2359304 | tf_op jit(solution)/shard_map/ppermute | solution.py:24
  473.0 30.7 %collective-permute-start.50 = (bf16[256,512]{1,0:T(8,128)(2,1)}, bf16[256,512]{1,0:T(8,128)(2,1)}, u32[]{:S(2)}, u32[]{:S(2)}) collective-permute-start(bf16[256,512]{1,0:T(8,128)(2,1)} %get-tuple-element.205), channel_id=1, source_target_pairs={{16,0},{20,4},{24,8},{28,12},{17,1},{21,5},{25,9},{29,13},{18,2},{... | collective-permute-start | bytes 786440 | tf_op jit(solution)/shard_map/ppermute | solution.py:24
  492.5 33.2 %collective-permute-start.52 = (bf16[256,768]{1,0:T(8,128)(2,1)}, bf16[256,768]{1,0:T(8,128)(2,1)}, u32[]{:S(2)}, u32[]{:S(2)}) collective-permute-start(bf16[256,768]{1,0:T(8,128)(2,1)} %get-tuple-element.195), channel_id=1, source_target_pairs={{0,3},{1,2},{2,1},{3,0},{4,7},{5,6},{6,5},{7,4},{8,11},{9,10},{10,... | collective-permute-start | bytes 1179656 | tf_op jit(solution)/shard_map/ppermute | solution.py:34
  602.3 33.6 %collective-permute-start.72 = (bf16[48,128]{1,0:T(8,128)(2,1)S(1)}, bf16[48,128]{1,0:T(8,128)(2,1)S(1)}, u32[]{:S(2)}, u32[]{:S(2)}) collective-permute-start(bf16[48,128]{1,0:T(8,128)(2,1)S(1)} %get-tuple-element.253), channel_id=1, source_target_pairs={{0,3},{1,2},{2,1},{3,0},{4,7},{5,6},{6,5},{7,4},{8,11},{9,10},{10,... | collective-permute-start | bytes 36872 | tf_op jit(solution)/shard_map/ppermute | solution.py:34
  603.2 32.8 %collective-permute-start.73 = (bf16[48,128]{1,0:T(8,128)(2,1)S(1)}, bf16[48,128]{1,0:T(8,128)(2,1)S(1)}, u32[]{:S(2)}, u32[]{:S(2)}) collective-permute-start(bf16[48,128]{1,0:T(8,128)(2,1)S(1)} %get-tuple-element.252), channel_id=1, source_target_pairs={{0,2},{1,3},{2,0},{3,1},{4,6},{5,7},{6,4},{7,5},{8,10},{9,11},{10,... | collective-permute-start | bytes 36872 | tf_op jit(solution)/shard_map/ppermute | solution.py:34
  (135 other events, 1699.1 us)
Sparse Core Ops, SparseCore 0:
  94.4 52.4 all-gather.5
  148.7 54.3 all-gather.7
  205.6 50.8 all-gather.9
  278.8 43.2 all-gather.11
  324.4 43.9 all-gather.13
  396.0 74.1 reduce-scatter.4
  492.6 63.4 reduce-scatter.6

commit v5 on v4

--- a/solution.py
+++ b/solution.py
@@ -626,7 +626,7 @@
     t = {0: grad_top, 1: chip_shift(top, 1)}
     if chips > 2:
         t[chips - 1] = chip_shift(top, -1)
-    qkv = qkv_project(after(normed, t[1]), qkv_full, bias, cosine, sine)
+    qkv = qkv_project(after(normed, t), qkv_full, bias, cosine, sine)
     own = qkv[:, q_cols:]
     kv_line = jnp.stack([own] + [chip_shift(own, s, cyclic=False) for s in range(1, chips)])
     kv_other = core_swap(after(kv_line, out_lines))

time: 662 us -> 668 us (level)
  starting transfers between devices: 94.1 us -> 112 us
  waiting for transfers between devices: 253 us -> 239 us
    ppermute x36, starting transfers between devices: 67.5 us -> 82.9 us  [chip_shift(): return lax.ppermute(block, 'blk', route)]
    ppermute x36, waiting for transfers between devices: 181 us -> 168 us  [chip_shift(): return lax.ppermute(block, 'blk', route)]
  transfers between devices with their start and end apart: 83 -> 83, of which waited for: 38 -> 37; matrix products, arithmetic and copies ran while one was open for 18% -> 18% of each run, Pallas kernels for 22% -> 22%
where the time goes in v5:
time: 668 us; the launch traced here: 657 us
  waiting for transfers between devices  239 us (36%)
  Pallas kernels  144 us (22%)
  starting transfers between devices  112 us (17%)
  other arithmetic  62.1 us (9%)
  local copies, waits for them, and re-layouts  51 us (8%)
  matrix products  32.8 us (5%)
  between operations  15.9 us (2%)
    ppermute x36, waiting for transfers between devices, chip_shift(): return lax.ppermute(block, 'blk', route)  168 us
    ppermute x36, starting transfers between devices, chip_shift(): return lax.ppermute(block, 'blk', route)  82.9 us
    pallas_call x2, Pallas kernels, feed(): pl.pallas_call(feed_kernel, grid=(count,), in_specs=[tokens] * 4 + [pl.Bl...  64.1 us
    ppermute x18, waiting for transfers between devices, pack_swap(): return lax.ppermute(block, 'pack', [(i, i ^ k) for i in range(n)])  58.1 us
    ppermute x18, starting transfers between devices, pack_swap(): return lax.ppermute(block, 'pack', [(i, i ^ k) for i in range(n)])  23.1 us
    pallas_call x1, Pallas kernels, gate_up_grads(): pl.pallas_call(functools.partial(grads_kernel, packs, len(hs)), grid=(4,)...  23 us
    dot_general x5, matrix products, matmul(): return jnp.dot(left, right, preferred_element_type=F32)  18 us
    pallas_call x1, Pallas kernels, down_grads(): pl.pallas_call(functools.partial(down_grads_kernel, len(acts)), grid=(4,)...  14.4 us
  transfers between devices with their start and end apart: 83, of which 37 were waited for; matrix products, arithmetic and copies ran while one was open for 18% of the time, Pallas kernels for 22%

profile of v5, /device:TPU:0, one launch (start us, length us, event | category | flops | bytes accessed | tf_op | source)
XLA Modules:
  0.0 657.0 jit_solution(15548853305780944258)
XLA Ops:
  26.4 10.3 %collective-permute-done.1 = bf16[56,2048]{1,0:T(8,128)(2,1)} collective-permute-done((bf16[56,2048]{1,0:T(8,128)(2,1)}, bf16[56,2048]{1,0:T(8,128)(2,1)}, u32[]{:S(2)}, u32[]{:S(2)}) %collective-permute-start.1) | collective-permute-done | bytes 229408 | tf_op jit(solution)/shard_map/ppermute | solution.py:24
  46.2 11.8 %collective-permute-done.10 = bf16[2,2,48,1120]{3,2,1,0:T(8,128)(2,1)S(1)} collective-permute-done((bf16[2,2,48,1120]{3,2,1,0:T(8,128)(2,1)S(1)}, bf16[2,2,48,1120]{3,2,1,0:T(8,128)(2,1)S(1)}, u32[]{:S(2)}, u32[]{:S(2)}) %collective-permute-start.10) | collective-permute-done | bytes 430112 | tf_op jit(solution)/shard_map/ppermute | solution.py:24
  62.4 17.6 %collective-permute-done.3.refs_2_ = bf16[4,56,2048]{2,1,0:T(8,128)(2,1)S(1)} collective-permute-done((bf16[4,56,2048]{2,1,0:T(8,128)(2,1)S(1)}, bf16[4,56,2048]{2,1,0:T(8,128)(2,1)S(1)}, u32[]{:S(2)}, u32[]{:S(2)}) %collective-permute-start.3) | collective-permute-done | bytes 917536 | tf_op jit(solution)/shard_map/ppermute | solution.py:34
  104.0 6.5 shard_map.186.w_ref
  120.4 16.1 %collective-permute-done.15 = bf16[256,1536]{1,0:T(8,128)(2,1)} collective-permute-done((bf16[256,1536]{1,0:T(8,128)(2,1)S(1)}, bf16[256,1536]{1,0:T(8,128)(2,1)}, u32[]{:S(2)}, u32[]{:S(2)}) %collective-permute-start.15) | collective-permute-done | bytes 786464 | tf_op jit(solution)/shard_map/ppermute | solution.py:24
  136.5 8.4 %shard_map.187.q_ref = bf16[256,2048]{1,0:T(8,128)(2,1)} custom-call(bf16[256,1536]{1,0:T(8,128)(2,1)} %fusion.2.xn_ref, bf16[1536,2048]{1,0:T(8,128)(2,1)} %shard_map.186.w_ref, f32[1,2048]{1,0:T(1,128)} %slice.265.bias_ref, f32[256,128]{1,0:T(8,128)} %get-tuple-element.268.cos_ref, f32[256,128]{1,0:T(8,128)} %get-tuple-element.269.sin_ref), custom_call_target="tpu_custom_call" | custom-call | flops 1610612736 | bytes 6291456 | tf_op jit(solution)/shard_map/pallas_call | solution.py:167
  169.1 7.5 %collective-permute-done.22.refs_2_ = bf16[4,48,1536]{2,1,0:T(8,128)(2,1)} collective-permute-done((bf16[4,48,1536]{2,1,0:T(8,128)(2,1)S(1)}, bf16[4,48,1536]{2,1,0:T(8,128)(2,1)}, u32[]{:S(2)}, u32[]{:S(2)}) %collective-permute-start.22) | collective-permute-done | bytes 589856 | tf_op jit(solution)/shard_map/ppermute | solution.py:34
  176.6 11.3 %collective-permute-done.23.refs_4_ = bf16[4,48,1536]{2,1,0:T(8,128)(2,1)} collective-permute-done((bf16[4,48,1536]{2,1,0:T(8,128)(2,1)S(1)}, bf16[4,48,1536]{2,1,0:T(8,128)(2,1)}, u32[]{:S(2)}, u32[]{:S(2)}) %collective-permute-start.23) | collective-permute-done | bytes 589856 | tf_op jit(solution)/shard_map/ppermute | solution.py:34
  191.5 8.8 %shard_map.188 = (f32[256,1536]{1,0:T(8,128)}, bf16[256,1536]{1,0:T(8,128)(2,1)}, f32[2,1,1536]{2,1,0:T(1,128)}) custom-call(s32[17]{0:T(128)} %pad_add_fusion.1.meta_ref, bf16[256,2048]{1,0:T(8,128)(2,1)} %shard_map.187.q_ref, s32[1,256]{1,0:T(1,128)} %bitcast.410, bf16[4,256,512]{2,1,0:T(8,128)(2,1)} %copy-done.30, bf16[4,256,512]{2,1,0:T(8,128)(2,1)} %copy-done.30, ...), custom_call_target="tpu_custom_call" | custom-call | flops 12884901888 | bytes 2097152 | tf_op jit(solution)/shard_map/pallas_call | solution.py:269
  229.6 18.4 %collective-permute-done.33 = bf16[256,1536]{1,0:T(8,128)(2,1)S(1)} collective-permute-done((bf16[256,1536]{1,0:T(8,128)(2,1)S(1)}, bf16[256,1536]{1,0:T(8,128)(2,1)S(1)}, u32[]{:S(2)}, u32[]{:S(2)}) %collective-permute-start.33) | collective-permute-done | bytes 786464 | tf_op jit(solution)/shard_map/ppermute | solution.py:24
  248.0 14.8 %collective-permute-start.34 = (bf16[256,1536]{1,0:T(8,128)(2,1)S(1)}, bf16[256,1536]{1,0:T(8,128)(2,1)}, u32[]{:S(2)}, u32[]{:S(2)}) collective-permute-start(bf16[256,1536]{1,0:T(8,128)(2,1)S(1)} %collective-permute-done.33), channel_id=1, source_target_pairs={{0,8},{4,12},{8,16},{12,20},{16,24},{20,28},{24,0},{28,4},{1,9},{5... | collective-permute-start | bytes 2359304 | tf_op jit(solution)/shard_map/ppermute | solution.py:24
  273.8 10.0 %collective-permute-done.34 = bf16[256,1536]{1,0:T(8,128)(2,1)} collective-permute-done((bf16[256,1536]{1,0:T(8,128)(2,1)S(1)}, bf16[256,1536]{1,0:T(8,128)(2,1)}, u32[]{:S(2)}, u32[]{:S(2)}) %collective-permute-start.34) | collective-permute-done | bytes 786464 | tf_op jit(solution)/shard_map/ppermute | solution.py:24
  290.0 32.5 %shard_map.190 = (bf16[2,256,1120]{2,1,0:T(8,128)(2,1)}, bf16[2,256,1120]{2,1,0:T(8,128)(2,1)}, bf16[2,256,1120]{2,1,0:T(8,128)(2,1)}, bf16[2,256,1120]{2,1,0:T(...) custom-call(bf16[2,256,1536]{2,1,0:T(8,128)(2,1)} %pad_maximum_fusio, ...), custom_call_target="tpu_custom_call" | custom-call | flops 66060288000 | bytes 10321920 | tf_op jit(solution)/shard_map/pallas_call | solution.py:482
  330.6 31.6 %shard_map.191 = (bf16[2,256,1120]{2,1,0:T(8,128)(2,1)}, bf16[2,256,1120]{2,1,0:T(8,128)(2,1)}, bf16[2,256,1120]{2,1,0:T(8,128)(2,1)}, bf16[2,256,1120]{2,1,0:T(...) custom-call(bf16[2,256,1536]{2,1,0:T(8,128)(2,1)} %pad_maximum_fusio, ...), custom_call_target="tpu_custom_call" | custom-call | flops 66060288000 | bytes 10321920 | tf_op jit(solution)/shard_map/pallas_call | solution.py:482
  366.0 23.0 %shard_map.192 = bf16[4,8,2,48,1120]{4,3,2,1,0:T(8,128)(2,1)} custom-call(bf16[512,1536]{1,0:T(8,128)(2,1)} %bitcast.61.refs_0_, bf16[512,1536]{1,0:T(8,128)(2,1)} %bitcast.62.refs_1_, bf16[512,1536]{1,0:T(8,128)(2,1)} %bitcast.63.refs_2_, bf16[512,1536]{1,0:T(8,128)(2,1)} %bitcast.64.refs_3_, bf16[512,1120]{1,0:T(8,128)(2,1)} %bitcast.422, ...), custom_call_target="tpu_custom_call" | custom-call | flops 24662507520 | bytes 13762560 | tf_op jit(solution)/shard_map/pallas_call | solution.py:528
  400.1 12.0 %collective-permute-done.42 = bf16[256,1536]{1,0:T(8,128)(2,1)} collective-permute-done((bf16[256,1536]{1,0:T(8,128)(2,1)}, bf16[256,1536]{1,0:T(8,128)(2,1)}, u32[]{:S(2)}, u32[]{:S(2)}) %collective-permute-start.42) | collective-permute-done | bytes 786464 | tf_op jit(solution)/shard_map/ppermute | solution.py:24
  433.1 13.4 %shard_map.193 = (bf16[256,1536]{1,0:T(8,128)(2,1)}, bf16[4,256,256]{2,1,0:T(8,128)(2,1)}, bf16[4,256,256]{2,1,0:T(8,128)(2,1)}, bf16[4,256,256]{2,1,0:T(8,128)(2,1)}, bf16[4,256,256]{2,1,0:T(8,128)(2,1)}) custom-call(s32[17]{0:T(128)} %pad_add_fusion.1.meta_ref, bf16[256,2048]{1,0:T(8,128)(2,1)} %shard_map.187.q_ref, ...), custom_call_target="tpu_custom_call" | custom-call | flops 322122547200 | bytes 2097152 | tf_op jit(solution)/shard_map/pallas_call | solution.py:367
  446.5 19.9 %collective-permute-done.45 = bf16[256,1536]{1,0:T(8,128)(2,1)} collective-permute-done((bf16[256,1536]{1,0:T(8,128)(2,1)}, bf16[256,1536]{1,0:T(8,128)(2,1)}, u32[]{:S(2)}, u32[]{:S(2)}) %collective-permute-start.45) | collective-permute-done | bytes 786464 | tf_op jit(solution)/shard_map/ppermute | solution.py:24
  479.4 14.4 %shard_map.194 = bf16[1120,1536]{1,0:T(8,128)(2,1)} custom-call(bf16[512,1120]{1,0:T(8,128)(2,1)} %bitcast.414, bf16[512,1120]{1,0:T(8,128)(2,1)} %bitcast.416, bf16[512,1120]{1,0:T(8,128)(2,1)} %bitcast.418, bf16[512,1120]{1,0:T(8,128)(2,1)} %bitcast.420, bf16[512,1536]{1,0:T(8,128)(2,1)} %bitcast.87.refs_4_, bf16[512,1536]{1,0:T(8,128)(2,1)} %bitcast.88.refs_5_, ...), custom_call_target="tpu_custom_call" | custom-call | flops 7046430720 | bytes 12582912 | tf_op jit(solution)/shard_map/pallas_call | solution.py:551
  498.7 8.5 %collective-permute-done.50 = bf16[256,512]{1,0:T(8,128)(2,1)} collective-permute-done((bf16[256,512]{1,0:T(8,128)(2,1)}, bf16[256,512]{1,0:T(8,128)(2,1)}, u32[]{:S(2)}, u32[]{:S(2)}) %collective-permute-start.50) | collective-permute-done | bytes 262176 | tf_op jit(solution)/shard_map/ppermute | solution.py:24
  530.1 10.1 %collective-permute-done.53 = bf16[256,768]{1,0:T(8,128)(2,1)S(1)} collective-permute-done((bf16[256,768]{1,0:T(8,128)(2,1)}, bf16[256,768]{1,0:T(8,128)(2,1)S(1)}, u32[]{:S(2)}, u32[]{:S(2)}) %collective-permute-start.53) | collective-permute-done | bytes 393248 | tf_op jit(solution)/shard_map/ppermute | solution.py:34
  577.0 16.2 %collective-permute-done.57 = bf16[2,2,48,1120]{3,2,1,0:T(8,128)(2,1)S(1)} collective-permute-done((bf16[2,2,48,1120]{3,2,1,0:T(8,128)(2,1)S(1)}, bf16[2,2,48,1120]{3,2,1,0:T(8,128)(2,1)S(1)}, u32[]{:S(2)}, u32[]{:S(2)}) %collective-permute-start.57) | collective-permute-done | bytes 430112 | tf_op jit(solution)/shard_map/ppermute | solution.py:24
  595.0 10.9 %collective-permute-start.61 = (bf16[192,768]{1,0:T(8,128)(2,1)S(1)}, bf16[192,768]{1,0:T(8,128)(2,1)}, u32[]{:S(2)}, u32[]{:S(2)}) collective-permute-start(bf16[192,768]{1,0:T(8,128)(2,1)S(1)} %get-tuple-element.201), channel_id=1, source_target_pairs={{0,24},{4,28},{8,0},{12,4},{16,8},{20,12},{24,16},{28,20},{1,25},{... | collective-permute-start | bytes 884744 | tf_op jit(solution)/shard_map/ppermute | solution.py:24
  613.4 18.2 %collective-permute-done.60 = bf16[192,768]{1,0:T(8,128)(2,1)} collective-permute-done((bf16[192,768]{1,0:T(8,128)(2,1)S(1)}, bf16[192,768]{1,0:T(8,128)(2,1)}, u32[]{:S(2)}, u32[]{:S(2)}) %collective-permute-start.60) | collective-permute-done | bytes 294944 | tf_op jit(solution)/shard_map/ppermute | solution.py:24
  (456 shorter events, 288.7 us)
Async XLA Ops:
  7.2 258.4 %all-gather.6.cloned.1.call-start = ((), (), s32[]{:S(2)}) async-start(), calls=%async_computation.2 | async-start | bytes 4423680 | tf_op jit(solution)/shard_map/all_gather | solution.py:617
  40.7 39.3 %collective-permute-start.3 = (bf16[4,56,2048]{2,1,0:T(8,128)(2,1)S(1)}, bf16[4,56,2048]{2,1,0:T(8,128)(2,1)S(1)}, u32[]{:S(2)}, u32[]{:S(2)}) collective-permute-start(bf16[4,56,2048]{2,1,0:T(8,128)(2,1)S(1)} %pad_maximum_fusion.10.refs_0_), channel_id=1, source_target_pairs={{0,1},{1,0},{2,3},{3,2},{4,5},{5,4},{6,7},{7,6},{8,9},{9,8},{10,11... | collective-permute-start | bytes 2752520 | tf_op jit(solution)/shard_map/ppermute | solution.py:34
  41.1 39.0 %collective-permute-start.6 = (bf16[4,56,2048]{2,1,0:T(8,128)(2,1)S(1)}, bf16[4,56,2048]{2,1,0:T(8,128)(2,1)S(1)}, u32[]{:S(2)}, u32[]{:S(2)}) collective-permute-start(bf16[4,56,2048]{2,1,0:T(8,128)(2,1)S(1)} %pad_maximum_fusion.10.refs_0_), channel_id=1, source_target_pairs={{0,2},{1,3},{2,0},{3,1},{4,6},{5,7},{6,4},{7,5},{8,10},{9,11},{10,... | collective-permute-start | bytes 2752520 | tf_op jit(solution)/shard_map/ppermute | solution.py:34
  43.9 36.8 %collective-permute-start.11 = (bf16[2,2,48,1120]{3,2,1,0:T(8,128)(2,1)S(1)}, bf16[2,2,48,1120]{3,2,1,0:T(8,128)(2,1)S(1)}, u32[]{:S(2)}, u32[]{:S(2)}) collective-permute-start(bf16[2,2,48,1120]{3,2,1,0:T(8,128)(2,1)S(1)} %bitcast.393), channel_id=1, source_target_pairs={{0,16},{4,20},{8,24},{12,28},{16,0},{20,4},{24,8},{28,12},{1,17},{... | collective-permute-start | bytes 1290248 | tf_op jit(solution)/shard_map/ppermute | solution.py:24
  94.3 175.3 %all-gather.8.cloned.1.call-start = ((), (), s32[]{:S(2)}) async-start(), calls=%async_computation.3 | async-start | bytes 4423680 | tf_op jit(solution)/shard_map/all_gather | solution.py:617
  95.4 190.8 %all-gather.10.cloned.1.call-start = ((), (), s32[]{:S(2)}) async-start(), calls=%async_computation.4 | async-start | bytes 4300800 | tf_op jit(solution)/shard_map/all_gather | solution.py:613
  99.2 37.3 %collective-permute-start.15 = (bf16[256,1536]{1,0:T(8,128)(2,1)S(1)}, bf16[256,1536]{1,0:T(8,128)(2,1)}, u32[]{:S(2)}, u32[]{:S(2)}) collective-permute-start(bf16[256,1536]{1,0:T(8,128)(2,1)S(1)} %bitcast.363), channel_id=1, source_target_pairs={{0,24},{4,28},{8,0},{12,4},{16,8},{20,12},{24,16},{28,20},{1,25},{... | collective-permute-start | bytes 2359304 | tf_op jit(solution)/shard_map/ppermute | solution.py:24
  111.7 40.1 %collective-permute-start.21 = (bf16[48,1536]{1,0:T(8,128)(2,1)S(1)}, bf16[48,1536]{1,0:T(8,128)(2,1)S(1)}, u32[]{:S(2)}, u32[]{:S(2)}) collective-permute-start(bf16[48,1536]{1,0:T(8,128)(2,1)S(1)} %convert_element_type.278), channel_id=1, source_target_pairs={{0,24},{4,28},{8,0},{12,4},{16,8},{20,12},{24,16},{28,20},{1,25},{... | collective-permute-start | bytes 442376 | tf_op jit(solution)/shard_map/ppermute | solution.py:24
  112.8 39.0 %collective-permute-start.20 = (bf16[48,1536]{1,0:T(8,128)(2,1)S(1)}, bf16[48,1536]{1,0:T(8,128)(2,1)S(1)}, u32[]{:S(2)}, u32[]{:S(2)}) collective-permute-start(bf16[48,1536]{1,0:T(8,128)(2,1)S(1)} %convert_element_type.278), channel_id=1, source_target_pairs={{0,16},{4,20},{8,24},{12,28},{16,0},{20,4},{24,8},{28,12},{1,17},{... | collective-permute-start | bytes 442376 | tf_op jit(solution)/shard_map/ppermute | solution.py:24
  113.3 38.6 %collective-permute-start.19 = (bf16[48,1536]{1,0:T(8,128)(2,1)S(1)}, bf16[48,1536]{1,0:T(8,128)(2,1)S(1)}, u32[]{:S(2)}, u32[]{:S(2)}) collective-permute-start(bf16[48,1536]{1,0:T(8,128)(2,1)S(1)} %convert_element_type.278), channel_id=1, source_target_pairs={{0,8},{4,12},{8,16},{12,20},{16,24},{20,28},{24,0},{28,4},{1,9},{5... | collective-permute-start | bytes 442376 | tf_op jit(solution)/shard_map/ppermute | solution.py:24
  153.6 34.3 %collective-permute-start.23 = (bf16[4,48,1536]{2,1,0:T(8,128)(2,1)S(1)}, bf16[4,48,1536]{2,1,0:T(8,128)(2,1)}, u32[]{:S(2)}, u32[]{:S(2)}) collective-permute-start(bf16[4,48,1536]{2,1,0:T(8,128)(2,1)S(1)} %pad_maximum_fusion.11.refs_0_), channel_id=1, source_target_pairs={{0,2},{1,3},{2,0},{3,1},{4,6},{5,7},{6,4},{7,5},{8,10},{9,11},{10,... | collective-permute-start | bytes 1769480 | tf_op jit(solution)/shard_map/ppermute | solution.py:34
  154.1 33.8 %collective-permute-start.24 = (bf16[4,48,1536]{2,1,0:T(8,128)(2,1)S(1)}, bf16[4,48,1536]{2,1,0:T(8,128)(2,1)}, u32[]{:S(2)}, u32[]{:S(2)}) collective-permute-start(bf16[4,48,1536]{2,1,0:T(8,128)(2,1)S(1)} %pad_maximum_fusion.11.refs_0_), channel_id=1, source_target_pairs={{0,3},{1,2},{2,1},{3,0},{4,7},{5,6},{6,5},{7,4},{8,11},{9,10},{10,... | collective-permute-start | bytes 1769480 | tf_op jit(solution)/shard_map/ppermute | solution.py:34
  205.5 194.5 %all-gather.12.cloned.1.call-start = ((), (), s32[]{:S(2)}) async-start(), calls=%async_computation.5 | async-start | bytes 3932160 | tf_op jit(solution)/shard_map/all_gather | solution.py:651
  223.7 50.1 %collective-permute-start.31 = (bf16[256,1536]{1,0:T(8,128)(2,1)S(1)}, bf16[256,1536]{1,0:T(8,128)(2,1)S(1)}, u32[]{:S(2)}, u32[]{:S(2)}) collective-permute-start(bf16[256,1536]{1,0:T(8,128)(2,1)S(1)} %multiply_convert_fusion), channel_id=1, source_target_pairs={{0,24},{4,28},{8,0},{12,4},{16,8},{20,12},{24,16},{28,20},{1,25},{... | collective-permute-start | bytes 2359304 | tf_op jit(solution)/shard_map/ppermute | solution.py:24
  248.0 35.7 %collective-permute-start.34 = (bf16[256,1536]{1,0:T(8,128)(2,1)S(1)}, bf16[256,1536]{1,0:T(8,128)(2,1)}, u32[]{:S(2)}, u32[]{:S(2)}) collective-permute-start(bf16[256,1536]{1,0:T(8,128)(2,1)S(1)} %collective-permute-done.33), channel_id=1, source_target_pairs={{0,8},{4,12},{8,16},{12,20},{16,24},{20,28},{24,0},{28,4},{1,9},{5... | collective-permute-start | bytes 2359304 | tf_op jit(solution)/shard_map/ppermute | solution.py:24
  286.2 113.8 %all-gather.14.cloned.1.call-start = ((), (), s32[]{:S(2)}) async-start(), calls=%async_computation.6 | async-start | bytes 3932160 | tf_op jit(solution)/shard_map/all_gather | solution.py:650
  325.8 233.6 %reduce-scatter.5.cloned.1.call-start = ((), (), s32[]{:S(2)}) async-start(), calls=%async_computation.7 | async-start | bytes 8847360 | tf_op jit(solution)/shard_map/reduce_scatter | solution.py:705
  364.6 35.5 %collective-permute-start.41 = (bf16[256,1536]{1,0:T(8,128)(2,1)}, bf16[256,1536]{1,0:T(8,128)(2,1)S(1)}, u32[]{:S(2)}, u32[]{:S(2)}) collective-permute-start(bf16[256,1536]{1,0:T(8,128)(2,1)} %fusion.9), channel_id=1, source_target_pairs={{0,24},{4,28},{8,0},{12,4},{16,8},{20,12},{24,16},{28,20},{1,25},{... | collective-permute-start | bytes 2359304 | tf_op jit(solution)/shard_map/ppermute | solution.py:24
  400.0 210.3 %reduce-scatter.7.cloned.1.call-start = ((), (), s32[]{:S(2)}) async-start(), calls=%async_computation.8 | async-start | bytes 4300800
  430.7 35.7 %collective-permute-start.45 = (bf16[256,1536]{1,0:T(8,128)(2,1)}, bf16[256,1536]{1,0:T(8,128)(2,1)}, u32[]{:S(2)}, u32[]{:S(2)}) collective-permute-start(bf16[256,1536]{1,0:T(8,128)(2,1)} %slice.276), channel_id=1, source_target_pairs={{0,24},{4,28},{8,0},{12,4},{16,8},{20,12},{24,16},{28,20},{1,25},{... | collective-permute-start | bytes 2359304 | tf_op jit(solution)/shard_map/ppermute | solution.py:24
  430.7 38.0 %collective-permute-start.46 = (bf16[256,1536]{1,0:T(8,128)(2,1)}, bf16[256,1536]{1,0:T(8,128)(2,1)}, u32[]{:S(2)}, u32[]{:S(2)}) collective-permute-start(bf16[256,1536]{1,0:T(8,128)(2,1)} %slice.277), channel_id=1, source_target_pairs={{0,8},{4,12},{8,16},{12,20},{16,24},{20,28},{24,0},{28,4},{1,9},{5... | collective-permute-start | bytes 2359304 | tf_op jit(solution)/shard_map/ppermute | solution.py:24
  470.6 84.0 %collective-permute-start.47 = (bf16[256,1536]{1,0:T(8,128)(2,1)}, bf16[256,1536]{1,0:T(8,128)(2,1)}, u32[]{:S(2)}, u32[]{:S(2)}) collective-permute-start(bf16[256,1536]{1,0:T(8,128)(2,1)} %convert_add_fusion.7), channel_id=1, source_target_pairs={{0,24},{4,28},{8,0},{12,4},{16,8},{20,12},{24,16},{28,20},{1,25},{... | collective-permute-start | bytes 2359304 | tf_op jit(solution)/shard_map/ppermute | solution.py:24
  496.1 34.1 %collective-permute-start.52 = (bf16[256,768]{1,0:T(8,128)(2,1)}, bf16[256,768]{1,0:T(8,128)(2,1)}, u32[]{:S(2)}, u32[]{:S(2)}) collective-permute-start(bf16[256,768]{1,0:T(8,128)(2,1)} %get-tuple-element.195), channel_id=1, source_target_pairs={{0,3},{1,2},{2,1},{3,0},{4,7},{5,6},{6,5},{7,4},{8,11},{9,10},{10,... | collective-permute-start | bytes 1179656 | tf_op jit(solution)/shard_map/ppermute | solution.py:34
  606.6 34.6 %collective-permute-start.72 = (bf16[48,128]{1,0:T(8,128)(2,1)S(1)}, bf16[48,128]{1,0:T(8,128)(2,1)S(1)}, u32[]{:S(2)}, u32[]{:S(2)}) collective-permute-start(bf16[48,128]{1,0:T(8,128)(2,1)S(1)} %get-tuple-element.253), channel_id=1, source_target_pairs={{0,3},{1,2},{2,1},{3,0},{4,7},{5,6},{6,5},{7,4},{8,11},{9,10},{10,... | collective-permute-start | bytes 36872 | tf_op jit(solution)/shard_map/ppermute | solution.py:34
  (130 other events, 1616.7 us)
Sparse Core Ops, SparseCore 0:
  94.4 47.1 all-gather.5
  143.4 64.6 all-gather.7
  210.6 51.5 all-gather.9
  286.4 43.4 all-gather.11
  332.2 43.9 all-gather.13
  400.1 75.9 reduce-scatter.4
  498.8 62.9 reduce-scatter.6
